TPU v7x, 256 devices: a whole 4x4x8 slice. The times are simulated.
256 devices in a mesh: lat: 64 (over x, z, core), chan: 4 (over y).
Axes of the slice: x: 4, y: 4, z: 8, core: 2. Of those that a mesh axis runs over, the one named last changes fastest.
Arguments:
- field_in: bfloat16 [768, 384, 720], P('lat', 'chan'), may hold values from -6 to 6
- cotangent: bfloat16 [768, 384, 720], P('lat', 'chan'), may hold values from -1.1953125 to 1.1953125
- weights: bfloat16 [512, 384, 384], P(('lat', 'chan')), may hold values from -0.3125 to 0.3125
- row_counts: int32 [64], replicated, may hold values from 0 to 12, as said below
- slot_degree: int32 [512], replicated, may hold values from 0 to 360, as said below
Outputs:
- field_grad: bfloat16 [768, 384, 720], P('lat', 'chan')
- weight_grad: float32 [512, 384, 384], P(('lat', 'chan'))
Inputs may be any that keep to these rules, and one draw needn't show every extreme that they name: `row_counts`: lat devices 2p and 2p+1 together hold exactly 12 live rows; some device holds 12. `slot_degree`: each degree 0 to 359 stands in exactly one slot; the other slots hold 360.
All inputs are finite; a program needn't handle non-finite values.
Results may differ from a plain program's by a relative error of at most 0.015.
Values may be sent and summed in bfloat16 or wider, within the bound.
No kernel may reach another device: no remote copies, remote signals or barrier semaphores. Data moves between devices by JAX's collectives and lax.ppermute only.
A program may use at most 128 MiB of HBM per device.

v0:
```python
import math

import jax
import jax.numpy as jnp
from jax import lax
from jax.sharding import PartitionSpec as P

NLON = 720
L = 360
M = 360


RESCALE = 2.0**40
RESCALE_LOG = 40.0 * math.log(2.0)


def legendre_rows(orders, cosine, logsine, degrees, latitudes):
    order_col = orders[:, None]
    start_log = (
        0.5 * jnp.log((2.0 * order_col + 1.0) / (4.0 * math.pi))
        + 0.5 * lax.lgamma(2.0 * order_col + 1.0)
        - order_col * math.log(2.0)
        - lax.lgamma(order_col + 1.0)
        + order_col * logsine[None, :]
        + 0.5 * math.log(2.0 * math.pi * math.pi / latitudes)
        + 0.5 * logsine[None, :]
    )
    grid_shape = start_log.shape
    cos_grid = jnp.broadcast_to(cosine[None, :], grid_shape)
    degree_list = jnp.arange(degrees).astype(jnp.float32)
    degree_col = degree_list[:, None]
    square = (orders * orders)[None, :]
    upper_all = jnp.sqrt(
        jnp.maximum(4.0 * degree_col * degree_col - 1.0, 1.0)
        / jnp.maximum(degree_col * degree_col - square, 1.0)
    )
    lower_all = jnp.sqrt(
        jnp.maximum((degree_col - 1.0) * (degree_col - 1.0) - square, 0.0)
        / jnp.maximum(4.0 * (degree_col - 1.0) * (degree_col - 1.0) - 1.0, 1.0)
    )

    def advance(carry, inputs):
        previous, current, scale_log = carry
        degree, coef_upper, coef_lower = inputs
        fresh_value = coef_upper[:, None] * (cos_grid * current - coef_lower[:, None] * previous)
        rising = degree > order_col
        previous = jnp.where(rising, current, previous)
        current = jnp.where(rising, fresh_value, current)
        too_large = jnp.abs(current) > RESCALE
        factor = jnp.where(too_large, 1.0 / RESCALE, 1.0)
        previous = previous * factor
        current = current * factor
        scale_log = scale_log + jnp.where(too_large, RESCALE_LOG, 0.0)
        result = jnp.where(degree >= order_col, current * jnp.exp(scale_log), 0.0)
        return ((previous, current, scale_log), result)

    initial = (jnp.zeros(grid_shape, jnp.float32), jnp.ones(grid_shape, jnp.float32), start_log)
    final_state, values = lax.scan(advance, initial, (degree_list, upper_all, lower_all), unroll=24)
    return values


def fourier_table(orders, live_mask, length_lon):
    longitude = jnp.arange(length_lon, dtype=jnp.int32)[:, None]
    turn_count = longitude * orders[None, :] % length_lon
    angles = turn_count.astype(jnp.float32) * (2.0 * math.pi / length_lon)
    scaling = 1.0 / math.sqrt(length_lon)
    paired = (
        jnp.stack([jnp.cos(angles) * scaling, -jnp.sin(angles) * scaling], axis=-1)
        * live_mask[None, :, None]
    )
    return paired.reshape(length_lon, 2 * orders.shape[0]).astype(jnp.bfloat16)


def lookup(entries, wanted):
    matches = wanted[..., None] == jnp.arange(entries.shape[0], dtype=jnp.int32)
    return jnp.sum(jnp.where(matches, entries, 0), axis=-1)


def on_device(field_in, cotangent, weights, row_counts, slot_degree):
    lat_count = lax.axis_size("lat")
    chan_count = lax.axis_size("chan")
    lat_rank = lax.axis_index("lat")
    rowmax = field_in.shape[0]
    half_rows = rowmax // 2
    narrow = field_in.shape[1]
    per_device = M // lat_count + 1
    order_slots = per_device * lat_count
    slot_index = jnp.arange(order_slots, dtype=jnp.int32)
    slot_orders = slot_index % per_device * lat_count + slot_index // per_device
    orders_safe = jnp.minimum(slot_orders, M - 1)
    live_orders = (slot_orders < M).astype(jnp.float32)
    fourier = fourier_table(orders_safe, live_orders, NLON)
    doubled = fourier * jnp.repeat(jnp.where(orders_safe == 0, 1.0, 2.0), 2).astype(jnp.bfloat16)
    latitude_total = lat_count * half_rows
    global_row = jnp.arange(lat_count * rowmax, dtype=jnp.int32)
    owner_dev = global_row // rowmax
    within = global_row % rowmax
    offsets = jnp.cumsum(row_counts) - row_counts
    live_bool = within < lookup(row_counts, owner_dev)
    row_latitude = jnp.where(live_bool, lookup(offsets, owner_dev) + within, 0)
    row_live = live_bool.astype(jnp.float32)
    spectra = jnp.dot(field_in, fourier, preferred_element_type=jnp.float32).astype(jnp.bfloat16)
    dspectra = jnp.dot(cotangent, doubled, preferred_element_type=jnp.float32).astype(jnp.bfloat16)
    spectra_cols, dspectra_cols = (
        lax.all_to_all(spectra, "lat", split_axis=2, concat_axis=0, tiled=True),
        lax.all_to_all(dspectra, "lat", split_axis=2, concat_axis=0, tiled=True),
    )
    row_total = spectra_cols.shape[0]
    my_orders = lax.dynamic_slice_in_dim(orders_safe, lat_rank * per_device, per_device)
    my_live = lax.dynamic_slice_in_dim(live_orders, lat_rank * per_device, per_device)
    colatitude = (row_latitude.astype(jnp.float32) + 0.5) * (math.pi / latitude_total)
    legendre_all = legendre_rows(
        my_orders.astype(jnp.float32),
        jnp.cos(colatitude),
        jnp.log(jnp.sin(colatitude)),
        L,
        latitude_total,
    )
    degree_live = (slot_degree < L).astype(jnp.float32)
    legendre = jnp.take(legendre_all, jnp.minimum(slot_degree, L - 1), axis=0)
    legendre = (
        legendre * degree_live[:, None, None] * my_live[None, :, None] * row_live[None, None, :]
    ).astype(jnp.bfloat16)
    slot_count = legendre.shape[0]
    coeffs = (
        jnp.einsum(
            "spk,kcpr->sprc",
            legendre,
            spectra_cols.reshape(row_total, narrow, per_device, 2),
            preferred_element_type=jnp.float32,
        )
        .astype(jnp.bfloat16)
        .reshape(slot_count, per_device * 2, narrow)
    )
    dcoeffs = (
        jnp.einsum(
            "spk,kcpr->sprc",
            legendre,
            dspectra_cols.reshape(row_total, narrow, per_device, 2),
            preferred_element_type=jnp.float32,
        )
        .astype(jnp.bfloat16)
        .reshape(slot_count, per_device * 2, narrow)
    )
    coeffs_deg, dcoeffs_deg = (
        lax.all_to_all(
            lax.all_to_all(coeffs, "lat", split_axis=0, concat_axis=1, tiled=True),
            "chan",
            split_axis=0,
            concat_axis=2,
            tiled=True,
        ),
        lax.all_to_all(
            lax.all_to_all(dcoeffs, "lat", split_axis=0, concat_axis=1, tiled=True),
            "chan",
            split_axis=0,
            concat_axis=2,
            tiled=True,
        ),
    )
    weight_grad = jnp.einsum(
        "dsi,dsc->dic", coeffs_deg, dcoeffs_deg, preferred_element_type=jnp.float32
    )
    dcoeffs_in = jnp.einsum(
        "dsc,dic->dsi", dcoeffs_deg, weights, preferred_element_type=jnp.float32
    ).astype(jnp.bfloat16)
    returned = lax.all_to_all(
        lax.all_to_all(dcoeffs_in, "lat", split_axis=1, concat_axis=0, tiled=True),
        "chan",
        split_axis=2,
        concat_axis=0,
        tiled=True,
    )
    degree_block = weights.shape[0]
    returned = returned.reshape(chan_count, lat_count, degree_block, per_device, 2, narrow)
    returned = returned.transpose(1, 0, 2, 3, 4, 5).reshape(slot_count, per_device, 2, narrow)
    dspectra_in = (
        jnp.einsum("spk,sprc->kcpr", legendre, returned, preferred_element_type=jnp.float32)
        .astype(jnp.bfloat16)
        .reshape(row_total, narrow, per_device * 2)
    )
    dspectra_rows = lax.all_to_all(dspectra_in, "lat", split_axis=0, concat_axis=2, tiled=True)
    grad_rows = jnp.dot(dspectra_rows, fourier.T, preferred_element_type=jnp.float32).astype(
        jnp.bfloat16
    )
    return (grad_rows, weight_grad)


def solution(mesh):
    placed = (
        P("lat", "chan", None),
        P("lat", "chan", None),
        P(("lat", "chan"), None, None),
        P(),
        P(),
    )
    return jax.shard_map(
        on_device,
        mesh=mesh,
        in_specs=placed,
        out_specs=(P("lat", "chan", None), P(("lat", "chan"), None, None)),
        check_vma=False,
    )
```

profile of v0, /device:TPU:1, one launch (start us, length us, event | category | flops | bytes accessed | tf_op | source)
XLA Modules:
  0.0 784.0 jit_solution(9152539711304057532)
XLA Ops:
  0.7 4.6 cosine_multiply_fusion
  7.3 5.4 copy.119
  12.7 4.1 stack.8
  23.6 4.7 copy.121
  28.3 13.9 %all-to-all-start = ((bf16[12,96,768]{1,0,2:T(8,128)(2,1)}), bf16[12,96,768]{1,0,2:T(8,128)(2,1)}, u32[]{:S(2)}, u32[]{:S(2)}) async-start(bf16[12,96,768]{1,0,2:T(8,128)(2,1)} %copy.121), calls=%async_computation | async-start | bytes 6291456 | tf_op jit(solution)/shard_map/all_to_all | solution.py:106
  43.4 304.0 %while.17 = (s32[]{:T(128)}, f32[6,768]{1,0:T(8,128)S(1)}, f32[6,768]{1,0:T(8,128)S(1)}, f32[6,768]{1,0:T(8,128)S(1)}, f32[15,24,6,768]{3,2,1,0:T(8,128)}, /*ind...) while((s32[]{:T(128)}, f32[6,768]{1,0:T(8,128)S(1)}, ...), condition=%wide.region_4.5_spmd.clone, body=%wide.region_3.4_spmd.clone.sunk | while | flops 3875641 | bytes 4602356 | solution.py:58
  49.5 11.3 %compare_bitcast_fusion.50 = (pred[6]{0:T(512)(128)(4,1)S(1)}, pred[6]{0:T(512)(128)(4,1)S(1)}, pred[6]{0:T(512)(128)(4,1)S(1)}, pred[6]{0:T(512)(128)(4,1)S(1)}...) fusion(f32[6,1]{0,1:T(1,128)S(1)} %get-tuple-element.788, ...), kind=kLoop, calls=%fused_computation.196.clone.1 | loop fusion | flops 216 | bytes 312 | tf_op jit(solution)/shard_map/while/body/eval_jaxpr/ge | solution.py:54
  69.8 11.3 %compare_bitcast_fusion.50 = (pred[6]{0:T(512)(128)(4,1)S(1)}, pred[6]{0:T(512)(128)(4,1)S(1)}, pred[6]{0:T(512)(128)(4,1)S(1)}, pred[6]{0:T(512)(128)(4,1)S(1)}...) fusion(f32[6,1]{0,1:T(1,128)S(1)} %get-tuple-element.788, ...), kind=kLoop, calls=%fused_computation.196.clone.1 | loop fusion | flops 216 | bytes 312 | tf_op jit(solution)/shard_map/while/body/eval_jaxpr/ge | solution.py:54
  90.1 11.3 %compare_bitcast_fusion.50 = (pred[6]{0:T(512)(128)(4,1)S(1)}, pred[6]{0:T(512)(128)(4,1)S(1)}, pred[6]{0:T(512)(128)(4,1)S(1)}, pred[6]{0:T(512)(128)(4,1)S(1)}...) fusion(f32[6,1]{0,1:T(1,128)S(1)} %get-tuple-element.788, ...), kind=kLoop, calls=%fused_computation.196.clone.1 | loop fusion | flops 216 | bytes 312 | tf_op jit(solution)/shard_map/while/body/eval_jaxpr/ge | solution.py:54
  110.3 11.3 %compare_bitcast_fusion.50 = (pred[6]{0:T(512)(128)(4,1)S(1)}, pred[6]{0:T(512)(128)(4,1)S(1)}, pred[6]{0:T(512)(128)(4,1)S(1)}, pred[6]{0:T(512)(128)(4,1)S(1)}...) fusion(f32[6,1]{0,1:T(1,128)S(1)} %get-tuple-element.788, ...), kind=kLoop, calls=%fused_computation.196.clone.1 | loop fusion | flops 216 | bytes 312 | tf_op jit(solution)/shard_map/while/body/eval_jaxpr/ge | solution.py:54
  130.6 11.3 %compare_bitcast_fusion.50 = (pred[6]{0:T(512)(128)(4,1)S(1)}, pred[6]{0:T(512)(128)(4,1)S(1)}, pred[6]{0:T(512)(128)(4,1)S(1)}, pred[6]{0:T(512)(128)(4,1)S(1)}...) fusion(f32[6,1]{0,1:T(1,128)S(1)} %get-tuple-element.788, ...), kind=kLoop, calls=%fused_computation.196.clone.1 | loop fusion | flops 216 | bytes 312 | tf_op jit(solution)/shard_map/while/body/eval_jaxpr/ge | solution.py:54
  150.9 11.3 %compare_bitcast_fusion.50 = (pred[6]{0:T(512)(128)(4,1)S(1)}, pred[6]{0:T(512)(128)(4,1)S(1)}, pred[6]{0:T(512)(128)(4,1)S(1)}, pred[6]{0:T(512)(128)(4,1)S(1)}...) fusion(f32[6,1]{0,1:T(1,128)S(1)} %get-tuple-element.788, ...), kind=kLoop, calls=%fused_computation.196.clone.1 | loop fusion | flops 216 | bytes 312 | tf_op jit(solution)/shard_map/while/body/eval_jaxpr/ge | solution.py:54
  171.2 11.3 %compare_bitcast_fusion.50 = (pred[6]{0:T(512)(128)(4,1)S(1)}, pred[6]{0:T(512)(128)(4,1)S(1)}, pred[6]{0:T(512)(128)(4,1)S(1)}, pred[6]{0:T(512)(128)(4,1)S(1)}...) fusion(f32[6,1]{0,1:T(1,128)S(1)} %get-tuple-element.788, ...), kind=kLoop, calls=%fused_computation.196.clone.1 | loop fusion | flops 216 | bytes 312 | tf_op jit(solution)/shard_map/while/body/eval_jaxpr/ge | solution.py:54
  191.4 11.3 %compare_bitcast_fusion.50 = (pred[6]{0:T(512)(128)(4,1)S(1)}, pred[6]{0:T(512)(128)(4,1)S(1)}, pred[6]{0:T(512)(128)(4,1)S(1)}, pred[6]{0:T(512)(128)(4,1)S(1)}...) fusion(f32[6,1]{0,1:T(1,128)S(1)} %get-tuple-element.788, ...), kind=kLoop, calls=%fused_computation.196.clone.1 | loop fusion | flops 216 | bytes 312 | tf_op jit(solution)/shard_map/while/body/eval_jaxpr/ge | solution.py:54
  211.7 11.3 %compare_bitcast_fusion.50 = (pred[6]{0:T(512)(128)(4,1)S(1)}, pred[6]{0:T(512)(128)(4,1)S(1)}, pred[6]{0:T(512)(128)(4,1)S(1)}, pred[6]{0:T(512)(128)(4,1)S(1)}...) fusion(f32[6,1]{0,1:T(1,128)S(1)} %get-tuple-element.788, ...), kind=kLoop, calls=%fused_computation.196.clone.1 | loop fusion | flops 216 | bytes 312 | tf_op jit(solution)/shard_map/while/body/eval_jaxpr/ge | solution.py:54
  231.9 11.3 %compare_bitcast_fusion.50 = (pred[6]{0:T(512)(128)(4,1)S(1)}, pred[6]{0:T(512)(128)(4,1)S(1)}, pred[6]{0:T(512)(128)(4,1)S(1)}, pred[6]{0:T(512)(128)(4,1)S(1)}...) fusion(f32[6,1]{0,1:T(1,128)S(1)} %get-tuple-element.788, ...), kind=kLoop, calls=%fused_computation.196.clone.1 | loop fusion | flops 216 | bytes 312 | tf_op jit(solution)/shard_map/while/body/eval_jaxpr/ge | solution.py:54
  252.2 11.3 %compare_bitcast_fusion.50 = (pred[6]{0:T(512)(128)(4,1)S(1)}, pred[6]{0:T(512)(128)(4,1)S(1)}, pred[6]{0:T(512)(128)(4,1)S(1)}, pred[6]{0:T(512)(128)(4,1)S(1)}...) fusion(f32[6,1]{0,1:T(1,128)S(1)} %get-tuple-element.788, ...), kind=kLoop, calls=%fused_computation.196.clone.1 | loop fusion | flops 216 | bytes 312 | tf_op jit(solution)/shard_map/while/body/eval_jaxpr/ge | solution.py:54
  272.5 11.3 %compare_bitcast_fusion.50 = (pred[6]{0:T(512)(128)(4,1)S(1)}, pred[6]{0:T(512)(128)(4,1)S(1)}, pred[6]{0:T(512)(128)(4,1)S(1)}, pred[6]{0:T(512)(128)(4,1)S(1)}...) fusion(f32[6,1]{0,1:T(1,128)S(1)} %get-tuple-element.788, ...), kind=kLoop, calls=%fused_computation.196.clone.1 | loop fusion | flops 216 | bytes 312 | tf_op jit(solution)/shard_map/while/body/eval_jaxpr/ge | solution.py:54
  292.7 11.3 %compare_bitcast_fusion.50 = (pred[6]{0:T(512)(128)(4,1)S(1)}, pred[6]{0:T(512)(128)(4,1)S(1)}, pred[6]{0:T(512)(128)(4,1)S(1)}, pred[6]{0:T(512)(128)(4,1)S(1)}...) fusion(f32[6,1]{0,1:T(1,128)S(1)} %get-tuple-element.788, ...), kind=kLoop, calls=%fused_computation.196.clone.1 | loop fusion | flops 216 | bytes 312 | tf_op jit(solution)/shard_map/while/body/eval_jaxpr/ge | solution.py:54
  313.0 11.3 %compare_bitcast_fusion.50 = (pred[6]{0:T(512)(128)(4,1)S(1)}, pred[6]{0:T(512)(128)(4,1)S(1)}, pred[6]{0:T(512)(128)(4,1)S(1)}, pred[6]{0:T(512)(128)(4,1)S(1)}...) fusion(f32[6,1]{0,1:T(1,128)S(1)} %get-tuple-element.788, ...), kind=kLoop, calls=%fused_computation.196.clone.1 | loop fusion | flops 216 | bytes 312 | tf_op jit(solution)/shard_map/while/body/eval_jaxpr/ge | solution.py:54
  333.2 11.3 %compare_bitcast_fusion.50 = (pred[6]{0:T(512)(128)(4,1)S(1)}, pred[6]{0:T(512)(128)(4,1)S(1)}, pred[6]{0:T(512)(128)(4,1)S(1)}, pred[6]{0:T(512)(128)(4,1)S(1)}...) fusion(f32[6,1]{0,1:T(1,128)S(1)} %get-tuple-element.788, ...), kind=kLoop, calls=%fused_computation.196.clone.1 | loop fusion | flops 216 | bytes 312 | tf_op jit(solution)/shard_map/while/body/eval_jaxpr/ge | solution.py:54
  347.5 9.5 %gather_fusion = f32[512,6,768]{2,1,0:T(8,128)} fusion(f32[360,6,768]{2,1,0:T(8,128)} %bitcast.466, s32[1024]{0:T(1024)S(1)} %pad_clamp_fusion), kind=kCustom, calls=%fused_computation | custom fusion | bytes 18876416 | tf_op jit(solution)/shard_map/jit(_take)/gather | solution.py:120
  357.0 10.3 %fusion.54 = bf16[512,6,768,1]{2,0,3,1:T(8,128)(2,1)} fusion(f32[512,6,768]{2,1,0:T(8,128)} %gather_fusion, f32[768]{0:T(1024)S(1)} %get-tuple-element.164, f32[6]{0:T(128)S(1)} %dynamic_slice.18, f32[512]{0:T(512)S(1)} %get-tuple-element.300, pred[512]{0:T(512)(128)(4,1)S(1)} %get-tuple-element.299), kind=kLoop, calls=%fused_computation.297 | loop fusion | flops 11796480 | bytes 14161432 | tf_op jit(solution)/shard_map/convert_element_type | solution.py:123
  367.3 4.3 copy.123
  371.6 5.3 reshape.1016
  376.9 4.7 convolution_convert_fusion.4
  384.6 61.6 %all_to_all.153 = bf16[512,12,96]{2,1,0:T(8,128)(2,1)S(1)} all-to-all(bf16[512,12,96]{2,1,0:T(8,128)(2,1)} %copy.127), channel_id=1, replica_groups=mesh['lat'=64,'chan'=4] {'lat'}, dimensions={0} | all-to-all | bytes 2359296 | tf_op jit(solution)/shard_map/all_to_all | solution.py:154
  448.3 4.2 all-to-all-start.2
  456.2 4.7 copy.146
  460.9 7.5 all-to-all-done.2
  468.4 7.0 all-to-all-start.6
  479.8 69.1 %all-to-all-done.6 = bf16[12,96,768]{1,0,2:T(8,128)(2,1)} async-done(((bf16[12,96,768]{1,0,2:T(8,128)(2,1)}), bf16[12,96,768]{1,0,2:T(8,128)(2,1)}, u32[]{:S(2)}, u32[]{:S(2)}) %all-to-all-start.6) | async-done | bytes 1769504 | tf_op jit(solution)/shard_map/all_to_all | solution.py:105
  548.9 6.1 all-to-all-start.3
  554.9 4.3 copy.148
  559.2 5.3 reshape.1024
  564.5 5.7 convolution_convert_fusion.2
  570.3 4.3 copy.150
  574.6 11.7 %all-to-all-done.3 = bf16[2,768,384]{2,0,1:T(2,128)(2,1)S(1)} async-done(((bf16[2,768,384]{2,0,1:T(2,128)(2,1)}), bf16[2,768,384]{2,0,1:T(2,128)(2,1)S(1)}, u32[]{:S(2)}, u32[]{:S(2)}) %all-to-all-start.3) | async-done | bytes 1179680 | tf_op jit(solution)/shard_map/all_to_all | solution.py:168
  586.3 6.8 all-to-all-start.7
  600.1 44.0 %all-to-all-done.7 = bf16[512,12,96]{2,1,0:T(8,128)(2,1)} async-done(((bf16[512,12,96]{2,1,0:T(8,128)(2,1)}), bf16[512,12,96]{2,1,0:T(8,128)(2,1)}, u32[]{:S(2)}, u32[]{:S(2)}) %all-to-all-start.7) | async-done | bytes 1179680 | tf_op jit(solution)/shard_map/all_to_all | solution.py:147
  653.7 14.4 %all-to-all-done.4 = bf16[128,12,384]{0,1,2:T(8,128)(2,1)S(1)} async-done(((bf16[128,12,384]{0,1,2:T(8,128)(2,1)}), bf16[128,12,384]{0,1,2:T(8,128)(2,1)S(1)}, u32[]{:S(2)}, u32[]{:S(2)}) %all-to-all-start.4) | async-done | bytes 1179680 | tf_op jit(solution)/shard_map/all_to_all | solution.py:167
  668.1 4.3 all-to-all-start.8
  680.6 4.7 copy.140
  687.8 8.3 %all-to-all-start.5 = ((bf16[768,96,12]{1,2,0:T(8,128)(2,1)}), bf16[768,96,12]{1,2,0:T(8,128)(2,1)}, u32[]{:S(2)}, u32[]{:S(2)}) async-start(bf16[768,96,12]{1,2,0:T(8,128)(2,1)} %copy.140), calls=%async_computation.5 | async-start | bytes 6291456 | tf_op jit(solution)/shard_map/all_to_all | solution.py:182
  704.6 64.9 %all-to-all-done.5 = bf16[768,96,12]{1,2,0:T(8,128)(2,1)} async-done(((bf16[768,96,12]{1,2,0:T(8,128)(2,1)}), bf16[768,96,12]{1,2,0:T(8,128)(2,1)}, u32[]{:S(2)}, u32[]{:S(2)}) %all-to-all-start.5) | async-done | bytes 1769504 | tf_op jit(solution)/shard_map/all_to_all | solution.py:182
  769.5 4.3 copy.142
  773.8 5.5 all_to_all.132
  779.3 4.5 convolution_convert_fusion.1
  (561 shorter events, 191.2 us)
Async XLA Ops:
  0.6 19.8 %copy-start = (bf16[12,96,720]{2,1,0:T(8,128)(2,1)S(1)}, bf16[12,96,720]{2,1,0:T(8,128)(2,1)}, u32[]{:S(2)}) copy-start(bf16[12,96,720]{2,1,0:T(8,128)(2,1)} %param.8) | copy-start | bytes 4976644
  28.3 14.2 %copy-start.5 = (s32[64]{0:T(128)S(1)}, s32[64]{0:T(128)}, u32[]{:S(2)}) copy-start(s32[64]{0:T(128)} %param.10) | copy-start | bytes 772
  28.3 339.0 %all-to-all-start = ((bf16[12,96,768]{1,0,2:T(8,128)(2,1)}), bf16[12,96,768]{1,0,2:T(8,128)(2,1)}, u32[]{:S(2)}, u32[]{:S(2)}) async-start(bf16[12,96,768]{1,0,2:T(8,128)(2,1)} %copy.121), calls=%async_computation | async-start | bytes 6291456 | tf_op jit(solution)/shard_map/all_to_all | solution.py:106
  43.4 304.1 %copy-start.4 = (s32[512]{0:T(512)S(1)}, s32[512]{0:T(512)}, u32[]{:S(2)}) copy-start(s32[512]{0:T(512)} %param.11) | copy-start | bytes 6148
  448.3 20.1 %all-to-all-start.2 = ((bf16[8,768,96]{1,2,0:T(8,128)(2,1)}), bf16[8,768,96]{1,2,0:T(8,128)(2,1)S(1)}, u32[]{:S(2)}, u32[]{:S(2)}) async-start(bf16[8,768,96]{1,2,0:T(8,128)(2,1)} %copy.130), calls=%async_computation.2 | async-start | bytes 2359296 | tf_op jit(solution)/shard_map/all_to_all | solution.py:153
  468.4 80.4 %all-to-all-start.6 = ((bf16[12,96,768]{1,0,2:T(8,128)(2,1)}), bf16[12,96,768]{1,0,2:T(8,128)(2,1)}, u32[]{:S(2)}, u32[]{:S(2)}) async-start(bf16[12,96,768]{1,0,2:T(8,128)(2,1)} %copy.146), calls=%async_computation.6 | async-start | bytes 6291456 | tf_op jit(solution)/shard_map/all_to_all | solution.py:105
  475.4 1.1 copy-start.3
  548.9 37.5 %all-to-all-start.3 = ((bf16[2,768,384]{2,0,1:T(2,128)(2,1)}), bf16[2,768,384]{2,0,1:T(2,128)(2,1)S(1)}, u32[]{:S(2)}, u32[]{:S(2)}) async-start(bf16[2,768,384]{2,0,1:T(2,128)(2,1)} %copy.133), calls=%async_computation.3 | async-start | bytes 2359296 | tf_op jit(solution)/shard_map/all_to_all | solution.py:168
  586.3 57.8 %all-to-all-start.7 = ((bf16[512,12,96]{2,1,0:T(8,128)(2,1)}), bf16[512,12,96]{2,1,0:T(8,128)(2,1)}, u32[]{:S(2)}, u32[]{:S(2)}) async-start(bf16[512,12,96]{2,1,0:T(8,128)(2,1)} %copy.150), calls=%async_computation.7 | async-start | bytes 4194304 | tf_op jit(solution)/shard_map/all_to_all | solution.py:147
  644.1 24.0 %all-to-all-start.4 = ((bf16[128,12,384]{0,1,2:T(8,128)(2,1)}), bf16[128,12,384]{0,1,2:T(8,128)(2,1)S(1)}, u32[]{:S(2)}, u32[]{:S(2)}) async-start(bf16[128,12,384]{0,1,2:T(8,128)(2,1)} %copy.135), calls=%async_computation.4 | async-start | bytes 3145728 | tf_op jit(solution)/shard_map/all_to_all | solution.py:167
  668.1 19.7 %all-to-all-start.8 = ((bf16[8,768,96]{1,2,0:T(8,128)(2,1)}), bf16[8,768,96]{1,2,0:T(8,128)(2,1)}, u32[]{:S(2)}, u32[]{:S(2)}) async-start(bf16[8,768,96]{1,2,0:T(8,128)(2,1)} %copy.153), calls=%async_computation.8 | async-start | bytes 2359296 | tf_op jit(solution)/shard_map/all_to_all | solution.py:146
  687.8 81.8 %all-to-all-start.5 = ((bf16[768,96,12]{1,2,0:T(8,128)(2,1)}), bf16[768,96,12]{1,2,0:T(8,128)(2,1)}, u32[]{:S(2)}, u32[]{:S(2)}) async-start(bf16[768,96,12]{1,2,0:T(8,128)(2,1)} %copy.140), calls=%async_computation.5 | async-start | bytes 6291456 | tf_op jit(solution)/shard_map/all_to_all | solution.py:182
  773.8 5.5 copy-start.2
  773.8 9.9 %copy-start.1 = (bf16[12,96,720]{2,1,0:T(8,128)(2,1)S(1)}, bf16[12,96,720]{2,1,0:T(8,128)(2,1)}, u32[]{:S(2)}) copy-start(bf16[12,96,720]{2,1,0:T(8,128)(2,1)} %param.8) | copy-start | bytes 4976644
where the time goes:
time: 796 us; the launch traced here: 784 us
  other arithmetic  281 us (35%)
  waiting for transfers between devices  214 us (27%)
  local copies, waits for them, and re-layouts  141 us (18%)
  blocking collectives  61.6 us (8%)
  starting transfers between devices  54.1 us (7%)
  matrix products  28.1 us (4%)
    ge x15, other arithmetic, advance(): result = jnp.where(degree >= order_col, current * jnp.exp(scale_log), 0.0)  169 us
    all_to_all x1, waiting for transfers between devices, on_device(): lax.all_to_all(spectra, 'lat', split_axis=2, concat_axis=0, tiled=True)  69.1 us
    all_to_all x1, waiting for transfers between devices, on_device(): lax.all_to_all(dspectra_in, 'lat', split_axis=0, concat_axis=2, tiled=True)  64.9 us
    all_to_all x1, blocking collectives, on_device(): lax.all_to_all(dcoeffs, 'lat', split_axis=0, concat_axis=1, tiled=True)  61.6 us
    gt x15, other arithmetic, advance(): rising = degree > order_col  56 us
    all_to_all x1, waiting for transfers between devices, on_device(): lax.all_to_all(coeffs, 'lat', split_axis=0, concat_axis=1, tiled=True)  44 us
    while x345, other arithmetic  34.9 us
    slice x30, local copies, waits for them, and re-layouts, legendre_rows(): lax.scan(advance, initial, (degree_list, upper_all, lower_all), unroll=24)  21 us
  transfers between devices with their start and end apart: 8, of which 7 were waited for; matrix products, arithmetic and copies ran while one was open for 49% of the time, Pallas kernels for 0%

commit v1 on v0

v1 whole, which is shorter than its diff:
```python
import functools
import math

import jax
import jax.numpy as jnp
import ml_dtypes
import numpy as np
from jax import lax
from jax.experimental import pallas as pl
from jax.experimental.pallas import tpu as pltpu
from jax.sharding import PartitionSpec as P

NLON = 720
L = 360
M = 360
LPAD = 384
ROWS = 6
GROUPS = 6
RESCALE = 2.0**40
RESCALE_LOG = 40.0 * math.log(2.0)
BF16 = jnp.bfloat16
F32 = jnp.float32
VMEM_BYTES = 56 * 1024 * 1024


def fourier_rows(lat_count):
    orders = np.arange(GROUPS * lat_count)
    turns = orders[:, None] * np.arange(NLON)[None, :] % NLON
    angles = turns * (2.0 * math.pi / NLON)
    live = (orders < M)[:, None] / math.sqrt(NLON)
    parts = np.stack([np.cos(angles) * live, -np.sin(angles) * live], axis=0)
    parts = parts.reshape(2, GROUPS, lat_count, NLON).transpose(1, 0, 2, 3)
    return parts.reshape(2 * GROUPS * lat_count, NLON).astype(ml_dtypes.bfloat16)


def order_norms(lat_count):
    orders = np.arange(8)[None, :] * lat_count + np.arange(lat_count)[:, None]
    logs = [
        0.5 * math.log((2.0 * m + 1.0) / (4.0 * math.pi))
        + 0.5 * math.lgamma(2.0 * m + 1.0)
        - m * math.log(2.0)
        - math.lgamma(m + 1.0)
        for m in orders.reshape(-1).tolist()
    ]
    latitudes = ROWS * lat_count
    total = np.array(logs).reshape(orders.shape) + 0.5 * math.log(2.0 * math.pi**2 / latitudes)
    return total.astype(np.float32)


def latitude_rows(lat_count):
    order = np.arange(lat_count)[None, :] * ROWS + np.arange(ROWS)[:, None]
    theta = (order.reshape(1, -1) + 0.5) * (math.pi / (ROWS * lat_count))
    return np.cos(theta).astype(np.float32), np.log(np.sin(theta)).astype(np.float32)


def whole(count):
    return [pl.BlockSpec(memory_space=pltpu.VMEM)] * count


def params():
    return pltpu.CompilerParams(vmem_limit_bytes=VMEM_BYTES)


def legendre_kernel(cosine_ref, logsine_ref, order_ref, norm_ref, slot_ref, out_ref, rows_ref):
    order = order_ref[...]
    square = order * order
    tiles = cosine_ref.shape[1] // 128
    cosines, scales = [], []
    for t in range(tiles):
        lanes = slice(128 * t, 128 * (t + 1))
        cosines.append(jnp.broadcast_to(cosine_ref[:, lanes], order.shape))
        logsine = jnp.broadcast_to(logsine_ref[:, lanes], order.shape)
        scales.append(norm_ref[...] + order * logsine + 0.5 * logsine)
    zero = jnp.zeros(order.shape, F32)
    one = jnp.ones(order.shape, F32)

    def advance(l, carry):
        degree = l.astype(F32)
        below = degree - 1.0
        upper = jnp.sqrt(
            jnp.maximum(4.0 * degree * degree - 1.0, 1.0)
            / jnp.maximum(degree * degree - square, 1.0)
        )
        lower = jnp.sqrt(
            jnp.maximum(below * below - square, 0.0)
            / jnp.maximum(4.0 * below * below - 1.0, 1.0)
        )
        rising = degree > order
        reached = degree >= order
        fresh = []
        for t in range(tiles):
            previous, current, scale = carry[3 * t : 3 * t + 3]
            value = upper * (cosines[t] * current - lower * previous)
            previous = jnp.where(rising, current, previous)
            current = jnp.where(rising, value, current)
            too_large = jnp.abs(current) > RESCALE
            factor = jnp.where(too_large, 1.0 / RESCALE, 1.0)
            previous = previous * factor
            current = current * factor
            scale = scale + jnp.where(too_large, RESCALE_LOG, 0.0)
            rows_ref[l, :, 128 * t : 128 * (t + 1)] = jnp.where(
                reached, current * jnp.exp(scale), 0.0
            )
            fresh += [previous, current, scale]
        return tuple(fresh)

    start = []
    for t in range(tiles):
        start += [zero, one, scales[t]]
    lax.fori_loop(0, L, advance, tuple(start), unroll=4)
    rows_ref[L:, :, :] = jnp.zeros((LPAD - L,) + rows_ref.shape[1:], F32)
    slots = slot_ref.shape[0]
    degrees = lax.broadcasted_iota(jnp.int32, (slots, LPAD), 1)
    pick = jnp.where((degrees == slot_ref[...]) & (degrees < L), 1.0, 0.0).astype(BF16)
    for j in range(GROUPS):
        table = rows_ref[:, j, :].astype(BF16)
        out_ref[j] = jnp.dot(pick, table, preferred_element_type=F32).astype(BF16)


def legendre_slots(rank, lat_count, slot_degree):
    slots = slot_degree.shape[0]
    latitudes = ROWS * lat_count
    cosine, logsine = latitude_rows(lat_count)
    norms = lax.dynamic_slice_in_dim(jnp.asarray(order_norms(lat_count)), rank, 1)
    order = (rank + lat_count * jnp.arange(8, dtype=jnp.int32)).astype(F32)
    return pl.pallas_call(
        legendre_kernel,
        out_shape=jax.ShapeDtypeStruct((GROUPS, slots, latitudes), BF16),
        in_specs=whole(5),
        out_specs=whole(1)[0],
        scratch_shapes=[pltpu.VMEM((LPAD, 8, latitudes), F32)],
        compiler_params=params(),
        name="legendre",
    )(
        jnp.asarray(cosine),
        jnp.asarray(logsine),
        jnp.broadcast_to(order[:, None], (8, 128)),
        jnp.broadcast_to(norms.reshape(8, 1), (8, 128)),
        slot_degree[:, None],
    )


def analysis_kernel(
    first_ref, rank_ref, field_ref, cotan_ref, field_in_ref, cotan_in_ref, fourier_ref,
    out_ref, rows_ref,
):
    narrow = field_ref.shape[1]
    lat_count = out_ref.shape[0]
    span = 2 * narrow
    first = first_ref[0]
    odd = rank_ref[0] % 2
    for k in range(ROWS):
        own = k + odd * (ROWS - first)
        mine = (own >= 0) & ((odd == 1) | (k < first))
        theirs = jnp.where(odd == 1, k, k - first)
        for w, (here, there) in enumerate(((field_ref, field_in_ref), (cotan_ref, cotan_in_ref))):
            at = slice((2 * k + w) * narrow, (2 * k + w + 1) * narrow)

            @pl.when(mine)
            def _():
                rows_ref[at, :] = here[jnp.clip(own, 0, 2 * ROWS - 1)]

            @pl.when(jnp.logical_not(mine))
            def _():
                rows_ref[at, :] = there[jnp.clip(theirs, 0, ROWS - 1)]

    rows = rows_ref[...]
    lane = lax.broadcasted_iota(jnp.int32, (2 * lat_count, 2 * ROWS * narrow), 1)
    line = lax.broadcasted_iota(jnp.int32, (2 * lat_count, 2 * ROWS * narrow), 0)
    cotangent = (lane // narrow) % 2 == 1
    for j in range(GROUPS):
        modes = lax.dot_general(
            fourier_ref[2 * lat_count * j : 2 * lat_count * (j + 1), :],
            rows,
            (((1,), (1,)), ((), ())),
            preferred_element_type=F32,
        )
        doubled = cotangent if j > 0 else cotangent & (line % lat_count > 0)
        modes = jnp.where(doubled, 2.0 * modes, modes).astype(BF16)
        for k in range(ROWS):
            slab = jnp.concatenate(
                [
                    modes[p * lat_count : (p + 1) * lat_count, k * span : (k + 1) * span]
                    for p in range(2)
                ],
                axis=1,
            )
            out_ref[:, (j * ROWS + k) * 2 * span : (j * ROWS + k + 1) * 2 * span] = slab


def forward_kernel(modes_ref, legendre_ref, out_ref):
    width = modes_ref.shape[1] // (GROUPS * ROWS)
    for j in range(GROUPS):
        slab = jnp.concatenate(
            [
                modes_ref[:, (j * ROWS + k) * width : (j * ROWS + k + 1) * width]
                for k in range(ROWS)
            ],
            axis=0,
        )
        out_ref[:, j * width : (j + 1) * width] = jnp.dot(
            legendre_ref[j], slab, preferred_element_type=F32
        ).astype(BF16)


def degree_kernel(coeffs_ref, weights_ref, grad_ref, back_ref):
    chans, lat_count = coeffs_ref.shape[1:3]
    narrow = coeffs_ref.shape[3] // (4 * GROUPS)
    sides = [[], []]
    for jp in range(2 * GROUPS):
        for w in range(2):
            at = (2 * jp + w) * narrow
            sides[w].append(
                jnp.concatenate(
                    [coeffs_ref[0, y, :, at : at + narrow] for y in range(chans)], axis=1
                )
            )
    coeffs = jnp.concatenate(sides[0], axis=0)
    dcoeffs = jnp.concatenate(sides[1], axis=0)
    grad_ref[0] = lax.dot_general(
        coeffs, dcoeffs, (((0,), (0,)), ((), ())), preferred_element_type=F32
    )
    back = lax.dot_general(
        dcoeffs, weights_ref[0], (((1,), (1,)), ((), ())), preferred_element_type=F32
    ).astype(BF16)
    for y in range(chans):
        back_ref[0, y] = jnp.concatenate(
            [
                back[jp * lat_count : (jp + 1) * lat_count, y * narrow : (y + 1) * narrow]
                for jp in range(2 * GROUPS)
            ],
            axis=1,
        )


def backward_kernel(back_ref, legendre_ref, out_ref):
    lat_count = out_ref.shape[0]
    span = back_ref.shape[1] // GROUPS
    narrow = span // 2
    for j in range(GROUPS):
        modes = lax.dot_general(
            legendre_ref[j],
            back_ref[:, j * span : (j + 1) * span],
            (((0,), (0,)), ((), ())),
            preferred_element_type=F32,
        ).astype(BF16)
        for p in range(2):
            out_ref[:, (2 * j + p) * ROWS * narrow : (2 * j + p + 1) * ROWS * narrow] = (
                jnp.concatenate(
                    [
                        modes[k * lat_count : (k + 1) * lat_count, p * narrow : (p + 1) * narrow]
                        for k in range(ROWS)
                    ],
                    axis=1,
                )
            )


def synthesis_kernel(modes_ref, fourier_ref, out_ref):
    narrow = out_ref.shape[1]
    width = ROWS * narrow
    modes = jnp.concatenate(
        [modes_ref[:, jp * width : (jp + 1) * width] for jp in range(2 * GROUPS)], axis=0
    )
    grad = lax.dot_general(
        modes, fourier_ref[...], (((0,), (0,)), ((), ())), preferred_element_type=F32
    ).astype(BF16)
    for k in range(ROWS):
        out_ref[k] = grad[k * narrow : (k + 1) * narrow, :]


def placing_kernel(first_ref, rank_ref, mine_ref, theirs_ref, out_ref):
    odd = rank_ref[0] % 2
    first = first_ref[0]
    start = odd * first
    count = jnp.where(odd == 1, 2 * ROWS - first, first)
    for r in range(2 * ROWS):
        at = start + r
        live = r < count
        own = (at // ROWS) == odd

        @pl.when(live & own)
        def _():
            out_ref[r] = mine_ref[jnp.clip(at - odd * ROWS, 0, ROWS - 1)]

        @pl.when(live & jnp.logical_not(own))
        def _():
            out_ref[r] = theirs_ref[jnp.clip(at - (1 - odd) * ROWS, 0, ROWS - 1)]

        @pl.when(jnp.logical_not(live))
        def _():
            out_ref[r] = jnp.zeros_like(out_ref[r])


def on_device(field_in, cotangent, weights, row_counts, slot_degree):
    lat_count = lax.axis_size("lat")
    chan_count = lax.axis_size("chan")
    rank = lax.axis_index("lat")
    narrow = field_in.shape[1]
    slots = slot_degree.shape[0]
    pairs = [(i, i ^ 1) for i in range(lat_count)]
    odd = rank % 2
    first = lax.dynamic_slice_in_dim(row_counts, rank - odd, 1)
    at_rank = jnp.reshape(rank, (1,)).astype(jnp.int32)
    fourier = jnp.asarray(fourier_rows(lat_count))
    scalar = pl.BlockSpec(memory_space=pltpu.SMEM)

    field_swap = lax.ppermute(
        lax.dynamic_slice_in_dim(field_in, (1 - odd) * ROWS, ROWS), "lat", pairs
    )
    cotan_swap = lax.ppermute(
        lax.dynamic_slice_in_dim(cotangent, (1 - odd) * ROWS, ROWS), "lat", pairs
    )
    modes = pl.pallas_call(
        analysis_kernel,
        out_shape=jax.ShapeDtypeStruct((lat_count, 4 * GROUPS * ROWS * narrow), BF16),
        in_specs=[scalar, scalar] + whole(5),
        out_specs=whole(1)[0],
        scratch_shapes=[pltpu.VMEM((2 * ROWS * narrow, NLON), BF16)],
        compiler_params=params(),
        name="analysis",
    )(first, at_rank, field_in, cotangent, field_swap, cotan_swap, fourier)
    modes = lax.all_to_all(
        modes.reshape(lat_count, 2, -1), "lat", split_axis=0, concat_axis=0, tiled=True
    ).reshape(lat_count, -1)
    legendre = legendre_slots(rank, lat_count, slot_degree)
    coeffs = pl.pallas_call(
        forward_kernel,
        out_shape=jax.ShapeDtypeStruct((slots, 4 * GROUPS * narrow), BF16),
        in_specs=whole(2),
        out_specs=whole(1)[0],
        compiler_params=params(),
        name="forward",
    )(modes, legendre)
    held = weights.shape[0]
    devices = lat_count * chan_count
    coeffs = lax.all_to_all(
        coeffs.reshape(devices, held, -1), ("lat", "chan"), split_axis=0, concat_axis=0, tiled=True
    )
    coeffs = coeffs.reshape(lat_count, chan_count, held, -1).transpose(2, 1, 0, 3)
    width = weights.shape[1]
    weight_grad, back = pl.pallas_call(
        degree_kernel,
        grid=(held,),
        out_shape=(
            jax.ShapeDtypeStruct((held, width, width), F32),
            jax.ShapeDtypeStruct((held, chan_count, lat_count, 2 * GROUPS * narrow), BF16),
        ),
        in_specs=[
            pl.BlockSpec((1, chan_count, lat_count, 4 * GROUPS * narrow), lambda s: (s, 0, 0, 0)),
            pl.BlockSpec((1, width, width), lambda s: (s, 0, 0)),
        ],
        out_specs=(
            pl.BlockSpec((1, width, width), lambda s: (s, 0, 0)),
            pl.BlockSpec((1, chan_count, lat_count, 2 * GROUPS * narrow), lambda s: (s, 0, 0, 0)),
        ),
        compiler_params=params(),
        name="degree",
    )(coeffs, weights)
    back = back.transpose(2, 1, 0, 3).reshape(devices, held, -1)
    back = lax.all_to_all(back, ("lat", "chan"), split_axis=0, concat_axis=0, tiled=True)
    back = back.reshape(slots, -1)
    modes_back = pl.pallas_call(
        backward_kernel,
        out_shape=jax.ShapeDtypeStruct((lat_count, 2 * GROUPS * ROWS * narrow), BF16),
        in_specs=whole(2),
        out_specs=whole(1)[0],
        compiler_params=params(),
        name="backward",
    )(back, legendre)
    modes_back = lax.all_to_all(
        modes_back.reshape(lat_count, 2, -1), "lat", split_axis=0, concat_axis=0, tiled=True
    ).reshape(lat_count, -1)
    grad = pl.pallas_call(
        synthesis_kernel,
        out_shape=jax.ShapeDtypeStruct((ROWS, narrow, NLON), BF16),
        in_specs=whole(2),
        out_specs=whole(1)[0],
        compiler_params=params(),
        name="synthesis",
    )(modes_back, fourier)
    grad_swap = lax.ppermute(grad, "lat", pairs)
    field_grad = pl.pallas_call(
        placing_kernel,
        out_shape=jax.ShapeDtypeStruct(field_in.shape, BF16),
        in_specs=[scalar, scalar] + whole(2),
        out_specs=whole(1)[0],
        compiler_params=params(),
        name="placing",
    )(first, at_rank, grad, grad_swap)
    return field_grad, weight_grad


def solution(mesh):
    placed = (
        P("lat", "chan", None),
        P("lat", "chan", None),
        P(("lat", "chan"), None, None),
        P(),
        P(),
    )
    return jax.shard_map(
        on_device,
        mesh=mesh,
        in_specs=placed,
        out_specs=(P("lat", "chan", None), P(("lat", "chan"), None, None)),
        check_vma=False,
    )
```

time: 796 us -> 259 us (0.33); the launches traced: 784 us -> 258 us
  other arithmetic: 281 us -> 0.01 us
  waiting for transfers between devices: 214 us -> 32.5 us
  local copies, waits for them, and re-layouts: 141 us -> 27.5 us
  blocking collectives: 61.6 us -> 139 us
  Pallas kernels: 0 us -> 44.3 us
  starting transfers between devices: 54.1 us -> 14.2 us
  matrix products: 28.1 us -> 0 us
    all_to_all x8 -> x1, waiting for transfers between devices: 214 us -> 28.5 us  [on_device(): lax.all_to_all(modes.reshape(lat_count, 2, -1), 'lat', split_axis=0, conc...]
    ge x15 -> x0, other arithmetic: 169 us -> none  [advance(): result = jnp.where(degree >= order_col, current * jnp.exp(scale_log), 0.0)]
    all_to_all x1 -> x3, blocking collectives: 61.6 us -> 139 us  [the longest x1 68.9 us: on_device(): lax.all_to_all(coeffs.reshape(devices, held, -1), ('lat', 'chan'), split_...]
    gt x15 -> x0, other arithmetic: 56 us -> none  [advance(): rising = degree > order_col]
    pallas_call x0 -> x7, Pallas kernels: none -> 44.3 us  [the longest x1 12.6 us: legendre_slots(): pl.pallas_call(legendre_kernel, out_shape=jax.ShapeDtypeStruct((GROUPS, s...]
    all_to_all x8 -> x1, starting transfers between devices: 54.1 us -> 10.2 us  [on_device(): lax.all_to_all(modes.reshape(lat_count, 2, -1), 'lat', split_axis=0, conc...]
    all_to_all x14 -> x0, local copies, waits for them, and re-layouts: 36.9 us -> none  [the longest x2 9.75 us: on_device(): lax.all_to_all(dspectra_in, 'lat', split_axis=0, concat_axis=2, tiled=True)]
    while x345 -> x0, other arithmetic: 34.9 us -> none
  transfers between devices with their start and end apart: 8 -> 4, of which waited for: 7 -> 4; matrix products, arithmetic and copies ran while one was open for 49% -> 2% of each run, Pallas kernels for 0% -> 5%
where the time goes in v1:
time: 259 us; the launch traced here: 258 us
  blocking collectives  139 us (54%)
  Pallas kernels  44.3 us (17%)
  waiting for transfers between devices  32.5 us (13%)
  local copies, waits for them, and re-layouts  27.5 us (11%)
  starting transfers between devices  14.2 us (5%)
    all_to_all x1, blocking collectives, on_device(): lax.all_to_all(coeffs.reshape(devices, held, -1), ('lat', 'chan'), split_...  68.9 us
    all_to_all x1, blocking collectives, on_device(): lax.all_to_all(back, ('lat', 'chan'), split_axis=0, concat_axis=0, tiled=...  41.3 us
    all_to_all x1, blocking collectives, on_device(): lax.all_to_all(modes_back.reshape(lat_count, 2, -1), 'lat', split_axis=0,...  29.1 us
    all_to_all x1, waiting for transfers between devices, on_device(): lax.all_to_all(modes.reshape(lat_count, 2, -1), 'lat', split_axis=0, conc...  28.5 us
    pallas_call x1, Pallas kernels, legendre_slots(): pl.pallas_call(legendre_kernel, out_shape=jax.ShapeDtypeStruct((GROUPS, s...  12.6 us
    all_to_all x1, starting transfers between devices, on_device(): lax.all_to_all(modes.reshape(lat_count, 2, -1), 'lat', split_axis=0, conc...  10.2 us
    pallas_call x1, Pallas kernels, on_device(): pl.pallas_call(analysis_kernel, out_shape=jax.ShapeDtypeStruct((lat_count...  8.29 us
    pallas_call x1, Pallas kernels, on_device(): pl.pallas_call(backward_kernel, out_shape=jax.ShapeDtypeStruct((lat_count...  5.46 us
  transfers between devices with their start and end apart: 4, of which 4 were waited for; matrix products, arithmetic and copies ran while one was open for 2% of the time, Pallas kernels for 5%

profile of v1, /device:TPU:1, one launch (start us, length us, event | category | flops | bytes accessed | tf_op | source)
XLA Modules:
  0.0 258.5 jit_solution(9658705188708904203)
XLA Ops:
  0.6 0.0 copy-start
  0.7 0.0 copy-start.5
  0.7 1.4 constant_dynamic-slice_fusion.1
  2.0 3.3 %collective-permute-start.1 = (bf16[6,96,720]{2,1,0:T(8,128)(2,1)S(1)}, bf16[6,96,720]{2,1,0:T(8,128)(2,1)S(1)}, u32[]{:S(2)}, u32[]{:S(2)}) collective-permute-start(bf16[6,96,720]{2,1,0:T(8,128)(2,1)S(1)} %constant_dynamic-slice_fusion.1), channel_id=1, source_target_pairs={{0,4},{4,0},{8,12},{12,8},{16,20},{20,16},{24,28},{28,24},{32,36},... | collective-permute-start | bytes 2488328 | tf_op jit(solution)/shard_map/ppermute | solution.py:311
  5.4 0.0 copy-done
  5.4 1.0 constant_dynamic-slice_fusion.2
  6.3 0.3 collective-permute-start
  6.6 0.0 copy-done.5
  6.6 0.7 dynamic_slice.12.first_ref
  7.3 0.2 collective-permute-done.1.cotan_in_ref
  7.4 0.0 copy-start.1
  7.4 1.6 collective-permute-done.field_in_ref
  9.0 0.0 copy-start.2
  9.0 0.0 copy-done.1
  9.0 0.9 copy-done.2
  9.9 8.3 %analysis.1 = bf16[64,13824]{1,0:T(8,128)(2,1)} custom-call(s32[1]{0:T(128)} %dynamic_slice.12.first_ref, s32[1]{0:T(128)} %bitcast.rank_ref, bf16[12,96,720]{2,1,0:T(8,128)(2,1)} %field_ref.1, bf16[12,96,720]{2,1,0:T(8,128)(2,1)} %cotan_ref.1, bf16[6,96,720]{2,1,0:T(8,128)(2,1)} %copy-done.2, bf16[6,96,720]{2,1,0:T(8,128)(2,1)} %copy-done.1, ...), custom_call_target="tpu_custom_call" | custom-call | tf_op jit(solution)/shard_map/analysis/pallas_call | solution.py:314
  18.2 4.8 %reshape.40 = bf16[64,2,6912]{2,1,0:T(2,128)(2,1)} reshape(bf16[64,13824]{1,0:T(8,128)(2,1)} %analysis.1) | data formatting | bytes 3538944 | tf_op jit(solution)/shard_map/reshape | solution.py:324
  22.9 0.0 copy-start.4
  22.9 10.2 %all-to-all-start = ((bf16[64,2,6912]{2,1,0:T(2,128)(2,1)}), bf16[64,2,6912]{2,1,0:T(2,128)(2,1)S(1)}, u32[]{:S(2)}, u32[]{:S(2)}) async-start(bf16[64,2,6912]{2,1,0:T(2,128)(2,1)} %reshape.40), calls=%async_computation | async-start | bytes 3538944 | tf_op jit(solution)/shard_map/all_to_all | solution.py:323
  33.1 0.0 copy-done.4
  33.1 0.9 copy.11.slot_ref
  34.0 0.7 fusion
  34.7 0.7 broadcast_in_dim.16.order_ref
  35.4 0.7 broadcast_in_dim.18.norm_ref
  36.0 12.6 %legendre.1.legendre_ref = bf16[6,512,384]{2,1,0:T(8,128)(2,1)} custom-call(f32[1,384]{1,0:T(1,128)} %constant.38.clone.cosine_ref, f32[1,384]{1,0:T(1,128)} %constant.39.clone.logsine_ref, f32[8,128]{1,0:T(8,128)} %broadcast_in_dim.16.order_ref, f32[8,128]{1,0:T(8,128)} %broadcast_in_dim.18.norm_ref, s32[512,1]{1,0:T(8,128)} %copy.11.slot_ref), custom_call_target="tpu_custom_call" | custom-call | tf_op jit(solution)/shard_map/legendre/pallas_call | solution.py:126
  48.6 28.5 %all-to-all-done = bf16[64,2,6912]{2,1,0:T(2,128)(2,1)S(1)} async-done(((bf16[64,2,6912]{2,1,0:T(2,128)(2,1)}), bf16[64,2,6912]{2,1,0:T(2,128)(2,1)S(1)}, u32[]{:S(2)}, u32[]{:S(2)}) %all-to-all-start) | async-done | bytes 1769504 | tf_op jit(solution)/shard_map/all_to_all | solution.py:323
  77.1 1.4 copy.14
  78.5 5.2 %forward.1 = bf16[512,2304]{1,0:T(8,128)(2,1)} custom-call(bf16[64,13824]{1,0:T(8,128)(2,1)} %bitcast.17, bf16[6,512,384]{2,1,0:T(8,128)(2,1)} %legendre.1.legendre_ref), custom_call_target="tpu_custom_call" | custom-call | tf_op jit(solution)/shard_map/forward/pallas_call | solution.py:327
  83.7 4.8 %reshape.42 = bf16[256,2,2304]{2,1,0:T(2,128)(2,1)S(1)} reshape(bf16[512,2304]{1,0:T(8,128)(2,1)} %forward.1) | data formatting | bytes 4718592 | tf_op jit(solution)/shard_map/reshape | solution.py:338
  88.5 68.9 %all_to_all.20 = bf16[256,2,2304]{2,1,0:T(2,128)(2,1)S(1)} all-to-all(bf16[256,2,2304]{2,1,0:T(2,128)(2,1)S(1)} %reshape.42), channel_id=1, replica_groups=mesh['lat'=64,'chan'=4] {'lat','chan'}, dimensions={0} | all-to-all | bytes 4718592 | tf_op jit(solution)/shard_map/all_to_all | solution.py:337
  157.4 1.8 copy.17
  159.2 5.4 %degree.1 = (f32[2,384,384]{2,1,0:T(8,128)}, bf16[2,4,64,1152]{3,2,1,0:T(8,128)(2,1)}) custom-call(bf16[2,4,64,2304]{3,2,1,0:T(8,128)(2,1)} %bitcast.14, bf16[2,384,384]{2,1,0:T(8,128)(2,1)} %weights_ref.1), custom_call_target="tpu_custom_call" | custom-call | tf_op jit(solution)/shard_map/degree/pallas_call | solution.py:342
  164.6 2.5 copy.13
  167.1 41.3 %all_to_all.21 = bf16[256,2,1152]{2,1,0:T(2,128)(2,1)S(1)} all-to-all(bf16[256,2,1152]{2,1,0:T(2,128)(2,1)S(1)} %bitcast.18), channel_id=1, replica_groups=mesh['lat'=64,'chan'=4] {'lat','chan'}, dimensions={0} | all-to-all | bytes 2359296 | tf_op jit(solution)/shard_map/all_to_all | solution.py:361
  208.3 1.3 reshape.45.back_ref
  209.6 5.5 %backward.1 = bf16[64,6912]{1,0:T(8,128)(2,1)} custom-call(bf16[512,1152]{1,0:T(8,128)(2,1)} %reshape.45.back_ref, bf16[6,512,384]{2,1,0:T(8,128)(2,1)} %legendre.1.legendre_ref), custom_call_target="tpu_custom_call" | custom-call | tf_op jit(solution)/shard_map/backward/pallas_call | solution.py:363
  215.1 2.3 reshape.46
  217.4 29.1 %all_to_all.22 = bf16[64,2,3456]{2,1,0:T(2,128)(2,1)S(1)} all-to-all(bf16[64,2,3456]{2,1,0:T(2,128)(2,1)S(1)} %reshape.46), channel_id=1, replica_groups=mesh['lat'=64,'chan'=4] {'lat'}, dimensions={0} | all-to-all | bytes 1769472 | tf_op jit(solution)/shard_map/all_to_all | solution.py:371
  246.5 1.0 copy.15
  247.5 3.7 %synthesis.1.mine_ref = bf16[6,96,720]{2,1,0:T(8,128)(2,1)} custom-call(bf16[64,6912]{1,0:T(8,128)(2,1)} %bitcast.19, bf16[768,720]{1,0:T(8,128)(2,1)} %constant.36.clone.fourier_ref), custom_call_target="tpu_custom_call" | custom-call | tf_op jit(solution)/shard_map/synthesis/pallas_call | solution.py:374
  251.2 0.4 collective-permute-start.2
  251.6 2.3 collective-permute-done.2.theirs_ref
  253.8 0.0 copy-start.3
  253.8 0.9 copy-done.3
  254.8 3.7 %placing.1 = bf16[12,96,720]{2,1,0:T(8,128)(2,1)} custom-call(s32[1]{0:T(128)} %dynamic_slice.12.first_ref, s32[1]{0:T(128)} %bitcast.rank_ref, bf16[6,96,720]{2,1,0:T(8,128)(2,1)} %synthesis.1.mine_ref, bf16[6,96,720]{2,1,0:T(8,128)(2,1)} %copy-done.3), custom_call_target="tpu_custom_call" | custom-call | tf_op jit(solution)/shard_map/placing/pallas_call | solution.py:383
  (1 shorter events, 0.0 us)
Async XLA Ops:
  0.6 4.7 %copy-start = (bf16[12,96,720]{2,1,0:T(8,128)(2,1)S(1)}, bf16[12,96,720]{2,1,0:T(8,128)(2,1)}, u32[]{:S(2)}) copy-start(bf16[12,96,720]{2,1,0:T(8,128)(2,1)} %field_ref.1) | copy-start | bytes 4976644
  0.7 5.9 %copy-start.5 = (s32[64]{0:T(128)S(1)}, s32[64]{0:T(128)}, u32[]{:S(2)}) copy-start(s32[64]{0:T(128)} %param.12) | copy-start | bytes 772
  2.0 5.4 %collective-permute-start.1 = (bf16[6,96,720]{2,1,0:T(8,128)(2,1)S(1)}, bf16[6,96,720]{2,1,0:T(8,128)(2,1)S(1)}, u32[]{:S(2)}, u32[]{:S(2)}) collective-permute-start(bf16[6,96,720]{2,1,0:T(8,128)(2,1)S(1)} %constant_dynamic-slice_fusion.1), channel_id=1, source_target_pairs={{0,4},{4,0},{8,12},{12,8},{16,20},{20,16},{24,28},{28,24},{32,36},... | collective-permute-start | bytes 2488328 | tf_op jit(solution)/shard_map/ppermute | solution.py:311
  6.3 2.6 %collective-permute-start = (bf16[6,96,720]{2,1,0:T(8,128)(2,1)}, bf16[6,96,720]{2,1,0:T(8,128)(2,1)S(1)}, u32[]{:S(2)}, u32[]{:S(2)}) collective-permute-start(bf16[6,96,720]{2,1,0:T(8,128)(2,1)} %constant_dynamic-slice_fusion.2), channel_id=1, source_target_pairs={{0,4},{4,0},{8,12},{12,8},{16,20},{20,16},{24,28},{28,24},{32,36},... | collective-permute-start | bytes 2488328 | tf_op jit(solution)/shard_map/ppermute | solution.py:308
  7.4 1.6 copy-start.1
  9.0 0.9 copy-start.2
  22.9 10.2 %copy-start.4 = (s32[512]{0:T(512)S(1)}, s32[512]{0:T(512)}, u32[]{:S(2)}) copy-start(s32[512]{0:T(512)} %param.13) | copy-start | bytes 6148
  22.9 54.2 %all-to-all-start = ((bf16[64,2,6912]{2,1,0:T(2,128)(2,1)}), bf16[64,2,6912]{2,1,0:T(2,128)(2,1)S(1)}, u32[]{:S(2)}, u32[]{:S(2)}) async-start(bf16[64,2,6912]{2,1,0:T(2,128)(2,1)} %reshape.40), calls=%async_computation | async-start | bytes 3538944 | tf_op jit(solution)/shard_map/all_to_all | solution.py:323
  251.2 2.7 %collective-permute-start.2 = (bf16[6,96,720]{2,1,0:T(8,128)(2,1)}, bf16[6,96,720]{2,1,0:T(8,128)(2,1)S(1)}, u32[]{:S(2)}, u32[]{:S(2)}) collective-permute-start(bf16[6,96,720]{2,1,0:T(8,128)(2,1)} %synthesis.1.mine_ref), channel_id=1, source_target_pairs={{0,4},{4,0},{8,12},{12,8},{16,20},{20,16},{24,28},{28,24},{32,36},... | collective-permute-start | bytes 2488328 | tf_op jit(solution)/shard_map/ppermute | solution.py:382
  253.8 1.0 copy-start.3

commit v2 on v1

v2 whole, which is shorter than its diff:
```python
import functools
import math

import jax
import jax.numpy as jnp
import ml_dtypes
import numpy as np
from jax import lax
from jax.experimental import pallas as pl
from jax.experimental.pallas import tpu as pltpu
from jax.sharding import PartitionSpec as P

NLON = 720
L = 360
M = 360
LPAD = 384
ROWS = 6
GROUPS = 6
RESCALE = 2.0**40
RESCALE_LOG = 40.0 * math.log(2.0)
BF16 = jnp.bfloat16
F32 = jnp.float32
VMEM_BYTES = 56 * 1024 * 1024


def fourier_rows(lat_count):
    orders = np.arange(GROUPS * lat_count)
    turns = orders[:, None] * np.arange(NLON)[None, :] % NLON
    angles = turns * (2.0 * math.pi / NLON)
    live = (orders < M)[:, None] / math.sqrt(NLON)
    parts = np.stack([np.cos(angles) * live, -np.sin(angles) * live], axis=0)
    parts = parts.reshape(2, GROUPS, lat_count, NLON).transpose(1, 0, 2, 3)
    return parts.astype(ml_dtypes.bfloat16)


def order_norms(lat_count):
    orders = np.arange(8)[None, :] * lat_count + np.arange(lat_count)[:, None]
    logs = [
        0.5 * math.log((2.0 * m + 1.0) / (4.0 * math.pi))
        + 0.5 * math.lgamma(2.0 * m + 1.0)
        - m * math.log(2.0)
        - math.lgamma(m + 1.0)
        for m in orders.reshape(-1).tolist()
    ]
    latitudes = ROWS * lat_count
    total = np.array(logs).reshape(orders.shape) + 0.5 * math.log(2.0 * math.pi**2 / latitudes)
    return np.broadcast_to(total[:, :, None], total.shape + (128,)).astype(np.float32)


def latitude_rows(lat_count):
    grid = np.arange(lat_count)[None, :] * ROWS + np.arange(ROWS)[:, None]
    paired = grid.reshape(ROWS // 2, 2, lat_count).transpose(0, 2, 1)
    order = np.concatenate([grid.reshape(-1), paired.reshape(-1)])[None, :]
    theta = (order + 0.5) * (math.pi / (ROWS * lat_count))
    return np.cos(theta).astype(np.float32), np.log(np.sin(theta)).astype(np.float32)


def params():
    return pltpu.CompilerParams(vmem_limit_bytes=VMEM_BYTES)


def legendre_kernel(
    rank_ref, cosine_ref, logsine_ref, norm_ref, slot_ref, rows_out_ref, pairs_out_ref, rows_ref
):
    rank = rank_ref[0]
    lat_count = norm_ref.shape[0]
    latitudes = rows_out_ref.shape[2]
    shape = (8, 128)
    groups = lax.broadcasted_iota(jnp.int32, shape, 0)
    order = (rank + groups * lat_count).astype(F32)
    square = order * order
    tiles = cosine_ref.shape[1] // 128
    cosines, scales = [], []
    for t in range(tiles):
        lanes = slice(128 * t, 128 * (t + 1))
        cosines.append(jnp.broadcast_to(cosine_ref[:, lanes], shape))
        logsine = jnp.broadcast_to(logsine_ref[:, lanes], shape)
        scales.append(norm_ref[rank] + order * logsine + 0.5 * logsine)
    zero = jnp.zeros(shape, F32)
    one = jnp.ones(shape, F32)

    def advance(l, carry):
        degree = l.astype(F32)
        below = degree - 1.0
        upper = jnp.sqrt(
            jnp.maximum(4.0 * degree * degree - 1.0, 1.0)
            / jnp.maximum(degree * degree - square, 1.0)
        )
        lower = jnp.sqrt(
            jnp.maximum(below * below - square, 0.0)
            / jnp.maximum(4.0 * below * below - 1.0, 1.0)
        )
        rising = degree > order
        reached = degree >= order
        fresh = []
        for t in range(tiles):
            previous, current, scale = carry[3 * t : 3 * t + 3]
            value = upper * (cosines[t] * current - lower * previous)
            previous = jnp.where(rising, current, previous)
            current = jnp.where(rising, value, current)
            too_large = jnp.abs(current) > RESCALE
            factor = jnp.where(too_large, 1.0 / RESCALE, 1.0)
            previous = previous * factor
            current = current * factor
            scale = scale + jnp.where(too_large, RESCALE_LOG, 0.0)
            rows_ref[l, :, 128 * t : 128 * (t + 1)] = jnp.where(
                reached, current * jnp.exp(scale), 0.0
            )
            fresh += [previous, current, scale]
        return tuple(fresh)

    start = []
    for t in range(tiles):
        start += [zero, one, scales[t]]
    lax.fori_loop(0, L, advance, tuple(start), unroll=4)
    rows_ref[L:, :, :] = jnp.zeros((LPAD - L,) + rows_ref.shape[1:], F32)
    slots = slot_ref.shape[0]
    degrees = lax.broadcasted_iota(jnp.int32, (slots, LPAD), 1)
    pick = jnp.where((degrees == slot_ref[...]) & (degrees < L), 1.0, 0.0).astype(BF16)
    for j in range(GROUPS):
        for half, out_ref in enumerate((rows_out_ref, pairs_out_ref)):
            table = rows_ref[:, j, half * latitudes : (half + 1) * latitudes].astype(BF16)
            out_ref[j] = jnp.dot(pick, table, preferred_element_type=F32).astype(BF16)


def legendre_slots(at_rank, lat_count, slot_rows):
    slots = slot_rows.shape[0]
    latitudes = ROWS * lat_count
    cosine, logsine = latitude_rows(lat_count)
    vmem = pl.BlockSpec(memory_space=pltpu.VMEM)
    table = jax.ShapeDtypeStruct((GROUPS, slots, latitudes), BF16)
    return pl.pallas_call(
        legendre_kernel,
        out_shape=(table, table),
        in_specs=[pl.BlockSpec(memory_space=pltpu.SMEM)] + [vmem] * 4,
        out_specs=(vmem, vmem),
        scratch_shapes=[pltpu.VMEM((LPAD, 8, 2 * latitudes), F32)],
        compiler_params=params(),
        name="legendre",
    )(
        at_rank,
        jnp.asarray(cosine),
        jnp.asarray(logsine),
        jnp.asarray(order_norms(lat_count)),
        slot_rows[:, None],
    )


def analysis_kernel(
    counts_ref, rank_ref, field_ref, cotan_ref, field_in_ref, cotan_in_ref, fourier_ref,
    out_ref, rows_ref, sems,
):
    narrow = field_ref.shape[1]
    lat_count = out_ref.shape[0]
    width = 2 * ROWS * narrow

    @pl.when(pl.program_id(0) == 0)
    def _():
        rank = rank_ref[0]
        odd = rank % 2
        first = counts_ref[rank - odd]
        copies = []
        for k in range(ROWS):
            own = k + odd * (ROWS - first)
            mine = (own >= 0) & ((odd == 1) | (k < first))
            theirs = jnp.where(odd == 1, k, k - first)
            for w, (here, there) in enumerate(
                ((field_ref, field_in_ref), (cotan_ref, cotan_in_ref))
            ):
                target = rows_ref.at[pl.ds((2 * k + w) * narrow, narrow), :]
                sem = sems.at[2 * k + w]
                near = pltpu.make_async_copy(here.at[jnp.clip(own, 0, 2 * ROWS - 1)], target, sem)
                far = pltpu.make_async_copy(there.at[jnp.clip(theirs, 0, ROWS - 1)], target, sem)
                pl.when(mine)(near.start)
                pl.when(jnp.logical_not(mine))(far.start)
                copies.append(near)
        for copy in copies:
            copy.wait()

    modes = lax.dot_general(
        fourier_ref[...], rows_ref[...], (((1,), (1,)), ((), ())), preferred_element_type=F32
    ).astype(BF16)
    for j in range(modes.shape[0] // (2 * lat_count)):
        out_ref[:, :, j * width : (j + 1) * width] = modes[
            2 * lat_count * j : 2 * lat_count * (j + 1)
        ].reshape(lat_count, 2, width)


def forward_kernel(rank_ref, modes_ref, legendre_ref, out_ref):
    groups = legendre_ref.shape[0]
    lat_count = modes_ref.shape[1]
    width = modes_ref.shape[2] // (groups * ROWS)
    narrow = width // 2
    owners = out_ref.shape[0]
    step = pl.program_id(0)
    for w in range(2):
        for j in range(groups):
            slab = jnp.concatenate(
                [
                    jnp.concatenate(
                        [
                            modes_ref[
                                p,
                                :,
                                (j * ROWS + k) * width + w * narrow : (j * ROWS + k) * width
                                + (w + 1) * narrow,
                            ]
                            for p in range(2)
                        ],
                        axis=1,
                    )
                    for k in range(ROWS)
                ],
                axis=0,
            )
            coeffs = jnp.dot(legendre_ref[j], slab, preferred_element_type=F32)
            if w == 1:
                zonal = (rank_ref[0] == 0) & (step == 0) & (j == 0)
                coeffs = coeffs * jnp.where(zonal, 1.0, 2.0)
            at = (w * groups + j) * width
            out_ref[:, :, at : at + width] = coeffs.astype(BF16).reshape(owners, 2, width)


def side(coeffs_ref, w, steps, groups, narrow):
    chans = coeffs_ref.shape[1]
    rows = []
    for i in range(steps):
        for j in range(groups):
            for p in range(2):
                at = (((i * 2 + w) * groups + j) * 2 + p) * narrow
                rows.append(
                    jnp.concatenate(
                        [coeffs_ref[0, y, :, at : at + narrow] for y in range(chans)], axis=1
                    )
                )
    return jnp.concatenate(rows, axis=0)


def degree_kernel(steps, coeffs_ref, weights_ref, back_ref):
    chans, lat_count = coeffs_ref.shape[1:3]
    narrow = coeffs_ref.shape[3] // (4 * GROUPS)
    dcoeffs = side(coeffs_ref, 1, steps, GROUPS // steps, narrow)
    back = lax.dot_general(
        dcoeffs, weights_ref[0], (((1,), (1,)), ((), ())), preferred_element_type=F32
    ).astype(BF16)
    messages = [
        jnp.concatenate(
            [
                back[jp * lat_count : (jp + 1) * lat_count, y * narrow : (y + 1) * narrow]
                for jp in range(2 * GROUPS)
            ],
            axis=1,
        )
        for y in range(chans)
    ]
    for s in range(2):

        @pl.when(pl.program_id(0) == s)
        def _():
            for y in range(chans):
                back_ref[y * lat_count : (y + 1) * lat_count, s, :] = messages[y]


def gradient_kernel(steps, coeffs_ref, grad_ref):
    narrow = coeffs_ref.shape[3] // (4 * GROUPS)
    coeffs = side(coeffs_ref, 0, steps, GROUPS // steps, narrow)
    dcoeffs = side(coeffs_ref, 1, steps, GROUPS // steps, narrow)
    grad_ref[0] = lax.dot_general(
        coeffs, dcoeffs, (((0,), (0,)), ((), ())), preferred_element_type=F32
    )


def backward_kernel(back_ref, legendre_ref, out_ref):
    groups = legendre_ref.shape[0]
    slots = legendre_ref.shape[1]
    lat_count = out_ref.shape[0]
    span = back_ref.shape[2] // groups
    half = ROWS // 2
    for j in range(groups):
        held = back_ref[:, :, j * span : (j + 1) * span].reshape(slots, span)
        modes = lax.dot_general(
            legendre_ref[j], held, (((0,), (0,)), ((), ())), preferred_element_type=F32
        ).astype(BF16)
        for k in range(half):
            out_ref[:, :, (j * half + k) * span : (j * half + k + 1) * span] = modes[
                2 * lat_count * k : 2 * lat_count * (k + 1)
            ].reshape(lat_count, 2, span)


def synthesis_kernel(modes_ref, fourier_ref, out_ref):
    narrow = out_ref.shape[1]
    half = ROWS // 2
    modes = jnp.concatenate(
        [
            jnp.concatenate(
                [
                    modes_ref[k % 2, :, at : at + narrow]
                    for k in range(ROWS)
                    for at in [((j * half + k // 2) * 2 + p) * narrow]
                ],
                axis=1,
            )
            for j in range(GROUPS)
            for p in range(2)
        ],
        axis=0,
    )
    grad = lax.dot_general(
        modes, fourier_ref[...], (((0,), (0,)), ((), ())), preferred_element_type=F32
    ).astype(BF16)
    for k in range(ROWS):
        out_ref[k] = grad[k * narrow : (k + 1) * narrow, :]


def placing_kernel(counts_ref, rank_ref, mine_ref, theirs_ref, out_ref, empty_ref, sems):
    rank = rank_ref[0]
    odd = rank % 2
    first = counts_ref[rank - odd]
    start = odd * first
    count = jnp.where(odd == 1, 2 * ROWS - first, first)
    empty_ref[...] = jnp.zeros_like(empty_ref)
    copies = []
    for r in range(2 * ROWS):
        at = start + r
        live = r < count
        own = (at // ROWS) == odd
        target, sem = out_ref.at[r], sems.at[r]
        near = pltpu.make_async_copy(
            mine_ref.at[jnp.clip(at - odd * ROWS, 0, ROWS - 1)], target, sem
        )
        far = pltpu.make_async_copy(
            theirs_ref.at[jnp.clip(at - (1 - odd) * ROWS, 0, ROWS - 1)], target, sem
        )
        dead = pltpu.make_async_copy(empty_ref, target, sem)
        pl.when(live & own)(near.start)
        pl.when(live & jnp.logical_not(own))(far.start)
        pl.when(jnp.logical_not(live))(dead.start)
        copies.append(near)
    for copy in copies:
        copy.wait()


def on_device(field_in, cotangent, weights, row_counts, slot_degree):
    lat_count = lax.axis_size("lat")
    chan_count = lax.axis_size("chan")
    rank = lax.axis_index("lat")
    narrow = field_in.shape[1]
    slots = slot_degree.shape[0]
    held = weights.shape[0]
    devices = lat_count * chan_count
    latitudes = ROWS * lat_count
    pairs = [(i, i ^ 1) for i in range(lat_count)]
    odd = rank % 2
    at_rank = jnp.reshape(rank, (1,)).astype(jnp.int32)
    table = fourier_rows(lat_count)
    by_part = jnp.asarray(table.reshape(-1, NLON))
    by_rank = jnp.asarray(table.transpose(0, 2, 1, 3).reshape(-1, NLON))
    scalar = pl.BlockSpec(memory_space=pltpu.SMEM)
    vmem = pl.BlockSpec(memory_space=pltpu.VMEM)
    hbm = pl.BlockSpec(memory_space=pl.ANY)
    step = 2
    steps = GROUPS // step
    everyone = ("chan", "lat")

    field_swap = lax.ppermute(
        lax.dynamic_slice_in_dim(field_in, (1 - odd) * ROWS, ROWS), "lat", pairs
    )
    cotan_swap = lax.ppermute(
        lax.dynamic_slice_in_dim(cotangent, (1 - odd) * ROWS, ROWS), "lat", pairs
    )
    width = 2 * ROWS * narrow
    modes = pl.pallas_call(
        analysis_kernel,
        grid=(steps,),
        out_shape=jax.ShapeDtypeStruct((lat_count, 2, GROUPS * width), BF16),
        in_specs=[scalar, scalar, hbm, hbm, hbm, hbm]
        + [pl.BlockSpec((2 * step * lat_count, NLON), lambda i: (i, 0))],
        out_specs=pl.BlockSpec((lat_count, 2, step * width), lambda i: (0, 0, i)),
        scratch_shapes=[
            pltpu.VMEM((width, NLON), BF16),
            pltpu.SemaphoreType.DMA((2 * ROWS,)),
        ],
        compiler_params=params(),
        name="analysis",
    )(row_counts, at_rank, field_in, cotangent, field_swap, cotan_swap, by_rank)
    modes = lax.all_to_all(modes, "lat", split_axis=0, concat_axis=0, tiled=True)
    modes = modes.transpose(1, 0, 2)
    slot_rows = slot_degree.reshape(lat_count, chan_count, held).transpose(1, 0, 2).reshape(-1)
    legendre, legendre_pairs = legendre_slots(at_rank, lat_count, slot_rows)
    coeffs = pl.pallas_call(
        forward_kernel,
        grid=(steps,),
        out_shape=jax.ShapeDtypeStruct((devices, held, 4 * GROUPS * narrow), BF16),
        in_specs=[
            scalar,
            pl.BlockSpec((2, lat_count, step * width), lambda i: (0, 0, i)),
            pl.BlockSpec((step, slots, latitudes), lambda i: (i, 0, 0)),
        ],
        out_specs=pl.BlockSpec((devices, held, step * 4 * narrow), lambda i: (0, 0, i)),
        compiler_params=params(),
        name="forward",
    )(at_rank, modes, legendre)
    coeffs = lax.all_to_all(coeffs, everyone, split_axis=0, concat_axis=0, tiled=True)
    coeffs = coeffs.transpose(1, 0, 2).reshape(held, chan_count, lat_count, 4 * GROUPS * narrow)
    full = weights.shape[1]
    slot_block = pl.BlockSpec(
        (1, chan_count, lat_count, 4 * GROUPS * narrow), lambda s: (s, 0, 0, 0)
    )
    back = pl.pallas_call(
        functools.partial(degree_kernel, steps),
        grid=(held,),
        out_shape=jax.ShapeDtypeStruct((devices, held, 2 * GROUPS * narrow), BF16),
        in_specs=[slot_block, pl.BlockSpec((1, full, full), lambda s: (s, 0, 0))],
        out_specs=pl.BlockSpec((devices, held, 2 * GROUPS * narrow), lambda s: (0, 0, 0)),
        compiler_params=params(),
        name="degree",
    )(coeffs, weights)
    back = lax.all_to_all(back, everyone, split_axis=0, concat_axis=0, tiled=True)
    weight_grad = pl.pallas_call(
        functools.partial(gradient_kernel, steps),
        grid=(held,),
        out_shape=jax.ShapeDtypeStruct((held, full, full), F32),
        in_specs=[slot_block],
        out_specs=pl.BlockSpec((1, full, full), lambda s: (s, 0, 0)),
        compiler_params=params(),
        name="gradient",
    )(coeffs)
    modes_back = pl.pallas_call(
        backward_kernel,
        grid=(steps,),
        out_shape=jax.ShapeDtypeStruct((lat_count, 2, GROUPS * ROWS * narrow), BF16),
        in_specs=[
            pl.BlockSpec((devices, held, step * 2 * narrow), lambda i: (0, 0, i)),
            pl.BlockSpec((step, slots, latitudes), lambda i: (i, 0, 0)),
        ],
        out_specs=pl.BlockSpec((lat_count, 2, step * ROWS * narrow), lambda i: (0, 0, i)),
        compiler_params=params(),
        name="backward",
    )(back, legendre_pairs)
    modes_back = lax.all_to_all(modes_back, "lat", split_axis=0, concat_axis=0, tiled=True)
    grad = pl.pallas_call(
        synthesis_kernel,
        out_shape=jax.ShapeDtypeStruct((ROWS, narrow, NLON), BF16),
        in_specs=[vmem, vmem],
        out_specs=vmem,
        compiler_params=params(),
        name="synthesis",
    )(modes_back.transpose(1, 0, 2), by_part)
    grad_swap = lax.ppermute(grad, "lat", pairs)
    field_grad = pl.pallas_call(
        placing_kernel,
        out_shape=jax.ShapeDtypeStruct(field_in.shape, BF16),
        in_specs=[scalar, scalar, hbm, hbm],
        out_specs=hbm,
        scratch_shapes=[
            pltpu.VMEM((narrow, NLON), BF16),
            pltpu.SemaphoreType.DMA((2 * ROWS,)),
        ],
        compiler_params=params(),
        name="placing",
    )(row_counts, at_rank, grad, grad_swap)
    return field_grad, weight_grad


def solution(mesh):
    placed = (
        P("lat", "chan", None),
        P("lat", "chan", None),
        P(("lat", "chan"), None, None),
        P(),
        P(),
    )
    return jax.shard_map(
        on_device,
        mesh=mesh,
        in_specs=placed,
        out_specs=(P("lat", "chan", None), P(("lat", "chan"), None, None)),
        check_vma=False,
    )
```

time: 259 us -> 291 us (1.12)
  the two profiles are of different devices: /device:TPU:1 before, /device:TPU:70 now
where the time goes in v2:
time: 291 us; the launch traced here: 288 us
  blocking collectives  138 us (47%)
  Pallas kernels  104 us (36%)
  waiting for transfers between devices  24.2 us (8%)
  starting transfers between devices  11.7 us (4%)
  local copies, waits for them, and re-layouts  8.56 us (3%)
    all_to_all x1, blocking collectives, on_device(): lax.all_to_all(coeffs, everyone, split_axis=0, concat_axis=0, tiled=True)  67 us
    pallas_call x1, Pallas kernels, on_device(): pl.pallas_call(placing_kernel, out_shape=jax.ShapeDtypeStruct(field_in.sh...  55.5 us
    all_to_all x1, blocking collectives, on_device(): lax.all_to_all(back, everyone, split_axis=0, concat_axis=0, tiled=True)  39.9 us
    all_to_all x1, blocking collectives, on_device(): lax.all_to_all(modes_back, 'lat', split_axis=0, concat_axis=0, tiled=True)  30.8 us
    all_to_all x1, waiting for transfers between devices, on_device(): lax.all_to_all(modes, 'lat', split_axis=0, concat_axis=0, tiled=True)  21.1 us
    pallas_call x1, Pallas kernels, legendre_slots(): pl.pallas_call(legendre_kernel, out_shape=(table, table), in_specs=[pl.Bl...  19.9 us
    all_to_all x1, starting transfers between devices, on_device(): lax.all_to_all(modes, 'lat', split_axis=0, concat_axis=0, tiled=True)  11.3 us
    pallas_call x1, Pallas kernels, on_device(): pl.pallas_call(analysis_kernel, grid=(steps,), out_shape=jax.ShapeDtypeSt...  6.08 us
  transfers between devices with their start and end apart: 4, of which 3 were waited for; matrix products, arithmetic and copies ran while one was open for 0% of the time, Pallas kernels for 8%

profile of v2, /device:TPU:70, one launch (start us, length us, event | category | flops | bytes accessed | tf_op | source)
XLA Modules:
  0.0 287.6 jit_solution(16910546821775113047)
XLA Ops:
  0.6 0.0 copy-start
  0.7 1.4 constant_dynamic-slice_fusion
  2.0 0.1 collective-permute-start.1
  2.1 0.3 copy-done
  2.4 0.1 constant_dynamic-slice_fusion.1
  2.4 0.3 collective-permute-start
  2.8 1.8 collective-permute-done.1.cotan_in_ref
  4.5 0.0 copy-start.1
  4.5 1.3 collective-permute-done.field_in_ref
  5.8 0.0 copy-start.2
  5.8 0.0 copy-done.1
  5.8 0.9 copy-done.2
  6.7 6.1 %analysis.1 = bf16[64,2,6912]{2,1,0:T(2,128)(2,1)} custom-call(s32[64]{0:T(128)} %counts_ref.3, s32[1]{0:T(128)} %bitcast.rank_ref, bf16[12,96,720]{2,1,0:T(8,128)(2,1)} %field_ref.1, bf16[12,96,720]{2,1,0:T(8,128)(2,1)} %cotan_ref.1, bf16[6,96,720]{2,1,0:T(8,128)(2,1)} %copy-done.2, bf16[6,96,720]{2,1,0:T(8,128)(2,1)} %copy-done.1, ...), custom_call_target="tpu_custom_call" | custom-call | tf_op jit(solution)/shard_map/analysis/pallas_call | solution.py:372
  12.8 0.0 copy-start.4
  12.8 11.3 %all-to-all-start = ((bf16[64,2,6912]{2,1,0:T(2,128)(2,1)}), bf16[64,2,6912]{2,1,0:T(2,128)(2,1)S(1)}, u32[]{:S(2)}, u32[]{:S(2)}) async-start(bf16[64,2,6912]{2,1,0:T(2,128)(2,1)} %analysis.1), calls=%async_computation | async-start | bytes 3538944 | tf_op jit(solution)/shard_map/all_to_all | solution.py:386
  24.1 0.0 copy-done.4
  24.1 0.2 reshape.14
  24.3 0.8 broadcast_in_dim_reshape.4.slot_ref
  25.2 19.9 %legendre.1 = (bf16[6,512,384]{2,1,0:T(8,128)(2,1)}, bf16[6,512,384]{2,1,0:T(8,128)(2,1)}) custom-call(s32[1]{0:T(128)} %bitcast.rank_ref, f32[1,768]{1,0:T(1,128)} %constant.37.clone.cosine_ref, f32[1,768]{1,0:T(1,128)} %constant.38.clone.logsine_ref, f32[64,8,128]{2,1,0:T(8,128)} %constant.39.clone.norm_ref, s32[512,1]{1,0:T(8,128)} %broadcast_in_dim_reshape.4.slot_ref), custom_call_target="tpu_custom_call" | custom-call | tf_op jit(solution)/shard_map/legendre/pallas_call | solution.py:132
  45.1 21.1 %all-to-all-done = bf16[64,2,6912]{2,1,0:T(2,128)(2,1)S(1)} async-done(((bf16[64,2,6912]{2,1,0:T(2,128)(2,1)}), bf16[64,2,6912]{2,1,0:T(2,128)(2,1)S(1)}, u32[]{:S(2)}, u32[]{:S(2)}) %all-to-all-start) | async-done | bytes 1769504 | tf_op jit(solution)/shard_map/all_to_all | solution.py:386
  66.2 1.4 copy.27
  67.6 5.9 %forward.1 = bf16[256,2,2304]{2,1,0:T(2,128)(2,1)} custom-call(s32[1]{0:T(128)} %bitcast.rank_ref, bf16[2,64,6912]{2,1,0:T(8,128)(2,1)} %bitcast.13, bf16[6,512,384]{2,1,0:T(8,128)(2,1)} %get-tuple-element.4.legendre_ref), custom_call_target="tpu_custom_call" | custom-call | tf_op jit(solution)/shard_map/forward/pallas_call | solution.py:390
  73.5 67.0 %all_to_all.20 = bf16[256,2,2304]{2,1,0:T(2,128)(2,1)S(1)} all-to-all(bf16[256,2,2304]{2,1,0:T(2,128)(2,1)} %forward.1), channel_id=1, replica_groups=mesh['lat'=64,'chan'=4] {'chan','lat'}, dimensions={0} | all-to-all | bytes 4718592 | tf_op jit(solution)/shard_map/all_to_all | solution.py:403
  140.6 1.6 copy.23
  142.2 4.4 %degree.1 = bf16[256,2,1152]{2,1,0:T(2,128)(2,1)} custom-call(bf16[2,4,64,2304]{3,2,1,0:T(8,128)(2,1)} %bitcast.10, bf16[2,384,384]{2,1,0:T(8,128)(2,1)} %weights_ref.1), custom_call_target="tpu_custom_call" | custom-call | tf_op jit(solution)/shard_map/degree/pallas_call | solution.py:409
  146.6 39.9 %all_to_all.21.back_ref = bf16[256,2,1152]{2,1,0:T(2,128)(2,1)} all-to-all(bf16[256,2,1152]{2,1,0:T(2,128)(2,1)} %degree.1), channel_id=1, replica_groups=mesh['lat'=64,'chan'=4] {'chan','lat'}, dimensions={0} | all-to-all | bytes 2359296 | tf_op jit(solution)/shard_map/all_to_all | solution.py:418
  186.5 4.7 %backward.1 = bf16[64,2,3456]{2,1,0:T(2,128)(2,1)} custom-call(bf16[256,2,1152]{2,1,0:T(2,128)(2,1)} %all_to_all.21.back_ref, bf16[6,512,384]{2,1,0:T(8,128)(2,1)} %get-tuple-element.5.legendre_ref), custom_call_target="tpu_custom_call" | custom-call | tf_op jit(solution)/shard_map/backward/pallas_call | solution.py:428
  191.2 30.8 %all_to_all.22 = bf16[64,2,3456]{2,1,0:T(2,128)(2,1)S(1)} all-to-all(bf16[64,2,3456]{2,1,0:T(2,128)(2,1)} %backward.1), channel_id=1, replica_groups=mesh['lat'=64,'chan'=4] {'lat'}, dimensions={0} | all-to-all | bytes 1769472 | tf_op jit(solution)/shard_map/all_to_all | solution.py:440
  222.0 1.0 copy.28
  223.0 3.9 %synthesis.1.mine_ref = bf16[6,96,720]{2,1,0:T(8,128)(2,1)} custom-call(bf16[2,64,3456]{2,1,0:T(8,128)(2,1)} %bitcast.14, bf16[768,720]{1,0:T(8,128)(2,1)} %constant.35.clone.fourier_ref), custom_call_target="tpu_custom_call" | custom-call | tf_op jit(solution)/shard_map/synthesis/pallas_call | solution.py:441
  226.9 0.0 collective-permute-start.2
  226.9 4.1 %gradient.1 = f32[2,384,384]{2,1,0:T(8,128)} custom-call(bf16[2,4,64,2304]{3,2,1,0:T(8,128)(2,1)} %bitcast.11), custom_call_target="tpu_custom_call" | custom-call | tf_op jit(solution)/shard_map/gradient/pallas_call | solution.py:419
  231.0 0.0 collective-permute-done.2.theirs_ref
  231.0 0.0 copy-start.3
  231.0 0.9 copy-done.3
  231.9 55.5 %placing.1 = bf16[12,96,720]{2,1,0:T(8,128)(2,1)} custom-call(s32[64]{0:T(128)} %counts_ref.3, s32[1]{0:T(128)} %bitcast.rank_ref, bf16[6,96,720]{2,1,0:T(8,128)(2,1)} %synthesis.1.mine_ref, bf16[6,96,720]{2,1,0:T(8,128)(2,1)} %copy-done.3), custom_call_target="tpu_custom_call" | custom-call | tf_op jit(solution)/shard_map/placing/pallas_call | solution.py:450
  (1 shorter events, 0.0 us)
Async XLA Ops:
  0.6 1.7 copy-start
  2.0 2.5 collective-permute-start.1
  2.4 3.4 %collective-permute-start = (bf16[6,96,720]{2,1,0:T(8,128)(2,1)S(1)}, bf16[6,96,720]{2,1,0:T(8,128)(2,1)S(1)}, u32[]{:S(2)}, u32[]{:S(2)}) collective-permute-start(bf16[6,96,720]{2,1,0:T(8,128)(2,1)S(1)} %constant_dynamic-slice_fusion.1), channel_id=1, source_target_pairs={{0,4},{4,0},{8,12},{12,8},{16,20},{20,16},{24,28},{28,24},{32,36},... | collective-permute-start | bytes 2488328 | tf_op jit(solution)/shard_map/ppermute | solution.py:365
  4.5 1.3 copy-start.1
  5.8 0.9 copy-start.2
  12.8 11.3 %copy-start.4 = (s32[512]{0:T(512)S(1)}, s32[512]{0:T(512)}, u32[]{:S(2)}) copy-start(s32[512]{0:T(512)} %param.14) | copy-start | bytes 6148
  12.8 53.4 %all-to-all-start = ((bf16[64,2,6912]{2,1,0:T(2,128)(2,1)}), bf16[64,2,6912]{2,1,0:T(2,128)(2,1)S(1)}, u32[]{:S(2)}, u32[]{:S(2)}) async-start(bf16[64,2,6912]{2,1,0:T(2,128)(2,1)} %analysis.1), calls=%async_computation | async-start | bytes 3538944 | tf_op jit(solution)/shard_map/all_to_all | solution.py:386
  226.9 4.1 %collective-permute-start.2 = (bf16[6,96,720]{2,1,0:T(8,128)(2,1)}, bf16[6,96,720]{2,1,0:T(8,128)(2,1)S(1)}, u32[]{:S(2)}, u32[]{:S(2)}) collective-permute-start(bf16[6,96,720]{2,1,0:T(8,128)(2,1)} %synthesis.1.mine_ref), channel_id=1, source_target_pairs={{0,4},{4,0},{8,12},{12,8},{16,20},{20,16},{24,28},{28,24},{32,36},... | collective-permute-start | bytes 2488328 | tf_op jit(solution)/shard_map/ppermute | solution.py:449
  231.0 0.9 copy-start.3

commit v3 on v2

v3 whole, which is shorter than its diff:
```python
import math

import jax
import jax.numpy as jnp
import ml_dtypes
import numpy as np
from jax import lax
from jax.experimental import pallas as pl
from jax.experimental.pallas import tpu as pltpu
from jax.sharding import PartitionSpec as P

NLON = 720
L = 360
M = 360
LPAD = 384
ROWS = 6
GROUPS = 6
RESCALE = 2.0**40
RESCALE_LOG = 40.0 * math.log(2.0)
BF16 = jnp.bfloat16
F32 = jnp.float32
VMEM_BYTES = 30 * 1024 * 1024


def fourier_rows(lat_count):
    orders = np.arange(GROUPS * lat_count)
    turns = orders[:, None] * np.arange(NLON)[None, :] % NLON
    angles = turns * (2.0 * math.pi / NLON)
    live = (orders < M)[:, None] / math.sqrt(NLON)
    parts = np.stack([np.cos(angles) * live, -np.sin(angles) * live], axis=0)
    parts = parts.reshape(2, GROUPS, lat_count, NLON).transpose(1, 0, 2, 3)
    return parts.astype(ml_dtypes.bfloat16)


def order_norms(lat_count):
    orders = np.arange(8)[None, :] * lat_count + np.arange(lat_count)[:, None]
    logs = [
        0.5 * math.log((2.0 * m + 1.0) / (4.0 * math.pi))
        + 0.5 * math.lgamma(2.0 * m + 1.0)
        - m * math.log(2.0)
        - math.lgamma(m + 1.0)
        for m in orders.reshape(-1).tolist()
    ]
    latitudes = ROWS * lat_count
    total = np.array(logs).reshape(orders.shape) + 0.5 * math.log(2.0 * math.pi**2 / latitudes)
    return np.broadcast_to(total[:, :, None], total.shape + (128,)).astype(np.float32)


def latitude_rows(lat_count):
    grid = np.arange(lat_count)[None, :] * ROWS + np.arange(ROWS)[:, None]
    paired = grid.reshape(ROWS // 2, 2, lat_count).transpose(0, 2, 1)
    order = np.concatenate([grid.reshape(-1), paired.reshape(-1)])[None, :]
    theta = (order + 0.5) * (math.pi / (ROWS * lat_count))
    return np.cos(theta).astype(np.float32), np.log(np.sin(theta)).astype(np.float32)


def run(kernel, name, outs, args, scratch=(), home=pltpu.VMEM):
    vmem = pl.BlockSpec(memory_space=pltpu.VMEM)
    scalar = pl.BlockSpec(memory_space=pltpu.SMEM)
    specs, operands = [], []
    for arg in args:
        small = arg.dtype == jnp.int32 and arg.ndim == 1
        specs.append(scalar if small else vmem)
        operands.append(arg if small else pltpu.with_memory_space_constraint(arg, pltpu.VMEM))
    results = pl.pallas_call(
        kernel,
        out_shape=tuple(outs),
        in_specs=specs,
        out_specs=tuple(pl.BlockSpec(memory_space=home) for _ in outs),
        scratch_shapes=list(scratch),
        compiler_params=pltpu.CompilerParams(vmem_limit_bytes=VMEM_BYTES),
        name=name,
    )(*operands)
    return results if len(outs) > 1 else results[0]


def legendre_kernel(
    rank_ref, cosine_ref, logsine_ref, norm_ref, slot_ref, rows_out_ref, pairs_out_ref, rows_ref
):
    rank = rank_ref[0]
    lat_count = norm_ref.shape[0]
    latitudes = rows_out_ref.shape[2]
    shape = (8, 128)
    groups = lax.broadcasted_iota(jnp.int32, shape, 0)
    order = (rank + groups * lat_count).astype(F32)
    square = order * order
    tiles = cosine_ref.shape[1] // 128
    cosines, scales = [], []
    for t in range(tiles):
        lanes = slice(128 * t, 128 * (t + 1))
        cosines.append(jnp.broadcast_to(cosine_ref[:, lanes], shape))
        logsine = jnp.broadcast_to(logsine_ref[:, lanes], shape)
        scales.append(norm_ref[rank] + order * logsine + 0.5 * logsine)
    zero = jnp.zeros(shape, F32)
    one = jnp.ones(shape, F32)

    def advance(l, carry):
        degree = l.astype(F32)
        below = degree - 1.0
        upper = jnp.sqrt(
            jnp.maximum(4.0 * degree * degree - 1.0, 1.0)
            / jnp.maximum(degree * degree - square, 1.0)
        )
        lower = jnp.sqrt(
            jnp.maximum(below * below - square, 0.0)
            / jnp.maximum(4.0 * below * below - 1.0, 1.0)
        )
        rising = degree > order
        reached = degree >= order
        fresh = []
        for t in range(tiles):
            previous, current, scale = carry[3 * t : 3 * t + 3]
            value = upper * (cosines[t] * current - lower * previous)
            previous = jnp.where(rising, current, previous)
            current = jnp.where(rising, value, current)
            too_large = jnp.abs(current) > RESCALE
            factor = jnp.where(too_large, 1.0 / RESCALE, 1.0)
            previous = previous * factor
            current = current * factor
            scale = scale + jnp.where(too_large, RESCALE_LOG, 0.0)
            rows_ref[l, :, 128 * t : 128 * (t + 1)] = jnp.where(
                reached, current * jnp.exp(scale), 0.0
            )
            fresh += [previous, current, scale]
        return tuple(fresh)

    start = []
    for t in range(tiles):
        start += [zero, one, scales[t]]
    lax.fori_loop(0, L, advance, tuple(start), unroll=4)
    rows_ref[L:, :, :] = jnp.zeros((LPAD - L,) + rows_ref.shape[1:], F32)
    slots = slot_ref.shape[0]
    degrees = lax.broadcasted_iota(jnp.int32, (slots, LPAD), 1)
    pick = jnp.where((degrees == slot_ref[...]) & (degrees < L), 1.0, 0.0).astype(BF16)
    for j in range(GROUPS):
        table = rows_ref[:, j, :latitudes].astype(BF16)
        rows_out_ref[j] = jnp.dot(pick, table, preferred_element_type=F32).astype(BF16)
        table = rows_ref[:, j, latitudes:].astype(BF16)
        pairs_out_ref[j] = lax.dot_general(
            table, pick, (((0,), (1,)), ((), ())), preferred_element_type=F32
        ).astype(BF16)


def legendre_slots(at_rank, lat_count, slot_rows):
    slots = slot_rows.shape[0]
    latitudes = ROWS * lat_count
    cosine, logsine = latitude_rows(lat_count)
    return run(
        legendre_kernel,
        "legendre",
        [pltpu.VMEM((GROUPS, slots, latitudes), BF16), pltpu.VMEM((GROUPS, latitudes, slots), BF16)],
        [
            at_rank,
            jnp.asarray(cosine),
            jnp.asarray(logsine),
            jnp.asarray(order_norms(lat_count)),
            slot_rows[:, None],
        ],
        [pltpu.VMEM((LPAD, 8, 2 * latitudes), F32)],
    )


def analysis_kernel(
    counts_ref, rank_ref, field_ref, cotan_ref, field_in_ref, cotan_in_ref, fourier_ref,
    out_ref, rows_ref,
):
    narrow = field_ref.shape[1]
    lat_count = out_ref.shape[0]
    width = 2 * ROWS * narrow
    rank = rank_ref[0]
    odd = rank % 2
    first = counts_ref[rank - odd]
    for k in range(ROWS):
        own = k + odd * (ROWS - first)
        mine = (own >= 0) & ((odd == 1) | (k < first))
        theirs = jnp.where(odd == 1, k, k - first)
        for w, (here, there) in enumerate(((field_ref, field_in_ref), (cotan_ref, cotan_in_ref))):
            at = slice((2 * k + w) * narrow, (2 * k + w + 1) * narrow)

            @pl.when(mine)
            def _():
                rows_ref[at, :] = here[jnp.clip(own, 0, 2 * ROWS - 1)]

            @pl.when(jnp.logical_not(mine))
            def _():
                rows_ref[at, :] = there[jnp.clip(theirs, 0, ROWS - 1)]

    modes = lax.dot_general(
        fourier_ref[...], rows_ref[...], (((1,), (1,)), ((), ())), preferred_element_type=F32
    ).astype(BF16)
    for j in range(GROUPS):
        out_ref[:, :, j * width : (j + 1) * width] = modes[
            2 * lat_count * j : 2 * lat_count * (j + 1)
        ].reshape(lat_count, 2, width)


def forward_kernel(rank_ref, modes_ref, legendre_ref, out_ref):
    width = modes_ref.shape[2] // (GROUPS * ROWS)
    owners = out_ref.shape[0]
    slots = legendre_ref.shape[1]
    lane = lax.broadcasted_iota(jnp.int32, (slots, 2 * width), 1)
    cotangent = lane // (width // 2) % 2 == 1
    for j in range(GROUPS):
        slab = jnp.concatenate(
            [
                jnp.concatenate(
                    [
                        modes_ref[p, :, (j * ROWS + k) * width : (j * ROWS + k + 1) * width]
                        for p in range(2)
                    ],
                    axis=1,
                )
                for k in range(ROWS)
            ],
            axis=0,
        )
        coeffs = jnp.dot(legendre_ref[j], slab, preferred_element_type=F32)
        doubled = jnp.where(rank_ref[0] + j == 0, 1.0, 2.0)
        coeffs = jnp.where(cotangent, coeffs * doubled, coeffs)
        out_ref[:, :, 2 * j * width : 2 * (j + 1) * width] = coeffs.astype(BF16).reshape(
            owners, 2, 2 * width
        )


def side(coeffs_ref, s, w):
    chans = coeffs_ref.shape[1]
    narrow = coeffs_ref.shape[3] // (4 * GROUPS)
    return jnp.concatenate(
        [
            jnp.concatenate(
                [
                    coeffs_ref[s, y, :, (2 * jp + w) * narrow : (2 * jp + w + 1) * narrow]
                    for y in range(chans)
                ],
                axis=1,
            )
            for jp in range(2 * GROUPS)
        ],
        axis=0,
    )


def degree_kernel(coeffs_ref, weights_ref, back_ref):
    chans, lat_count = coeffs_ref.shape[1:3]
    narrow = coeffs_ref.shape[3] // (4 * GROUPS)
    for s in range(2):
        back = lax.dot_general(
            side(coeffs_ref, s, 1),
            weights_ref[s],
            (((1,), (1,)), ((), ())),
            preferred_element_type=F32,
        ).astype(BF16)
        for y in range(chans):
            back_ref[y * lat_count : (y + 1) * lat_count, s, :] = jnp.concatenate(
                [
                    back[jp * lat_count : (jp + 1) * lat_count, y * narrow : (y + 1) * narrow]
                    for jp in range(2 * GROUPS)
                ],
                axis=1,
            )


def gradient_kernel(coeffs_ref, grad_ref):
    for s in range(2):
        grad_ref[s] = lax.dot_general(
            side(coeffs_ref, s, 0),
            side(coeffs_ref, s, 1),
            (((0,), (0,)), ((), ())),
            preferred_element_type=F32,
        )


def backward_kernel(back_ref, legendre_ref, out_ref):
    slots = legendre_ref.shape[2]
    lat_count = out_ref.shape[0]
    span = back_ref.shape[2] // GROUPS
    half = ROWS // 2
    for j in range(GROUPS):
        held = back_ref[:, :, j * span : (j + 1) * span].reshape(slots, span)
        modes = jnp.dot(legendre_ref[j], held, preferred_element_type=F32).astype(BF16)
        for k in range(half):
            out_ref[:, :, (j * half + k) * span : (j * half + k + 1) * span] = modes[
                2 * lat_count * k : 2 * lat_count * (k + 1)
            ].reshape(lat_count, 2, span)


def synthesis_kernel(modes_ref, fourier_ref, out_ref):
    narrow = out_ref.shape[1]
    half = ROWS // 2
    modes = jnp.concatenate(
        [
            jnp.concatenate(
                [
                    modes_ref[k % 2, :, at : at + narrow]
                    for k in range(ROWS)
                    for at in [((j * half + k // 2) * 2 + p) * narrow]
                ],
                axis=1,
            )
            for j in range(GROUPS)
            for p in range(2)
        ],
        axis=0,
    )
    grad = lax.dot_general(
        modes, fourier_ref[...], (((0,), (0,)), ((), ())), preferred_element_type=F32
    ).astype(BF16)
    for k in range(ROWS):
        out_ref[k] = grad[k * narrow : (k + 1) * narrow, :]


def placing_kernel(counts_ref, rank_ref, mine_ref, theirs_ref, out_ref, empty_ref, sems):
    rank = rank_ref[0]
    odd = rank % 2
    first = counts_ref[rank - odd]
    start = odd * first
    count = jnp.where(odd == 1, 2 * ROWS - first, first)
    empty_ref[...] = jnp.zeros_like(empty_ref)
    copies = []
    for r in range(2 * ROWS):
        at = start + r
        live = r < count
        own = (at // ROWS) == odd
        target, sem = out_ref.at[r], sems.at[r]
        near = pltpu.make_async_copy(
            mine_ref.at[jnp.clip(at - odd * ROWS, 0, ROWS - 1)], target, sem
        )
        far = pltpu.make_async_copy(
            theirs_ref.at[jnp.clip(at - (1 - odd) * ROWS, 0, ROWS - 1)], target, sem
        )
        dead = pltpu.make_async_copy(empty_ref, target, sem)
        pl.when(live & own)(near.start)
        pl.when(live & jnp.logical_not(own))(far.start)
        pl.when(jnp.logical_not(live))(dead.start)
        copies.append(near)
    for copy in copies:
        copy.wait()


def on_device(field_in, cotangent, weights, row_counts, slot_degree):
    lat_count = lax.axis_size("lat")
    chan_count = lax.axis_size("chan")
    rank = lax.axis_index("lat")
    narrow = field_in.shape[1]
    held, full = weights.shape[:2]
    devices = lat_count * chan_count
    pairs = [(i, i ^ 1) for i in range(lat_count)]
    odd = rank % 2
    at_rank = jnp.reshape(rank, (1,)).astype(jnp.int32)
    table = fourier_rows(lat_count)
    by_part = jnp.asarray(table.reshape(-1, NLON))
    by_rank = jnp.asarray(table.transpose(0, 2, 1, 3).reshape(-1, NLON))
    everyone = ("chan", "lat")

    field_swap = lax.ppermute(
        lax.dynamic_slice_in_dim(field_in, (1 - odd) * ROWS, ROWS), "lat", pairs
    )
    cotan_swap = lax.ppermute(
        lax.dynamic_slice_in_dim(cotangent, (1 - odd) * ROWS, ROWS), "lat", pairs
    )
    width = 2 * ROWS * narrow
    modes = run(
        analysis_kernel,
        "analysis",
        [pltpu.VMEM((lat_count, 2, GROUPS * width), BF16)],
        [row_counts, at_rank, field_in, cotangent, field_swap, cotan_swap, by_rank],
        [pltpu.VMEM((width, NLON), BF16)],
    )
    modes = lax.all_to_all(modes, "lat", split_axis=0, concat_axis=0, tiled=True)
    modes = modes.transpose(1, 0, 2)
    slot_rows = slot_degree.reshape(lat_count, chan_count, held).transpose(1, 0, 2).reshape(-1)
    legendre, legendre_pairs = legendre_slots(at_rank, lat_count, slot_rows)
    coeffs = run(
        forward_kernel,
        "forward",
        [pltpu.VMEM((devices, held, 4 * GROUPS * narrow), BF16)],
        [at_rank, modes, legendre],
    )
    coeffs = lax.all_to_all(coeffs, everyone, split_axis=0, concat_axis=0, tiled=True)
    coeffs = coeffs.transpose(1, 0, 2).reshape(held, chan_count, lat_count, 4 * GROUPS * narrow)
    back = run(
        degree_kernel,
        "degree",
        [pltpu.VMEM((devices, held, 2 * GROUPS * narrow), BF16)],
        [coeffs, weights],
    )
    back, coeffs = lax.optimization_barrier((back, coeffs))
    back = lax.all_to_all(back, everyone, split_axis=0, concat_axis=0, tiled=True)
    weight_grad = run(
        gradient_kernel, "gradient", [jax.ShapeDtypeStruct((held, full, full), F32)], [coeffs]
    )
    back, weight_grad = lax.optimization_barrier((back, weight_grad))
    modes_back = run(
        backward_kernel,
        "backward",
        [pltpu.VMEM((lat_count, 2, GROUPS * ROWS * narrow), BF16)],
        [back, legendre_pairs],
    )
    modes_back = lax.all_to_all(modes_back, "lat", split_axis=0, concat_axis=0, tiled=True)
    grad = run(
        synthesis_kernel,
        "synthesis",
        [pltpu.VMEM((ROWS, narrow, NLON), BF16)],
        [modes_back.transpose(1, 0, 2), by_part],
    )
    grad_swap = lax.ppermute(grad, "lat", pairs)
    field_grad = run(
        placing_kernel,
        "placing",
        [jax.ShapeDtypeStruct(field_in.shape, BF16)],
        [row_counts, at_rank, grad, grad_swap],
        [pltpu.VMEM((narrow, NLON), BF16), pltpu.SemaphoreType.DMA((2 * ROWS,))],
        pl.ANY,
    )
    return field_grad, weight_grad


def solution(mesh):
    placed = (
        P("lat", "chan", None),
        P("lat", "chan", None),
        P(("lat", "chan"), None, None),
        P(),
        P(),
    )
    return jax.shard_map(
        on_device,
        mesh=mesh,
        in_specs=placed,
        out_specs=(P("lat", "chan", None), P(("lat", "chan"), None, None)),
        check_vma=False,
    )
```

time: 291 us -> 223 us (0.77)
  the two profiles are of different devices: /device:TPU:70 before, /device:TPU:1 now
where the time goes in v3:
time: 223 us; the launch traced here: 222 us
  blocking collectives  97.9 us (44%)
  waiting for transfers between devices  61.8 us (28%)
  Pallas kernels  31.7 us (14%)
  starting transfers between devices  19.7 us (9%)
  local copies, waits for them, and re-layouts  9.93 us (4%)
    all_to_all x1, blocking collectives, on_device(): lax.all_to_all(coeffs, everyone, split_axis=0, concat_axis=0, tiled=True)  69 us
    all_to_all x1, waiting for transfers between devices, on_device(): lax.all_to_all(back, everyone, split_axis=0, concat_axis=0, tiled=True)  31.9 us
    pallas_call x8, Pallas kernels, run(): pl.pallas_call(kernel, out_shape=tuple(outs), in_specs=specs, out_specs=t...  31.7 us
    all_to_all x1, blocking collectives, on_device(): lax.all_to_all(modes_back, 'lat', split_axis=0, concat_axis=0, tiled=True)  28.9 us
    all_to_all x1, waiting for transfers between devices, on_device(): lax.all_to_all(modes, 'lat', split_axis=0, concat_axis=0, tiled=True)  24.9 us
    all_to_all x1, starting transfers between devices, on_device(): lax.all_to_all(modes, 'lat', split_axis=0, concat_axis=0, tiled=True)  10.4 us
    unnamed x26, local copies, waits for them, and re-layouts  6.22 us
    all_to_all x1, starting transfers between devices, on_device(): lax.all_to_all(back, everyone, split_axis=0, concat_axis=0, tiled=True)  5.18 us
  transfers between devices with their start and end apart: 5, of which 5 were waited for; matrix products, arithmetic and copies ran while one was open for 0% of the time, Pallas kernels for 9%

profile of v3, /device:TPU:1, one launch (start us, length us, event | category | flops | bytes accessed | tf_op | source)
XLA Modules:
  0.0 222.0 jit_solution(12039059066928185666)
XLA Ops:
  0.6 0.0 copy-start.1
  0.7 0.0 copy-start.2
  0.7 0.0 copy-start.11
  0.7 1.4 constant_dynamic-slice_fusion
  2.1 3.3 %collective-permute-start.1 = (bf16[6,96,720]{2,1,0:T(8,128)(2,1)S(1)}, bf16[6,96,720]{2,1,0:T(8,128)(2,1)S(1)}, u32[]{:S(2)}, u32[]{:S(2)}) collective-permute-start(bf16[6,96,720]{2,1,0:T(8,128)(2,1)S(1)} %constant_dynamic-slice_fusion), channel_id=1, source_target_pairs={{0,4},{4,0},{8,12},{12,8},{16,20},{20,16},{24,28},{28,24},{32,36},... | collective-permute-start | bytes 2488328 | tf_op jit(solution)/shard_map/ppermute | solution.py:358
  5.4 0.0 copy-done.1
  5.4 0.1 constant_dynamic-slice_fusion.1
  5.5 0.3 collective-permute-start
  5.8 1.7 collective-permute-done.1.cotan_in_ref
  7.4 1.3 collective-permute-done.field_in_ref
  8.7 0.0 copy-done.2
  8.7 0.0 copy-done.11
  8.7 1.3 copy-done.5
  10.0 3.8 %analysis.1 = bf16[64,2,6912]{2,1,0:T(2,128)(2,1)} custom-call(s32[64]{0:T(128)S(1)} %copy-done.11, s32[1]{0:T(128)} %bitcast.rank_ref, bf16[12,96,720]{2,1,0:T(8,128)(2,1)S(1)} %copy-done.1, bf16[12,96,720]{2,1,0:T(8,128)(2,1)S(1)} %copy-done.2, bf16[6,96,720]{2,1,0:T(8,128)(2,1)S(1)} %collective-permute-done.field_in_ref, ...), custom_call_target="tpu_custom_call" | custom-call | tf_op jit(solution)/shard_map/analysis/pallas_call | solution.py:65
  13.8 0.0 copy-start.12
  13.8 0.0 copy-start.8
  13.8 10.4 %all-to-all-start = ((bf16[64,2,6912]{2,1,0:T(2,128)(2,1)}), bf16[64,2,6912]{2,1,0:T(2,128)(2,1)}, u32[]{:S(2)}, u32[]{:S(2)}) async-start(bf16[64,2,6912]{2,1,0:T(2,128)(2,1)} %analysis.1), calls=%async_computation | async-start | bytes 3538944 | tf_op jit(solution)/shard_map/all_to_all | solution.py:369
  24.3 0.0 copy-done.12
  24.3 0.2 reshape.14
  24.5 0.1 broadcast_in_dim_reshape.4.slot_ref
  24.6 0.0 copy-done.8
  24.6 0.0 copy-done.9
  24.6 0.0 copy-done.10
  24.7 17.3 %legendre.1 = (bf16[6,512,384]{2,1,0:T(8,128)(2,1)S(1)}, bf16[6,384,512]{2,1,0:T(8,128)(2,1)S(1)}) custom-call(s32[1]{0:T(128)} %bitcast.rank_ref, f32[1,768]{1,0:T(1,128)S(1)} %copy-done.10, f32[1,768]{1,0:T(1,128)S(1)} %copy-done.9, f32[64,8,128]{2,1,0:T(8,128)S(1)} %copy-done.8, s32[512,1]{1,0:T(8,128)S(1)} %broadcast_in_dim_reshape.4.slot_ref), custom_call_target="tpu_custom_call" | custom-call | tf_op jit(solution)/shard_map/legendre/pallas_call | solution.py:65
  41.9 0.0 copy-start.3
  41.9 1.4 copy-done.3
  43.4 24.9 %all-to-all-done = bf16[64,2,6912]{2,1,0:T(2,128)(2,1)} async-done(((bf16[64,2,6912]{2,1,0:T(2,128)(2,1)}), bf16[64,2,6912]{2,1,0:T(2,128)(2,1)}, u32[]{:S(2)}, u32[]{:S(2)}) %all-to-all-start) | async-done | bytes 1769504 | tf_op jit(solution)/shard_map/all_to_all | solution.py:369
  68.2 1.6 copy.27
  69.9 1.9 forward.1
  71.8 69.0 %all_to_all.20 = bf16[256,2,2304]{2,1,0:T(2,128)(2,1)S(1)} all-to-all(bf16[256,2,2304]{2,1,0:T(2,128)(2,1)S(1)} %forward.1), channel_id=1, replica_groups=mesh['lat'=64,'chan'=4] {'chan','lat'}, dimensions={0} | all-to-all | bytes 4718592 | tf_op jit(solution)/shard_map/all_to_all | solution.py:379
  140.8 0.2 copy.23
  141.1 0.8 copy-done.7
  141.9 1.5 degree.1
  143.4 0.0 copy-start
  143.4 1.0 copy-done
  144.4 5.2 %all-to-all-start.2 = ((bf16[256,2,1152]{2,1,0:T(2,128)(2,1)}), bf16[256,2,1152]{2,1,0:T(2,128)(2,1)S(1)}, u32[]{:S(2)}, u32[]{:S(2)}) async-start(bf16[256,2,1152]{2,1,0:T(2,128)(2,1)} %copy-done), calls=%async_computation.2 | async-start | bytes 2359296 | tf_op jit(solution)/shard_map/all_to_all | solution.py:388
  149.6 2.7 %gradient.1 = f32[2,384,384]{2,1,0:T(8,128)} custom-call(bf16[2,4,64,2304]{3,2,1,0:T(8,128)(2,1)S(1)} %bitcast.11), custom_call_target="tpu_custom_call" | custom-call | tf_op jit(solution)/shard_map/gradient/pallas_call | solution.py:65
  152.4 31.9 %all-to-all-done.2.back_ref = bf16[256,2,1152]{2,1,0:T(2,128)(2,1)S(1)} async-done(((bf16[256,2,1152]{2,1,0:T(2,128)(2,1)}), bf16[256,2,1152]{2,1,0:T(2,128)(2,1)S(1)}, u32[]{:S(2)}, u32[]{:S(2)}) %all-to-all-start.2) | async-done | bytes 1179680 | tf_op jit(solution)/shard_map/all_to_all | solution.py:388
  184.3 1.7 copy-done.4
  185.9 1.1 backward.1
  187.1 0.0 copy-start.6
  187.1 28.9 %all_to_all.21 = bf16[64,2,3456]{2,1,0:T(2,128)(2,1)S(1)} all-to-all(bf16[64,2,3456]{2,1,0:T(2,128)(2,1)S(1)} %backward.1), channel_id=1, replica_groups=mesh['lat'=64,'chan'=4] {'lat'}, dimensions={0} | all-to-all | bytes 1769472 | tf_op jit(solution)/shard_map/all_to_all | solution.py:399
  216.0 0.1 copy.28
  216.1 0.0 copy-done.6
  216.1 1.4 synthesis.1.mine_ref
  217.5 0.4 collective-permute-start.2
  217.9 2.1 collective-permute-done.2.theirs_ref
  220.0 1.9 placing.1
  (6 shorter events, 0.0 us)
Async XLA Ops:
  0.6 4.8 %copy-start.1 = (bf16[12,96,720]{2,1,0:T(8,128)(2,1)S(1)}, bf16[12,96,720]{2,1,0:T(8,128)(2,1)}, u32[]{:S(2)}) copy-start(bf16[12,96,720]{2,1,0:T(8,128)(2,1)} %field_ref.1) | copy-start | bytes 4976644
  0.7 8.1 %copy-start.2 = (bf16[12,96,720]{2,1,0:T(8,128)(2,1)S(1)}, bf16[12,96,720]{2,1,0:T(8,128)(2,1)}, u32[]{:S(2)}) copy-start(bf16[12,96,720]{2,1,0:T(8,128)(2,1)} %cotan_ref.1) | copy-start | bytes 4976644
  0.7 8.0 %copy-start.11 = (s32[64]{0:T(128)S(1)}, s32[64]{0:T(128)}, u32[]{:S(2)}) copy-start(s32[64]{0:T(128)} %counts_ref.3) | copy-start | bytes 772
  2.1 5.4 %collective-permute-start.1 = (bf16[6,96,720]{2,1,0:T(8,128)(2,1)S(1)}, bf16[6,96,720]{2,1,0:T(8,128)(2,1)S(1)}, u32[]{:S(2)}, u32[]{:S(2)}) collective-permute-start(bf16[6,96,720]{2,1,0:T(8,128)(2,1)S(1)} %constant_dynamic-slice_fusion), channel_id=1, source_target_pairs={{0,4},{4,0},{8,12},{12,8},{16,20},{20,16},{24,28},{28,24},{32,36},... | collective-permute-start | bytes 2488328 | tf_op jit(solution)/shard_map/ppermute | solution.py:358
  5.5 3.3 %collective-permute-start = (bf16[6,96,720]{2,1,0:T(8,128)(2,1)S(1)}, bf16[6,96,720]{2,1,0:T(8,128)(2,1)S(1)}, u32[]{:S(2)}, u32[]{:S(2)}) collective-permute-start(bf16[6,96,720]{2,1,0:T(8,128)(2,1)S(1)} %constant_dynamic-slice_fusion.1), channel_id=1, source_target_pairs={{0,4},{4,0},{8,12},{12,8},{16,20},{20,16},{24,28},{28,24},{32,36},... | collective-permute-start | bytes 2488328 | tf_op jit(solution)/shard_map/ppermute | solution.py:355
  8.7 1.3 copy-start.5
  13.8 10.5 %copy-start.12 = (s32[512]{0:T(512)S(1)}, s32[512]{0:T(512)}, u32[]{:S(2)}) copy-start(s32[512]{0:T(512)} %param.14) | copy-start | bytes 6148
  13.8 10.8 %copy-start.8 = (f32[64,8,128]{2,1,0:T(8,128)S(1)}, f32[64,8,128]{2,1,0:T(8,128)}, u32[]{:S(2)}) copy-start(f32[64,8,128]{2,1,0:T(8,128)} %constant.39.clone.norm_ref) | copy-start | bytes 786436
  13.8 10.8 %copy-start.9 = (f32[1,768]{1,0:T(1,128)S(1)}, f32[1,768]{1,0:T(1,128)}, u32[]{:S(2)}) copy-start(f32[1,768]{1,0:T(1,128)} %constant.38.clone.logsine_ref) | copy-start | bytes 9220
  13.8 10.8 %copy-start.10 = (f32[1,768]{1,0:T(1,128)S(1)}, f32[1,768]{1,0:T(1,128)}, u32[]{:S(2)}) copy-start(f32[1,768]{1,0:T(1,128)} %constant.37.clone.cosine_ref) | copy-start | bytes 9220
  13.8 54.4 %all-to-all-start = ((bf16[64,2,6912]{2,1,0:T(2,128)(2,1)}), bf16[64,2,6912]{2,1,0:T(2,128)(2,1)}, u32[]{:S(2)}, u32[]{:S(2)}) async-start(bf16[64,2,6912]{2,1,0:T(2,128)(2,1)} %analysis.1), calls=%async_computation | async-start | bytes 3538944 | tf_op jit(solution)/shard_map/all_to_all | solution.py:369
  41.9 1.4 copy-start.3
  140.8 1.1 copy-start.7
  143.4 1.0 copy-start
  144.4 39.8 %all-to-all-start.2 = ((bf16[256,2,1152]{2,1,0:T(2,128)(2,1)}), bf16[256,2,1152]{2,1,0:T(2,128)(2,1)S(1)}, u32[]{:S(2)}, u32[]{:S(2)}) async-start(bf16[256,2,1152]{2,1,0:T(2,128)(2,1)} %copy-done), calls=%async_computation.2 | async-start | bytes 2359296 | tf_op jit(solution)/shard_map/all_to_all | solution.py:388
  184.3 1.7 copy-start.4
  187.1 29.0 %copy-start.6 = (bf16[768,720]{1,0:T(8,128)(2,1)S(1)}, bf16[768,720]{1,0:T(8,128)(2,1)}, u32[]{:S(2)}) copy-start(bf16[768,720]{1,0:T(8,128)(2,1)} %constant.35.clone.fourier_ref) | copy-start | bytes 3317764
  217.5 2.5 %collective-permute-start.2 = (bf16[6,96,720]{2,1,0:T(8,128)(2,1)S(1)}, bf16[6,96,720]{2,1,0:T(8,128)(2,1)S(1)}, u32[]{:S(2)}, u32[]{:S(2)}) collective-permute-start(bf16[6,96,720]{2,1,0:T(8,128)(2,1)S(1)} %synthesis.1.mine_ref), channel_id=1, source_target_pairs={{0,4},{4,0},{8,12},{12,8},{16,20},{20,16},{24,28},{28,24},{32,36},... | collective-permute-start | bytes 2488328 | tf_op jit(solution)/shard_map/ppermute | solution.py:406

commit v4 on v3

--- a/solution.py
+++ b/solution.py
@@ -54,14 +54,17 @@
     return np.cos(theta).astype(np.float32), np.log(np.sin(theta)).astype(np.float32)
 
 
-def run(kernel, name, outs, args, scratch=(), home=pltpu.VMEM):
-    vmem = pl.BlockSpec(memory_space=pltpu.VMEM)
-    scalar = pl.BlockSpec(memory_space=pltpu.SMEM)
+def run(kernel, name, outs, args, scratch=(), far=(), home=pltpu.VMEM):
     specs, operands = [], []
-    for arg in args:
-        small = arg.dtype == jnp.int32 and arg.ndim == 1
-        specs.append(scalar if small else vmem)
-        operands.append(arg if small else pltpu.with_memory_space_constraint(arg, pltpu.VMEM))
+    for at, arg in enumerate(args):
+        if arg.dtype == jnp.int32 and arg.ndim == 1:
+            specs.append(pl.BlockSpec(memory_space=pltpu.SMEM))
+        elif at in far:
+            specs.append(pl.BlockSpec(memory_space=pl.ANY))
+        else:
+            specs.append(pl.BlockSpec(memory_space=pltpu.VMEM))
+            arg = pltpu.with_memory_space_constraint(arg, pltpu.VMEM)
+        operands.append(arg)
     results = pl.pallas_call(
         kernel,
         out_shape=tuple(outs),
@@ -148,7 +151,10 @@
     return run(
         legendre_kernel,
         "legendre",
-        [pltpu.VMEM((GROUPS, slots, latitudes), BF16), pltpu.VMEM((GROUPS, latitudes, slots), BF16)],
+        [
+            pltpu.VMEM((GROUPS, slots, latitudes), BF16),
+            jax.ShapeDtypeStruct((GROUPS, latitudes, slots), BF16),
+        ],
         [
             at_rank,
             jnp.asarray(cosine),
@@ -161,12 +167,18 @@
 
 
 def analysis_kernel(
-    counts_ref, rank_ref, field_ref, cotan_ref, field_in_ref, cotan_in_ref, fourier_ref,
-    out_ref, rows_ref,
+    counts_ref, rank_ref, field_ref, cotan_ref, field_in_ref, cotan_in_ref, table_ref,
+    out_ref, rows_ref, fourier_ref, held_ref, sems,
 ):
     narrow = field_ref.shape[1]
     lat_count = out_ref.shape[0]
     width = 2 * ROWS * narrow
+    loads = []
+    block = 2 * lat_count * (GROUPS // 2)
+    for half in range(2):
+        at = pl.ds(half * block, block)
+        loads.append(pltpu.make_async_copy(table_ref.at[at], fourier_ref.at[at], sems.at[half]))
+        loads[-1].start()
     rank = rank_ref[0]
     odd = rank % 2
     first = counts_ref[rank - odd]
@@ -185,13 +197,29 @@
             def _():
                 rows_ref[at, :] = there[jnp.clip(theirs, 0, ROWS - 1)]
 
-    modes = lax.dot_general(
-        fourier_ref[...], rows_ref[...], (((1,), (1,)), ((), ())), preferred_element_type=F32
-    ).astype(BF16)
-    for j in range(GROUPS):
-        out_ref[:, :, j * width : (j + 1) * width] = modes[
-            2 * lat_count * j : 2 * lat_count * (j + 1)
-        ].reshape(lat_count, 2, width)
+    stores = []
+    for half in range(2):
+        loads[half].wait()
+        modes = lax.dot_general(
+            fourier_ref[half * block : (half + 1) * block, :],
+            rows_ref[...],
+            (((1,), (1,)), ((), ())),
+            preferred_element_type=F32,
+        ).astype(BF16)
+        for i in range(GROUPS // 2):
+            j = half * (GROUPS // 2) + i
+            held_ref[:, :, j * width : (j + 1) * width] = modes[
+                2 * lat_count * i : 2 * lat_count * (i + 1)
+            ].reshape(lat_count, 2, width)
+        lanes = pl.ds(half * (GROUPS // 2) * width, (GROUPS // 2) * width)
+        stores.append(
+            pltpu.make_async_copy(
+                held_ref.at[:, :, lanes], out_ref.at[:, :, lanes], sems.at[2 + half]
+            )
+        )
+        stores[-1].start()
+    for store in stores:
+        store.wait()
 
 
 def forward_kernel(rank_ref, modes_ref, legendre_ref, out_ref):
@@ -240,12 +268,19 @@
     )
 
 
-def degree_kernel(coeffs_ref, weights_ref, back_ref):
+def degree_kernel(coeffs_ref, stored_ref, back_ref, weights_ref, sems):
     chans, lat_count = coeffs_ref.shape[1:3]
     narrow = coeffs_ref.shape[3] // (4 * GROUPS)
+    loads = [
+        pltpu.make_async_copy(stored_ref.at[s], weights_ref.at[s], sems.at[s]) for s in range(2)
+    ]
+    for load in loads:
+        load.start()
     for s in range(2):
+        dcoeffs = side(coeffs_ref, s, 1)
+        loads[s].wait()
         back = lax.dot_general(
-            side(coeffs_ref, s, 1),
+            dcoeffs,
             weights_ref[s],
             (((1,), (1,)), ((), ())),
             preferred_element_type=F32,
@@ -270,13 +305,20 @@
         )
 
 
-def backward_kernel(back_ref, legendre_ref, out_ref):
+def backward_kernel(back_ref, stored_ref, out_ref, legendre_ref, sems):
     slots = legendre_ref.shape[2]
+    loads = [
+        pltpu.make_async_copy(stored_ref.at[j], legendre_ref.at[j], sems.at[j])
+        for j in range(GROUPS)
+    ]
+    for load in loads:
+        load.start()
     lat_count = out_ref.shape[0]
     span = back_ref.shape[2] // GROUPS
     half = ROWS // 2
     for j in range(GROUPS):
         held = back_ref[:, :, j * span : (j + 1) * span].reshape(slots, span)
+        loads[j].wait()
         modes = jnp.dot(legendre_ref[j], held, preferred_element_type=F32).astype(BF16)
         for k in range(half):
             out_ref[:, :, (j * half + k) * span : (j * half + k + 1) * span] = modes[
@@ -362,9 +404,16 @@
     modes = run(
         analysis_kernel,
         "analysis",
-        [pltpu.VMEM((lat_count, 2, GROUPS * width), BF16)],
+        [jax.ShapeDtypeStruct((lat_count, 2, GROUPS * width), BF16)],
         [row_counts, at_rank, field_in, cotangent, field_swap, cotan_swap, by_rank],
-        [pltpu.VMEM((width, NLON), BF16)],
+        [
+            pltpu.VMEM((width, NLON), BF16),
+            pltpu.VMEM(by_rank.shape, BF16),
+            pltpu.VMEM((lat_count, 2, GROUPS * width), BF16),
+            pltpu.SemaphoreType.DMA((4,)),
+        ],
+        far=(6,),
+        home=pl.ANY,
     )
     modes = lax.all_to_all(modes, "lat", split_axis=0, concat_axis=0, tiled=True)
     modes = modes.transpose(1, 0, 2)
@@ -381,8 +430,10 @@
     back = run(
         degree_kernel,
         "degree",
-        [pltpu.VMEM((devices, held, 2 * GROUPS * narrow), BF16)],
+        [jax.ShapeDtypeStruct((devices, held, 2 * GROUPS * narrow), BF16)],
         [coeffs, weights],
+        [pltpu.VMEM(weights.shape, BF16), pltpu.SemaphoreType.DMA((held,))],
+        far=(1,),
     )
     back, coeffs = lax.optimization_barrier((back, coeffs))
     back = lax.all_to_all(back, everyone, split_axis=0, concat_axis=0, tiled=True)
@@ -395,6 +446,8 @@
         "backward",
         [pltpu.VMEM((lat_count, 2, GROUPS * ROWS * narrow), BF16)],
         [back, legendre_pairs],
+        [pltpu.VMEM(legendre_pairs.shape, BF16), pltpu.SemaphoreType.DMA((GROUPS,))],
+        far=(1,),
     )
     modes_back = lax.all_to_all(modes_back, "lat", split_axis=0, concat_axis=0, tiled=True)
     grad = run(
@@ -410,7 +463,7 @@
         [jax.ShapeDtypeStruct(field_in.shape, BF16)],
         [row_counts, at_rank, grad, grad_swap],
         [pltpu.VMEM((narrow, NLON), BF16), pltpu.SemaphoreType.DMA((2 * ROWS,))],
-        pl.ANY,
+        home=pl.ANY,
     )
     return field_grad, weight_grad
 

time: 223 us -> 227 us (1.018)
  Pallas kernels: 31.7 us -> 35.9 us
    pallas_call x8, Pallas kernels: 31.7 us -> 35.9 us  [run(): pl.pallas_call(kernel, out_shape=tuple(outs), in_specs=specs, out_specs=t...]
where the time goes in v4:
time: 227 us; the launch traced here: 226 us
  blocking collectives  97.9 us (43%)
  waiting for transfers between devices  61.8 us (27%)
  Pallas kernels  35.9 us (16%)
  starting transfers between devices  19.7 us (9%)
  local copies, waits for them, and re-layouts  9.95 us (4%)
    all_to_all x1, blocking collectives, on_device(): lax.all_to_all(coeffs, everyone, split_axis=0, concat_axis=0, tiled=True)  69 us
    pallas_call x8, Pallas kernels, run(): pl.pallas_call(kernel, out_shape=tuple(outs), in_specs=specs, out_specs=t...  35.9 us
    all_to_all x1, waiting for transfers between devices, on_device(): lax.all_to_all(back, everyone, split_axis=0, concat_axis=0, tiled=True)  31.9 us
    all_to_all x1, blocking collectives, on_device(): lax.all_to_all(modes_back, 'lat', split_axis=0, concat_axis=0, tiled=True)  28.9 us
    all_to_all x1, waiting for transfers between devices, on_device(): lax.all_to_all(modes, 'lat', split_axis=0, concat_axis=0, tiled=True)  24.9 us
    all_to_all x1, starting transfers between devices, on_device(): lax.all_to_all(modes, 'lat', split_axis=0, concat_axis=0, tiled=True)  10.4 us
    unnamed x26, local copies, waits for them, and re-layouts  6.23 us
    all_to_all x1, starting transfers between devices, on_device(): lax.all_to_all(back, everyone, split_axis=0, concat_axis=0, tiled=True)  5.18 us
  transfers between devices with their start and end apart: 5, of which 5 were waited for; matrix products, arithmetic and copies ran while one was open for 0% of the time, Pallas kernels for 9%

profile of v4, /device:TPU:1, one launch (start us, length us, event | category | flops | bytes accessed | tf_op | source)
XLA Modules:
  0.0 226.3 jit_solution(3096034701360024491)
XLA Ops:
  0.6 0.0 copy-start.1
  0.7 0.0 copy-start.2
  0.7 0.0 copy-start.11
  0.7 1.4 constant_dynamic-slice_fusion
  2.1 3.3 %collective-permute-start.1 = (bf16[6,96,720]{2,1,0:T(8,128)(2,1)S(1)}, bf16[6,96,720]{2,1,0:T(8,128)(2,1)S(1)}, u32[]{:S(2)}, u32[]{:S(2)}) collective-permute-start(bf16[6,96,720]{2,1,0:T(8,128)(2,1)S(1)} %constant_dynamic-slice_fusion), channel_id=1, source_target_pairs={{0,4},{4,0},{8,12},{12,8},{16,20},{20,16},{24,28},{28,24},{32,36},... | collective-permute-start | bytes 2488328 | tf_op jit(solution)/shard_map/ppermute | solution.py:400
  5.4 0.0 copy-done.1
  5.4 0.1 constant_dynamic-slice_fusion.1
  5.5 0.3 collective-permute-start
  5.8 1.7 collective-permute-done.1.cotan_in_ref
  7.4 1.3 collective-permute-done.field_in_ref
  8.7 0.0 copy-done.2
  8.7 0.0 copy-done.11
  8.7 1.3 copy-done.5
  10.0 4.2 %analysis.1 = bf16[64,2,6912]{2,1,0:T(2,128)(2,1)} custom-call(s32[64]{0:T(128)S(1)} %copy-done.11, s32[1]{0:T(128)} %bitcast.rank_ref, bf16[12,96,720]{2,1,0:T(8,128)(2,1)S(1)} %copy-done.1, bf16[12,96,720]{2,1,0:T(8,128)(2,1)S(1)} %copy-done.2, bf16[6,96,720]{2,1,0:T(8,128)(2,1)S(1)} %collective-permute-done.field_in_ref, ...), custom_call_target="tpu_custom_call" | custom-call | tf_op jit(solution)/shard_map/analysis/pallas_call | solution.py:68
  14.2 0.0 copy-start.12
  14.2 0.0 copy-start.8
  14.2 0.0 copy-start.9
  14.2 0.0 copy-start.10
  14.2 10.4 %all-to-all-start = ((bf16[64,2,6912]{2,1,0:T(2,128)(2,1)}), bf16[64,2,6912]{2,1,0:T(2,128)(2,1)}, u32[]{:S(2)}, u32[]{:S(2)}) async-start(bf16[64,2,6912]{2,1,0:T(2,128)(2,1)} %analysis.1), calls=%async_computation | async-start | bytes 3538944 | tf_op jit(solution)/shard_map/all_to_all | solution.py:418
  24.7 0.0 copy-done.12
  24.7 0.2 reshape.14
  24.9 0.1 broadcast_in_dim_reshape.4.slot_ref
  25.0 0.0 copy-done.8
  25.0 0.0 copy-done.9
  25.1 17.3 %legendre.1 = (bf16[6,512,384]{2,1,0:T(8,128)(2,1)S(1)}, bf16[6,384,512]{2,1,0:T(8,128)(2,1)S(1)}) custom-call(s32[1]{0:T(128)} %bitcast.rank_ref, f32[1,768]{1,0:T(1,128)S(1)} %copy-done.10, f32[1,768]{1,0:T(1,128)S(1)} %copy-done.9, f32[64,8,128]{2,1,0:T(8,128)S(1)} %copy-done.8, s32[512,1]{1,0:T(8,128)S(1)} %broadcast_in_dim_reshape.4.slot_ref), custom_call_target="tpu_custom_call" | custom-call | tf_op jit(solution)/shard_map/legendre/pallas_call | solution.py:68
  42.3 1.4 copy-done.3
  43.8 24.9 %all-to-all-done = bf16[64,2,6912]{2,1,0:T(2,128)(2,1)} async-done(((bf16[64,2,6912]{2,1,0:T(2,128)(2,1)}), bf16[64,2,6912]{2,1,0:T(2,128)(2,1)}, u32[]{:S(2)}, u32[]{:S(2)}) %all-to-all-start) | async-done | bytes 1769504 | tf_op jit(solution)/shard_map/all_to_all | solution.py:418
  68.6 1.6 copy.27
  70.3 1.9 forward.1
  72.2 69.0 %all_to_all.20 = bf16[256,2,2304]{2,1,0:T(2,128)(2,1)S(1)} all-to-all(bf16[256,2,2304]{2,1,0:T(2,128)(2,1)S(1)} %forward.1), channel_id=1, replica_groups=mesh['lat'=64,'chan'=4] {'chan','lat'}, dimensions={0} | all-to-all | bytes 4718592 | tf_op jit(solution)/shard_map/all_to_all | solution.py:428
  141.2 0.2 copy.23
  141.5 0.8 copy-done.7
  142.3 2.2 degree.1
  144.5 0.0 copy-start
  144.5 1.0 copy-done
  145.5 5.2 %all-to-all-start.2 = ((bf16[256,2,1152]{2,1,0:T(2,128)(2,1)}), bf16[256,2,1152]{2,1,0:T(2,128)(2,1)S(1)}, u32[]{:S(2)}, u32[]{:S(2)}) async-start(bf16[256,2,1152]{2,1,0:T(2,128)(2,1)} %copy-done), calls=%async_computation.2 | async-start | bytes 2359296 | tf_op jit(solution)/shard_map/all_to_all | solution.py:439
  150.7 2.7 %gradient.1 = f32[2,384,384]{2,1,0:T(8,128)} custom-call(bf16[2,4,64,2304]{3,2,1,0:T(8,128)(2,1)S(1)} %bitcast.11), custom_call_target="tpu_custom_call" | custom-call | tf_op jit(solution)/shard_map/gradient/pallas_call | solution.py:68
  153.4 31.9 %all-to-all-done.2.back_ref = bf16[256,2,1152]{2,1,0:T(2,128)(2,1)S(1)} async-done(((bf16[256,2,1152]{2,1,0:T(2,128)(2,1)}), bf16[256,2,1152]{2,1,0:T(2,128)(2,1)S(1)}, u32[]{:S(2)}, u32[]{:S(2)}) %all-to-all-start.2) | async-done | bytes 1179680 | tf_op jit(solution)/shard_map/all_to_all | solution.py:439
  185.3 1.7 copy-done.4
  187.0 4.3 %backward.1 = bf16[64,2,3456]{2,1,0:T(2,128)(2,1)S(1)} custom-call(bf16[256,2,1152]{2,1,0:T(2,128)(2,1)S(1)} %all-to-all-done.2.back_ref, bf16[6,384,512]{2,1,0:T(8,128)(2,1)S(1)} %copy-done.4), custom_call_target="tpu_custom_call" | custom-call | tf_op jit(solution)/shard_map/backward/pallas_call | solution.py:68
  191.3 0.0 copy-start.6
  191.3 28.9 %all_to_all.21 = bf16[64,2,3456]{2,1,0:T(2,128)(2,1)S(1)} all-to-all(bf16[64,2,3456]{2,1,0:T(2,128)(2,1)S(1)} %backward.1), channel_id=1, replica_groups=mesh['lat'=64,'chan'=4] {'lat'}, dimensions={0} | all-to-all | bytes 1769472 | tf_op jit(solution)/shard_map/all_to_all | solution.py:452
  220.3 0.1 copy.28
  220.4 0.0 copy-done.6
  220.4 1.4 synthesis.1.mine_ref
  221.8 0.4 collective-permute-start.2
  222.2 2.1 collective-permute-done.2.theirs_ref
  224.3 1.9 placing.1
  (6 shorter events, 0.0 us)
Async XLA Ops:
  0.6 4.8 %copy-start.1 = (bf16[12,96,720]{2,1,0:T(8,128)(2,1)S(1)}, bf16[12,96,720]{2,1,0:T(8,128)(2,1)}, u32[]{:S(2)}) copy-start(bf16[12,96,720]{2,1,0:T(8,128)(2,1)} %field_ref.1) | copy-start | bytes 4976644
  0.7 8.1 %copy-start.2 = (bf16[12,96,720]{2,1,0:T(8,128)(2,1)S(1)}, bf16[12,96,720]{2,1,0:T(8,128)(2,1)}, u32[]{:S(2)}) copy-start(bf16[12,96,720]{2,1,0:T(8,128)(2,1)} %cotan_ref.1) | copy-start | bytes 4976644
  0.7 8.0 %copy-start.11 = (s32[64]{0:T(128)S(1)}, s32[64]{0:T(128)}, u32[]{:S(2)}) copy-start(s32[64]{0:T(128)} %counts_ref.3) | copy-start | bytes 772
  2.1 5.4 %collective-permute-start.1 = (bf16[6,96,720]{2,1,0:T(8,128)(2,1)S(1)}, bf16[6,96,720]{2,1,0:T(8,128)(2,1)S(1)}, u32[]{:S(2)}, u32[]{:S(2)}) collective-permute-start(bf16[6,96,720]{2,1,0:T(8,128)(2,1)S(1)} %constant_dynamic-slice_fusion), channel_id=1, source_target_pairs={{0,4},{4,0},{8,12},{12,8},{16,20},{20,16},{24,28},{28,24},{32,36},... | collective-permute-start | bytes 2488328 | tf_op jit(solution)/shard_map/ppermute | solution.py:400
  5.5 3.3 %collective-permute-start = (bf16[6,96,720]{2,1,0:T(8,128)(2,1)S(1)}, bf16[6,96,720]{2,1,0:T(8,128)(2,1)S(1)}, u32[]{:S(2)}, u32[]{:S(2)}) collective-permute-start(bf16[6,96,720]{2,1,0:T(8,128)(2,1)S(1)} %constant_dynamic-slice_fusion.1), channel_id=1, source_target_pairs={{0,4},{4,0},{8,12},{12,8},{16,20},{20,16},{24,28},{28,24},{32,36},... | collective-permute-start | bytes 2488328 | tf_op jit(solution)/shard_map/ppermute | solution.py:397
  8.7 1.3 copy-start.5
  14.2 10.5 %copy-start.12 = (s32[512]{0:T(512)S(1)}, s32[512]{0:T(512)}, u32[]{:S(2)}) copy-start(s32[512]{0:T(512)} %param.14) | copy-start | bytes 6148
  14.2 10.8 %copy-start.8 = (f32[64,8,128]{2,1,0:T(8,128)S(1)}, f32[64,8,128]{2,1,0:T(8,128)}, u32[]{:S(2)}) copy-start(f32[64,8,128]{2,1,0:T(8,128)} %constant.39.clone.norm_ref) | copy-start | bytes 786436
  14.2 10.8 %copy-start.9 = (f32[1,768]{1,0:T(1,128)S(1)}, f32[1,768]{1,0:T(1,128)}, u32[]{:S(2)}) copy-start(f32[1,768]{1,0:T(1,128)} %constant.38.clone.logsine_ref) | copy-start | bytes 9220
  14.2 10.8 %copy-start.10 = (f32[1,768]{1,0:T(1,128)S(1)}, f32[1,768]{1,0:T(1,128)}, u32[]{:S(2)}) copy-start(f32[1,768]{1,0:T(1,128)} %constant.37.clone.cosine_ref) | copy-start | bytes 9220
  14.2 54.4 %all-to-all-start = ((bf16[64,2,6912]{2,1,0:T(2,128)(2,1)}), bf16[64,2,6912]{2,1,0:T(2,128)(2,1)}, u32[]{:S(2)}, u32[]{:S(2)}) async-start(bf16[64,2,6912]{2,1,0:T(2,128)(2,1)} %analysis.1), calls=%async_computation | async-start | bytes 3538944 | tf_op jit(solution)/shard_map/all_to_all | solution.py:418
  42.3 1.4 copy-start.3
  141.2 1.1 copy-start.7
  144.5 1.0 copy-start
  145.5 39.8 %all-to-all-start.2 = ((bf16[256,2,1152]{2,1,0:T(2,128)(2,1)}), bf16[256,2,1152]{2,1,0:T(2,128)(2,1)S(1)}, u32[]{:S(2)}, u32[]{:S(2)}) async-start(bf16[256,2,1152]{2,1,0:T(2,128)(2,1)} %copy-done), calls=%async_computation.2 | async-start | bytes 2359296 | tf_op jit(solution)/shard_map/all_to_all | solution.py:439
  185.3 1.7 copy-start.4
  191.3 29.0 %copy-start.6 = (bf16[768,720]{1,0:T(8,128)(2,1)S(1)}, bf16[768,720]{1,0:T(8,128)(2,1)}, u32[]{:S(2)}) copy-start(bf16[768,720]{1,0:T(8,128)(2,1)} %constant.35.clone.fourier_ref) | copy-start | bytes 3317764
  221.8 2.5 %collective-permute-start.2 = (bf16[6,96,720]{2,1,0:T(8,128)(2,1)S(1)}, bf16[6,96,720]{2,1,0:T(8,128)(2,1)S(1)}, u32[]{:S(2)}, u32[]{:S(2)}) collective-permute-start(bf16[6,96,720]{2,1,0:T(8,128)(2,1)S(1)} %synthesis.1.mine_ref), channel_id=1, source_target_pairs={{0,4},{4,0},{8,12},{12,8},{16,20},{20,16},{24,28},{28,24},{32,36},... | collective-permute-start | bytes 2488328 | tf_op jit(solution)/shard_map/ppermute | solution.py:459

commit v5 on v4

--- a/solution.py
+++ b/solution.py
@@ -60,7 +60,8 @@
         if arg.dtype == jnp.int32 and arg.ndim == 1:
             specs.append(pl.BlockSpec(memory_space=pltpu.SMEM))
         elif at in far:
-            specs.append(pl.BlockSpec(memory_space=pl.ANY))
+            specs.append(pl.BlockSpec(memory_space=pltpu.HBM))
+            arg = pltpu.with_memory_space_constraint(arg, pltpu.HBM)
         else:
             specs.append(pl.BlockSpec(memory_space=pltpu.VMEM))
             arg = pltpu.with_memory_space_constraint(arg, pltpu.VMEM)
@@ -153,7 +154,7 @@
         "legendre",
         [
             pltpu.VMEM((GROUPS, slots, latitudes), BF16),
-            jax.ShapeDtypeStruct((GROUPS, latitudes, slots), BF16),
+            pltpu.HBM((GROUPS, latitudes, slots), BF16),
         ],
         [
             at_rank,
@@ -404,7 +405,7 @@
     modes = run(
         analysis_kernel,
         "analysis",
-        [jax.ShapeDtypeStruct((lat_count, 2, GROUPS * width), BF16)],
+        [pltpu.HBM((lat_count, 2, GROUPS * width), BF16)],
         [row_counts, at_rank, field_in, cotangent, field_swap, cotan_swap, by_rank],
         [
             pltpu.VMEM((width, NLON), BF16),
@@ -413,7 +414,7 @@
             pltpu.SemaphoreType.DMA((4,)),
         ],
         far=(6,),
-        home=pl.ANY,
+        home=pltpu.HBM,
     )
     modes = lax.all_to_all(modes, "lat", split_axis=0, concat_axis=0, tiled=True)
     modes = modes.transpose(1, 0, 2)
@@ -430,7 +431,7 @@
     back = run(
         degree_kernel,
         "degree",
-        [jax.ShapeDtypeStruct((devices, held, 2 * GROUPS * narrow), BF16)],
+        [pltpu.HBM((devices, held, 2 * GROUPS * narrow), BF16)],
         [coeffs, weights],
         [pltpu.VMEM(weights.shape, BF16), pltpu.SemaphoreType.DMA((held,))],
         far=(1,),
@@ -463,7 +464,7 @@
         [jax.ShapeDtypeStruct(field_in.shape, BF16)],
         [row_counts, at_rank, grad, grad_swap],
         [pltpu.VMEM((narrow, NLON), BF16), pltpu.SemaphoreType.DMA((2 * ROWS,))],
-        home=pl.ANY,
+        home=pltpu.HBM,
     )
     return field_grad, weight_grad
 

time: 227 us -> 224 us (0.987)
  local copies, waits for them, and re-layouts: 9.95 us -> 3.76 us
  Pallas kernels: 35.9 us -> 39.7 us
    unnamed x26 -> x16, local copies, waits for them, and re-layouts: 6.23 us -> 0.05 us
    pallas_call x8, Pallas kernels: 35.9 us -> 39.7 us  [run(): pl.pallas_call(kernel, out_shape=tuple(outs), in_specs=specs, out_specs=t...]
  transfers between devices with their start and end apart: 5 -> 5, of which waited for: 5 -> 5; matrix products, arithmetic and copies ran while one was open for 0% -> 0% of each run, Pallas kernels for 9% -> 10%
where the time goes in v5:
time: 224 us
  blocking collectives  97.9 us (44%)
  waiting for transfers between devices  61.8 us (28%)
  Pallas kernels  39.7 us (18%)
  starting transfers between devices  19.7 us (9%)
  local copies, waits for them, and re-layouts  3.76 us (2%)
    all_to_all x1, blocking collectives, on_device(): lax.all_to_all(coeffs, everyone, split_axis=0, concat_axis=0, tiled=True)  69 us
    pallas_call x8, Pallas kernels, run(): pl.pallas_call(kernel, out_shape=tuple(outs), in_specs=specs, out_specs=t...  39.7 us
    all_to_all x1, waiting for transfers between devices, on_device(): lax.all_to_all(back, everyone, split_axis=0, concat_axis=0, tiled=True)  31.9 us
    all_to_all x1, blocking collectives, on_device(): lax.all_to_all(modes_back, 'lat', split_axis=0, concat_axis=0, tiled=True)  28.9 us
    all_to_all x1, waiting for transfers between devices, on_device(): lax.all_to_all(modes, 'lat', split_axis=0, concat_axis=0, tiled=True)  24.9 us
    all_to_all x1, starting transfers between devices, on_device(): lax.all_to_all(modes, 'lat', split_axis=0, concat_axis=0, tiled=True)  10.4 us
    all_to_all x1, starting transfers between devices, on_device(): lax.all_to_all(back, everyone, split_axis=0, concat_axis=0, tiled=True)  5.19 us
  transfers between devices with their start and end apart: 5, of which 5 were waited for; matrix products, arithmetic and copies ran while one was open for 0% of the time, Pallas kernels for 10%

profile of v5, /device:TPU:1, one launch (start us, length us, event | category | flops | bytes accessed | tf_op | source)
XLA Modules:
  0.0 223.8 jit_solution(7814298822661554748)
XLA Ops:
  0.6 0.0 copy-start
  0.7 0.0 copy-start.1
  0.7 0.0 copy-start.6
  0.7 1.4 constant_dynamic-slice_fusion
  2.1 3.3 %collective-permute-start.1 = (bf16[6,96,720]{2,1,0:T(8,128)(2,1)S(1)}, bf16[6,96,720]{2,1,0:T(8,128)(2,1)S(1)}, u32[]{:S(2)}, u32[]{:S(2)}) collective-permute-start(bf16[6,96,720]{2,1,0:T(8,128)(2,1)S(1)} %constant_dynamic-slice_fusion), channel_id=1, source_target_pairs={{0,4},{4,0},{8,12},{12,8},{16,20},{20,16},{24,28},{28,24},{32,36},... | collective-permute-start | bytes 2488328 | tf_op jit(solution)/shard_map/ppermute | solution.py:401
  5.4 0.0 copy-done
  5.4 0.1 constant_dynamic-slice_fusion.1
  5.5 0.3 collective-permute-start
  5.8 1.7 collective-permute-done.1.cotan_in_ref
  7.4 1.3 collective-permute-done.field_in_ref
  8.7 0.0 copy-done.1
  8.7 0.0 copy-done.6
  8.7 4.8 %analysis.1 = bf16[64,2,6912]{2,1,0:T(2,128)(2,1)} custom-call(s32[64]{0:T(128)S(1)} %copy-done.6, s32[1]{0:T(128)} %bitcast.rank_ref, bf16[12,96,720]{2,1,0:T(8,128)(2,1)S(1)} %copy-done, bf16[12,96,720]{2,1,0:T(8,128)(2,1)S(1)} %copy-done.1, bf16[6,96,720]{2,1,0:T(8,128)(2,1)S(1)} %collective-permute-done.field_in_ref, ...), custom_call_target="tpu_custom_call" | custom-call | tf_op jit(solution)/shard_map/analysis/pallas_call | solution.py:69
  13.5 0.0 copy-start.7
  13.5 0.0 copy-start.3
  13.5 0.0 copy-start.4
  13.6 0.0 copy-start.5
  13.6 10.4 %all-to-all-start = ((bf16[64,2,6912]{2,1,0:T(2,128)(2,1)}), bf16[64,2,6912]{2,1,0:T(2,128)(2,1)}, u32[]{:S(2)}, u32[]{:S(2)}) async-start(bf16[64,2,6912]{2,1,0:T(2,128)(2,1)} %analysis.1), calls=%async_computation | async-start | bytes 3538944 | tf_op jit(solution)/shard_map/all_to_all | solution.py:419
  24.0 0.0 copy-done.7
  24.0 0.2 reshape.14
  24.2 0.1 broadcast_in_dim_reshape.4.slot_ref
  24.4 0.0 copy-done.3
  24.4 0.0 copy-done.4
  24.4 0.0 copy-done.5
  24.4 18.7 %legendre.1 = (bf16[6,512,384]{2,1,0:T(8,128)(2,1)S(1)}, bf16[6,384,512]{2,1,0:T(8,128)(2,1)}) custom-call(s32[1]{0:T(128)} %bitcast.rank_ref, f32[1,768]{1,0:T(1,128)S(1)} %copy-done.5, f32[1,768]{1,0:T(1,128)S(1)} %copy-done.4, f32[64,8,128]{2,1,0:T(8,128)S(1)} %copy-done.3, s32[512,1]{1,0:T(8,128)S(1)} %broadcast_in_dim_reshape.4.slot_ref), custom_call_target="tpu_custom_call" | custom-call | tf_op jit(solution)/shard_map/legendre/pallas_call | solution.py:69
  43.1 24.9 %all-to-all-done = bf16[64,2,6912]{2,1,0:T(2,128)(2,1)} async-done(((bf16[64,2,6912]{2,1,0:T(2,128)(2,1)}), bf16[64,2,6912]{2,1,0:T(2,128)(2,1)}, u32[]{:S(2)}, u32[]{:S(2)}) %all-to-all-start) | async-done | bytes 1769504 | tf_op jit(solution)/shard_map/all_to_all | solution.py:419
  67.9 1.6 copy.27
  69.6 2.0 forward.1
  71.6 69.0 %all_to_all.20 = bf16[256,2,2304]{2,1,0:T(2,128)(2,1)S(1)} all-to-all(bf16[256,2,2304]{2,1,0:T(2,128)(2,1)S(1)} %forward.1), channel_id=1, replica_groups=mesh['lat'=64,'chan'=4] {'chan','lat'}, dimensions={0} | all-to-all | bytes 4718592 | tf_op jit(solution)/shard_map/all_to_all | solution.py:429
  140.6 0.2 copy.23
  140.9 3.9 %degree.1 = bf16[256,2,1152]{2,1,0:T(2,128)(2,1)} custom-call(bf16[2,4,64,2304]{3,2,1,0:T(8,128)(2,1)S(1)} %bitcast.10, bf16[2,384,384]{2,1,0:T(8,128)(2,1)} %stored_ref.1), custom_call_target="tpu_custom_call" | custom-call | tf_op jit(solution)/shard_map/degree/pallas_call | solution.py:69
  144.7 5.2 %all-to-all-start.2 = ((bf16[256,2,1152]{2,1,0:T(2,128)(2,1)}), bf16[256,2,1152]{2,1,0:T(2,128)(2,1)S(1)}, u32[]{:S(2)}, u32[]{:S(2)}) async-start(bf16[256,2,1152]{2,1,0:T(2,128)(2,1)} %degree.1), calls=%async_computation.2 | async-start | bytes 2359296 | tf_op jit(solution)/shard_map/all_to_all | solution.py:440
  149.9 2.8 %gradient.1 = f32[2,384,384]{2,1,0:T(8,128)} custom-call(bf16[2,4,64,2304]{3,2,1,0:T(8,128)(2,1)S(1)} %bitcast.11), custom_call_target="tpu_custom_call" | custom-call | tf_op jit(solution)/shard_map/gradient/pallas_call | solution.py:69
  152.7 31.9 %all-to-all-done.2.back_ref = bf16[256,2,1152]{2,1,0:T(2,128)(2,1)S(1)} async-done(((bf16[256,2,1152]{2,1,0:T(2,128)(2,1)}), bf16[256,2,1152]{2,1,0:T(2,128)(2,1)S(1)}, u32[]{:S(2)}, u32[]{:S(2)}) %all-to-all-start.2) | async-done | bytes 1179680 | tf_op jit(solution)/shard_map/all_to_all | solution.py:440
  184.6 4.3 %backward.1 = bf16[64,2,3456]{2,1,0:T(2,128)(2,1)S(1)} custom-call(bf16[256,2,1152]{2,1,0:T(2,128)(2,1)S(1)} %all-to-all-done.2.back_ref, bf16[6,384,512]{2,1,0:T(8,128)(2,1)} %get-tuple-element.12.stored_ref), custom_call_target="tpu_custom_call" | custom-call | tf_op jit(solution)/shard_map/backward/pallas_call | solution.py:69
  188.8 0.0 copy-start.2
  188.9 28.9 %all_to_all.21 = bf16[64,2,3456]{2,1,0:T(2,128)(2,1)S(1)} all-to-all(bf16[64,2,3456]{2,1,0:T(2,128)(2,1)S(1)} %backward.1), channel_id=1, replica_groups=mesh['lat'=64,'chan'=4] {'lat'}, dimensions={0} | all-to-all | bytes 1769472 | tf_op jit(solution)/shard_map/all_to_all | solution.py:453
  217.8 0.1 copy.28
  217.9 0.0 copy-done.2
  217.9 1.4 synthesis.1.mine_ref
  219.3 0.4 collective-permute-start.2
  219.7 2.1 collective-permute-done.2.theirs_ref
  221.8 1.9 placing.1
  (1 shorter events, 0.0 us)
Async XLA Ops:
  0.6 4.8 %copy-start = (bf16[12,96,720]{2,1,0:T(8,128)(2,1)S(1)}, bf16[12,96,720]{2,1,0:T(8,128)(2,1)}, u32[]{:S(2)}) copy-start(bf16[12,96,720]{2,1,0:T(8,128)(2,1)} %field_ref.1) | copy-start | bytes 4976644
  0.7 8.1 %copy-start.1 = (bf16[12,96,720]{2,1,0:T(8,128)(2,1)S(1)}, bf16[12,96,720]{2,1,0:T(8,128)(2,1)}, u32[]{:S(2)}) copy-start(bf16[12,96,720]{2,1,0:T(8,128)(2,1)} %cotan_ref.1) | copy-start | bytes 4976644
  0.7 8.0 %copy-start.6 = (s32[64]{0:T(128)S(1)}, s32[64]{0:T(128)}, u32[]{:S(2)}) copy-start(s32[64]{0:T(128)} %counts_ref.3) | copy-start | bytes 772
  2.1 5.4 %collective-permute-start.1 = (bf16[6,96,720]{2,1,0:T(8,128)(2,1)S(1)}, bf16[6,96,720]{2,1,0:T(8,128)(2,1)S(1)}, u32[]{:S(2)}, u32[]{:S(2)}) collective-permute-start(bf16[6,96,720]{2,1,0:T(8,128)(2,1)S(1)} %constant_dynamic-slice_fusion), channel_id=1, source_target_pairs={{0,4},{4,0},{8,12},{12,8},{16,20},{20,16},{24,28},{28,24},{32,36},... | collective-permute-start | bytes 2488328 | tf_op jit(solution)/shard_map/ppermute | solution.py:401
  5.5 3.3 %collective-permute-start = (bf16[6,96,720]{2,1,0:T(8,128)(2,1)S(1)}, bf16[6,96,720]{2,1,0:T(8,128)(2,1)S(1)}, u32[]{:S(2)}, u32[]{:S(2)}) collective-permute-start(bf16[6,96,720]{2,1,0:T(8,128)(2,1)S(1)} %constant_dynamic-slice_fusion.1), channel_id=1, source_target_pairs={{0,4},{4,0},{8,12},{12,8},{16,20},{20,16},{24,28},{28,24},{32,36},... | collective-permute-start | bytes 2488328 | tf_op jit(solution)/shard_map/ppermute | solution.py:398
  13.5 10.5 %copy-start.7 = (s32[512]{0:T(512)S(1)}, s32[512]{0:T(512)}, u32[]{:S(2)}) copy-start(s32[512]{0:T(512)} %param.14) | copy-start | bytes 6148
  13.5 10.8 %copy-start.3 = (f32[64,8,128]{2,1,0:T(8,128)S(1)}, f32[64,8,128]{2,1,0:T(8,128)}, u32[]{:S(2)}) copy-start(f32[64,8,128]{2,1,0:T(8,128)} %constant.39.clone.norm_ref) | copy-start | bytes 786436
  13.5 10.8 %copy-start.4 = (f32[1,768]{1,0:T(1,128)S(1)}, f32[1,768]{1,0:T(1,128)}, u32[]{:S(2)}) copy-start(f32[1,768]{1,0:T(1,128)} %constant.38.clone.logsine_ref) | copy-start | bytes 9220
  13.6 10.8 %copy-start.5 = (f32[1,768]{1,0:T(1,128)S(1)}, f32[1,768]{1,0:T(1,128)}, u32[]{:S(2)}) copy-start(f32[1,768]{1,0:T(1,128)} %constant.37.clone.cosine_ref) | copy-start | bytes 9220
  13.6 54.4 %all-to-all-start = ((bf16[64,2,6912]{2,1,0:T(2,128)(2,1)}), bf16[64,2,6912]{2,1,0:T(2,128)(2,1)}, u32[]{:S(2)}, u32[]{:S(2)}) async-start(bf16[64,2,6912]{2,1,0:T(2,128)(2,1)} %analysis.1), calls=%async_computation | async-start | bytes 3538944 | tf_op jit(solution)/shard_map/all_to_all | solution.py:419
  144.7 39.8 %all-to-all-start.2 = ((bf16[256,2,1152]{2,1,0:T(2,128)(2,1)}), bf16[256,2,1152]{2,1,0:T(2,128)(2,1)S(1)}, u32[]{:S(2)}, u32[]{:S(2)}) async-start(bf16[256,2,1152]{2,1,0:T(2,128)(2,1)} %degree.1), calls=%async_computation.2 | async-start | bytes 2359296 | tf_op jit(solution)/shard_map/all_to_all | solution.py:440
  188.8 29.0 %copy-start.2 = (bf16[768,720]{1,0:T(8,128)(2,1)S(1)}, bf16[768,720]{1,0:T(8,128)(2,1)}, u32[]{:S(2)}) copy-start(bf16[768,720]{1,0:T(8,128)(2,1)} %constant.35.clone.fourier_ref) | copy-start | bytes 3317764
  219.3 2.5 %collective-permute-start.2 = (bf16[6,96,720]{2,1,0:T(8,128)(2,1)S(1)}, bf16[6,96,720]{2,1,0:T(8,128)(2,1)S(1)}, u32[]{:S(2)}, u32[]{:S(2)}) collective-permute-start(bf16[6,96,720]{2,1,0:T(8,128)(2,1)S(1)} %synthesis.1.mine_ref), channel_id=1, source_target_pairs={{0,4},{4,0},{8,12},{12,8},{16,20},{20,16},{24,28},{28,24},{32,36},... | collective-permute-start | bytes 2488328 | tf_op jit(solution)/shard_map/ppermute | solution.py:460

commit v6 on v3

--- a/solution.py
+++ b/solution.py
@@ -14,7 +14,10 @@
 M = 360
 LPAD = 384
 ROWS = 6
-GROUPS = 6
+FULL = 5
+UNITS = 2
+BLOCKS = 3
+GROUPS = FULL + UNITS
 RESCALE = 2.0**40
 RESCALE_LOG = 40.0 * math.log(2.0)
 BF16 = jnp.bfloat16
@@ -22,28 +25,73 @@
 VMEM_BYTES = 30 * 1024 * 1024
 
 
-def fourier_rows(lat_count):
-    orders = np.arange(GROUPS * lat_count)
+def block_rows(units):
+    lat_count = units[0].shape[0]
+    last = M - FULL * lat_count
+    parts = []
+    for at in range(0, BLOCKS * last, last):
+        ends = [(max(at, u * lat_count), min(at + last, (u + 1) * lat_count)) for u in range(UNITS)]
+        pieces = [
+            units[u][lo - u * lat_count : hi - u * lat_count]
+            for u, (lo, hi) in enumerate(ends)
+            if lo < hi
+        ]
+        parts.append(pieces[0] if len(pieces) == 1 else jnp.concatenate(pieces, axis=0))
+    return parts
+
+
+def unit_rows(blocks, lat_count, height=1):
+    last = M - FULL * lat_count
+    units = []
+    for u in range(UNITS):
+        pieces = []
+        for b in range(BLOCKS):
+            lo, hi = max(b * last, u * lat_count), min((b + 1) * last, (u + 1) * lat_count)
+            if lo < hi:
+                pieces.append(blocks[b][(lo - b * last) * height : (hi - b * last) * height])
+        dead = (u + 1) * lat_count - max(BLOCKS * last, u * lat_count)
+        if dead > 0:
+            pieces.append(jnp.zeros((dead * height, blocks[0].shape[1]), blocks[0].dtype))
+        units.append(jnp.concatenate(pieces, axis=0))
+    return units
+
+
+def fourier_rows(orders):
     turns = orders[:, None] * np.arange(NLON)[None, :] % NLON
     angles = turns * (2.0 * math.pi / NLON)
-    live = (orders < M)[:, None] / math.sqrt(NLON)
-    parts = np.stack([np.cos(angles) * live, -np.sin(angles) * live], axis=0)
-    parts = parts.reshape(2, GROUPS, lat_count, NLON).transpose(1, 0, 2, 3)
+    parts = np.stack([np.cos(angles), -np.sin(angles)], axis=1) / math.sqrt(NLON)
     return parts.astype(ml_dtypes.bfloat16)
 
 
-def order_norms(lat_count):
-    orders = np.arange(8)[None, :] * lat_count + np.arange(lat_count)[:, None]
+def fourier_tables(lat_count):
+    first = fourier_rows(np.arange(FULL * lat_count)).reshape(FULL, lat_count, 2, NLON)
+    last = fourier_rows(np.arange(FULL * lat_count, M))
+    by_rank = np.concatenate([first.reshape(-1, NLON), last.reshape(-1, NLON)])
+    by_part = np.concatenate(
+        [first.transpose(0, 2, 1, 3).reshape(-1, NLON), last.transpose(1, 0, 2).reshape(-1, NLON)]
+    )
+    return by_rank, by_part
+
+
+def order_tables(lat_count):
+    rank = np.arange(lat_count)[:, None]
+    unit = np.arange(UNITS)[None, :] * lat_count + rank
+    last = M - FULL * lat_count
+    units = np.where(unit < BLOCKS * last, FULL * lat_count + unit % last, 10**6)
+    firsts = np.arange(FULL)[None, :] * lat_count + rank
+    dead = np.full((lat_count, 8 - GROUPS), 10**6)
+    orders = np.concatenate([firsts, units, dead], axis=1)
     logs = [
         0.5 * math.log((2.0 * m + 1.0) / (4.0 * math.pi))
         + 0.5 * math.lgamma(2.0 * m + 1.0)
         - m * math.log(2.0)
         - math.lgamma(m + 1.0)
-        for m in orders.reshape(-1).tolist()
+        for m in np.minimum(orders, M).reshape(-1).tolist()
     ]
     latitudes = ROWS * lat_count
-    total = np.array(logs).reshape(orders.shape) + 0.5 * math.log(2.0 * math.pi**2 / latitudes)
-    return np.broadcast_to(total[:, :, None], total.shape + (128,)).astype(np.float32)
+    norms = np.array(logs).reshape(orders.shape) + 0.5 * math.log(2.0 * math.pi**2 / latitudes)
+    shape = orders.shape + (128,)
+    return tuple(np.broadcast_to(t[:, :, None], shape).astype(np.float32) for t in (orders, norms))
 
 
 def latitude_rows(lat_count):
@@ -75,14 +123,13 @@
 
 
 def legendre_kernel(
-    rank_ref, cosine_ref, logsine_ref, norm_ref, slot_ref, rows_out_ref, pairs_out_ref, rows_ref
+    rank_ref, cosine_ref, logsine_ref, order_ref, norm_ref, slot_ref,
+    rows_out_ref, pairs_out_ref, rows_ref,
 ):
     rank = rank_ref[0]
-    lat_count = norm_ref.shape[0]
     latitudes = rows_out_ref.shape[2]
     shape = (8, 128)
-    groups = lax.broadcasted_iota(jnp.int32, shape, 0)
-    order = (rank + groups * lat_count).astype(F32)
+    order = order_ref[rank]
     square = order * order
     tiles = cosine_ref.shape[1] // 128
     cosines, scales = [], []
@@ -145,6 +192,7 @@
     slots = slot_rows.shape[0]
     latitudes = ROWS * lat_count
     cosine, logsine = latitude_rows(lat_count)
+    orders, norms = order_tables(lat_count)
     return run(
         legendre_kernel,
         "legendre",
@@ -153,7 +201,8 @@
             at_rank,
             jnp.asarray(cosine),
             jnp.asarray(logsine),
-            jnp.asarray(order_norms(lat_count)),
+            jnp.asarray(orders),
+            jnp.asarray(norms),
             slot_rows[:, None],
         ],
         [pltpu.VMEM((LPAD, 8, 2 * latitudes), F32)],
@@ -185,27 +234,46 @@
             def _():
                 rows_ref[at, :] = there[jnp.clip(theirs, 0, ROWS - 1)]
 
+    contract = (((1,), (1,)), ((), ()))
+    full = 2 * lat_count * FULL
     modes = lax.dot_general(
-        fourier_ref[...], rows_ref[...], (((1,), (1,)), ((), ())), preferred_element_type=F32
+        fourier_ref[:full, :], rows_ref[...], contract, preferred_element_type=F32
     ).astype(BF16)
-    for j in range(GROUPS):
+    for j in range(FULL):
         out_ref[:, :, j * width : (j + 1) * width] = modes[
             2 * lat_count * j : 2 * lat_count * (j + 1)
         ].reshape(lat_count, 2, width)
+    third = narrow // BLOCKS
+    blocks = []
+    for b in range(BLOCKS):
+        rows = jnp.concatenate(
+            [
+                rows_ref[i * narrow + b * third : i * narrow + (b + 1) * third, :]
+                for i in range(2 * ROWS)
+            ],
+            axis=0,
+        )
+        blocks.append(
+            lax.dot_general(
+                fourier_ref[full:, :], rows, contract, preferred_element_type=F32
+            ).astype(BF16)
+        )
+    for u, unit in enumerate(unit_rows(blocks, lat_count, 2)):
+        at = FULL * width + u * (width // BLOCKS)
+        out_ref[:, :, at : at + width // BLOCKS] = unit.reshape(lat_count, 2, width // BLOCKS)
 
 
 def forward_kernel(rank_ref, modes_ref, legendre_ref, out_ref):
-    width = modes_ref.shape[2] // (GROUPS * ROWS)
     owners = out_ref.shape[0]
     slots = legendre_ref.shape[1]
-    lane = lax.broadcasted_iota(jnp.int32, (slots, 2 * width), 1)
-    cotangent = lane // (width // 2) % 2 == 1
+    read = write = 0
     for j in range(GROUPS):
+        width = modes_ref.shape[2] // (ROWS * (FULL * BLOCKS + UNITS)) * (BLOCKS if j < FULL else 1)
         slab = jnp.concatenate(
             [
                 jnp.concatenate(
                     [
-                        modes_ref[p, :, (j * ROWS + k) * width : (j * ROWS + k + 1) * width]
+                        modes_ref[p, :, read + k * width : read + (k + 1) * width]
                         for p in range(2)
                     ],
                     axis=1,
@@ -215,34 +283,51 @@
             axis=0,
         )
         coeffs = jnp.dot(legendre_ref[j], slab, preferred_element_type=F32)
+        lane = lax.broadcasted_iota(jnp.int32, (slots, 2 * width), 1)
+        cotangent = lane // (width // 2) % 2 == 1
         doubled = jnp.where(rank_ref[0] + j == 0, 1.0, 2.0)
         coeffs = jnp.where(cotangent, coeffs * doubled, coeffs)
-        out_ref[:, :, 2 * j * width : 2 * (j + 1) * width] = coeffs.astype(BF16).reshape(
+        out_ref[:, :, write : write + 2 * width] = coeffs.astype(BF16).reshape(
             owners, 2, 2 * width
         )
+        read += ROWS * width
+        write += 2 * width
 
 
 def side(coeffs_ref, s, w):
     chans = coeffs_ref.shape[1]
-    narrow = coeffs_ref.shape[3] // (4 * GROUPS)
-    return jnp.concatenate(
-        [
-            jnp.concatenate(
+    third = coeffs_ref.shape[3] // (4 * (FULL * BLOCKS + UNITS))
+    narrow = BLOCKS * third
+    rows = [
+        jnp.concatenate(
+            [
+                coeffs_ref[s, y, :, (2 * jp + w) * narrow : (2 * jp + w + 1) * narrow]
+                for y in range(chans)
+            ],
+            axis=1,
+        )
+        for jp in range(2 * FULL)
+    ]
+    for p in range(2):
+        at = 4 * FULL * narrow + (2 * p + w) * third
+        pieces = []
+        for y in range(chans):
+            pieces += block_rows(
                 [
-                    coeffs_ref[s, y, :, (2 * jp + w) * narrow : (2 * jp + w + 1) * narrow]
-                    for y in range(chans)
-                ],
-                axis=1,
+                    coeffs_ref[s, y, :, at + u * 4 * third : at + u * 4 * third + third]
+                    for u in range(UNITS)
+                ]
             )
-            for jp in range(2 * GROUPS)
-        ],
-        axis=0,
-    )
+        rows.append(jnp.concatenate(pieces, axis=1))
+    return jnp.concatenate(rows, axis=0)
 
 
 def degree_kernel(coeffs_ref, weights_ref, back_ref):
     chans, lat_count = coeffs_ref.shape[1:3]
-    narrow = coeffs_ref.shape[3] // (4 * GROUPS)
+    third = coeffs_ref.shape[3] // (4 * (FULL * BLOCKS + UNITS))
+    narrow = BLOCKS * third
+    full = 2 * FULL * lat_count
+    last = M - FULL * lat_count
     for s in range(2):
         back = lax.dot_general(
             side(coeffs_ref, s, 1),
@@ -251,13 +336,22 @@
             preferred_element_type=F32,
         ).astype(BF16)
         for y in range(chans):
-            back_ref[y * lat_count : (y + 1) * lat_count, s, :] = jnp.concatenate(
-                [
-                    back[jp * lat_count : (jp + 1) * lat_count, y * narrow : (y + 1) * narrow]
-                    for jp in range(2 * GROUPS)
-                ],
-                axis=1,
-            )
+            lanes = slice(y * narrow, (y + 1) * narrow)
+            pieces = [back[jp * lat_count : (jp + 1) * lat_count, lanes] for jp in range(2 * FULL)]
+            units = []
+            for p in range(2):
+                rows = slice(full + p * last, full + (p + 1) * last)
+                units.append(
+                    unit_rows(
+                        [
+                            back[rows, y * narrow + b * third : y * narrow + (b + 1) * third]
+                            for b in range(BLOCKS)
+                        ],
+                        lat_count,
+                    )
+                )
+            pieces += [units[p][u] for u in range(UNITS) for p in range(2)]
+            back_ref[y * lat_count : (y + 1) * lat_count, s, :] = jnp.concatenate(pieces, axis=1)
 
 
 def gradient_kernel(coeffs_ref, grad_ref):
@@ -273,37 +367,47 @@
 def backward_kernel(back_ref, legendre_ref, out_ref):
     slots = legendre_ref.shape[2]
     lat_count = out_ref.shape[0]
-    span = back_ref.shape[2] // GROUPS
+    third = back_ref.shape[2] // (2 * (FULL * BLOCKS + UNITS))
     half = ROWS // 2
+    read = write = 0
     for j in range(GROUPS):
-        held = back_ref[:, :, j * span : (j + 1) * span].reshape(slots, span)
+        span = 2 * third * (BLOCKS if j < FULL else 1)
+        held = back_ref[:, :, read : read + span].reshape(slots, span)
         modes = jnp.dot(legendre_ref[j], held, preferred_element_type=F32).astype(BF16)
         for k in range(half):
-            out_ref[:, :, (j * half + k) * span : (j * half + k + 1) * span] = modes[
+            out_ref[:, :, write + k * span : write + (k + 1) * span] = modes[
                 2 * lat_count * k : 2 * lat_count * (k + 1)
             ].reshape(lat_count, 2, span)
+        read += span
+        write += half * span
 
 
 def synthesis_kernel(modes_ref, fourier_ref, out_ref):
     narrow = out_ref.shape[1]
+    third = narrow // BLOCKS
     half = ROWS // 2
-    modes = jnp.concatenate(
-        [
-            jnp.concatenate(
-                [
-                    modes_ref[k % 2, :, at : at + narrow]
-                    for k in range(ROWS)
-                    for at in [((j * half + k // 2) * 2 + p) * narrow]
-                ],
-                axis=1,
-            )
-            for j in range(GROUPS)
-            for p in range(2)
-        ],
-        axis=0,
-    )
+
+    def piece(k, p, j):
+        width = narrow if j < FULL else third
+        start = (j if j < FULL else FULL) * half * 2 * narrow + max(j - FULL, 0) * half * 2 * third
+        at = start + (2 * (k // 2) + p) * width
+        return modes_ref[k % 2, :, at : at + width]
+
+    rows = [
+        jnp.concatenate([piece(k, p, j) for k in range(ROWS)], axis=1)
+        for j in range(FULL)
+        for p in range(2)
+    ]
+    for p in range(2):
+        blocks = []
+        for k in range(ROWS):
+            blocks += block_rows([piece(k, p, FULL + u) for u in range(UNITS)])
+        rows.append(jnp.concatenate(blocks, axis=1))
     grad = lax.dot_general(
-        modes, fourier_ref[...], (((0,), (0,)), ((), ())), preferred_element_type=F32
+        jnp.concatenate(rows, axis=0),
+        fourier_ref[...],
+        (((0,), (0,)), ((), ())),
+        preferred_element_type=F32,
     ).astype(BF16)
     for k in range(ROWS):
         out_ref[k] = grad[k * narrow : (k + 1) * narrow, :]
@@ -347,9 +451,9 @@
     pairs = [(i, i ^ 1) for i in range(lat_count)]
     odd = rank % 2
     at_rank = jnp.reshape(rank, (1,)).astype(jnp.int32)
-    table = fourier_rows(lat_count)
-    by_part = jnp.asarray(table.reshape(-1, NLON))
-    by_rank = jnp.asarray(table.transpose(0, 2, 1, 3).reshape(-1, NLON))
+    by_rank, by_part = (jnp.asarray(table) for table in fourier_tables(lat_count))
+    pieces = FULL * BLOCKS + UNITS
+    third = narrow // BLOCKS
     everyone = ("chan", "lat")
 
     field_swap = lax.ppermute(
@@ -362,7 +466,7 @@
     modes = run(
         analysis_kernel,
         "analysis",
-        [pltpu.VMEM((lat_count, 2, GROUPS * width), BF16)],
+        [pltpu.VMEM((lat_count, 2, pieces * width // BLOCKS), BF16)],
         [row_counts, at_rank, field_in, cotangent, field_swap, cotan_swap, by_rank],
         [pltpu.VMEM((width, NLON), BF16)],
     )
@@ -373,15 +477,15 @@
     coeffs = run(
         forward_kernel,
         "forward",
-        [pltpu.VMEM((devices, held, 4 * GROUPS * narrow), BF16)],
+        [pltpu.VMEM((devices, held, 4 * pieces * third), BF16)],
         [at_rank, modes, legendre],
     )
     coeffs = lax.all_to_all(coeffs, everyone, split_axis=0, concat_axis=0, tiled=True)
-    coeffs = coeffs.transpose(1, 0, 2).reshape(held, chan_count, lat_count, 4 * GROUPS * narrow)
+    coeffs = coeffs.transpose(1, 0, 2).reshape(held, chan_count, lat_count, 4 * pieces * third)
     back = run(
         degree_kernel,
         "degree",
-        [pltpu.VMEM((devices, held, 2 * GROUPS * narrow), BF16)],
+        [pltpu.VMEM((devices, held, 2 * pieces * third), BF16)],
         [coeffs, weights],
     )
     back, coeffs = lax.optimization_barrier((back, coeffs))
@@ -393,7 +497,7 @@
     modes_back = run(
         backward_kernel,
         "backward",
-        [pltpu.VMEM((lat_count, 2, GROUPS * ROWS * narrow), BF16)],
+        [pltpu.VMEM((lat_count, 2, ROWS * pieces * third), BF16)],
         [back, legendre_pairs],
     )
     modes_back = lax.all_to_all(modes_back, "lat", split_axis=0, concat_axis=0, tiled=True)

time: 223 us -> 217 us (0.973)
  waiting for transfers between devices: 61.8 us -> 57.9 us
  blocking collectives: 97.9 us -> 94.4 us
    all_to_all x1, waiting for transfers between devices: 24.9 us -> 21.1 us  [on_device(): lax.all_to_all(modes, 'lat', split_axis=0, concat_axis=0, tiled=True)]
    all_to_all x1, blocking collectives: 69 us -> 66.2 us  [on_device(): lax.all_to_all(coeffs, everyone, split_axis=0, concat_axis=0, tiled=True)]
    unnamed x26 -> x28, local copies, waits for them, and re-layouts: 6.22 us -> 6.46 us
  transfers between devices with their start and end apart: 5 -> 5, of which waited for: 5 -> 5; matrix products, arithmetic and copies ran while one was open for 0% -> 0% of each run, Pallas kernels for 9% -> 10%
where the time goes in v6:
time: 217 us
  blocking collectives  94.4 us (44%)
  waiting for transfers between devices  57.9 us (27%)
  Pallas kernels  33.8 us (16%)
  starting transfers between devices  19.7 us (9%)
  local copies, waits for them, and re-layouts  10.1 us (5%)
    all_to_all x1, blocking collectives, on_device(): lax.all_to_all(coeffs, everyone, split_axis=0, concat_axis=0, tiled=True)  66.2 us
    pallas_call x8, Pallas kernels, run(): pl.pallas_call(kernel, out_shape=tuple(outs), in_specs=specs, out_specs=t...  33.8 us
    all_to_all x1, waiting for transfers between devices, on_device(): lax.all_to_all(back, everyone, split_axis=0, concat_axis=0, tiled=True)  31.9 us
    all_to_all x1, blocking collectives, on_device(): lax.all_to_all(modes_back, 'lat', split_axis=0, concat_axis=0, tiled=True)  28.2 us
    all_to_all x1, waiting for transfers between devices, on_device(): lax.all_to_all(modes, 'lat', split_axis=0, concat_axis=0, tiled=True)  21.1 us
    all_to_all x1, starting transfers between devices, on_device(): lax.all_to_all(modes, 'lat', split_axis=0, concat_axis=0, tiled=True)  10.4 us
    unnamed x28, local copies, waits for them, and re-layouts  6.46 us
    all_to_all x1, starting transfers between devices, on_device(): lax.all_to_all(back, everyone, split_axis=0, concat_axis=0, tiled=True)  5.18 us
  transfers between devices with their start and end apart: 5, of which 5 were waited for; matrix products, arithmetic and copies ran while one was open for 0% of the time, Pallas kernels for 10%

profile of v6, /device:TPU:1, one launch (start us, length us, event | category | flops | bytes accessed | tf_op | source)
XLA Modules:
  0.0 217.0 jit_solution(10282175405753811705)
XLA Ops:
  0.6 0.0 copy-start.1
  0.7 0.0 copy-start.2
  0.7 0.0 copy-start.12
  0.7 1.4 constant_dynamic-slice_fusion
  2.1 3.3 %collective-permute-start.1 = (bf16[6,96,720]{2,1,0:T(8,128)(2,1)S(1)}, bf16[6,96,720]{2,1,0:T(8,128)(2,1)S(1)}, u32[]{:S(2)}, u32[]{:S(2)}) collective-permute-start(bf16[6,96,720]{2,1,0:T(8,128)(2,1)S(1)} %constant_dynamic-slice_fusion), channel_id=1, source_target_pairs={{0,4},{4,0},{8,12},{12,8},{16,20},{20,16},{24,28},{28,24},{32,36},... | collective-permute-start | bytes 2488328 | tf_op jit(solution)/shard_map/ppermute | solution.py:462
  5.4 0.0 copy-done.1
  5.4 0.1 constant_dynamic-slice_fusion.1
  5.5 0.3 collective-permute-start
  5.8 1.7 collective-permute-done.1.cotan_in_ref
  7.4 1.3 collective-permute-done.field_in_ref
  8.7 0.0 copy-done.2
  8.7 0.0 copy-done.12
  8.7 1.2 copy-done.5
  10.0 3.9 %analysis.1 = bf16[64,2,6528]{2,1,0:T(2,128)(2,1)} custom-call(s32[64]{0:T(128)S(1)} %copy-done.12, s32[1]{0:T(128)} %bitcast.rank_ref, bf16[12,96,720]{2,1,0:T(8,128)(2,1)S(1)} %copy-done.1, bf16[12,96,720]{2,1,0:T(8,128)(2,1)S(1)} %copy-done.2, bf16[6,96,720]{2,1,0:T(8,128)(2,1)S(1)} %collective-permute-done.field_in_ref, ...), custom_call_target="tpu_custom_call" | custom-call | tf_op jit(solution)/shard_map/analysis/pallas_call | solution.py:113
  13.9 0.0 copy-start.11
  13.9 10.4 %all-to-all-start = ((bf16[64,2,6528]{2,1,0:T(2,128)(2,1)}), bf16[64,2,6528]{2,1,0:T(2,128)(2,1)}, u32[]{:S(2)}, u32[]{:S(2)}) async-start(bf16[64,2,6528]{2,1,0:T(2,128)(2,1)} %analysis.1), calls=%async_computation | async-start | bytes 3342336 | tf_op jit(solution)/shard_map/all_to_all | solution.py:473
  24.3 0.0 copy-done.13
  24.3 0.2 reshape.14
  24.5 0.1 broadcast_in_dim_reshape.4.slot_ref
  24.6 0.0 copy-done.8
  24.7 0.0 copy-done.9
  24.7 0.0 copy-done.10
  24.7 0.0 copy-done.11
  24.7 18.8 %legendre.1 = (bf16[7,512,384]{2,1,0:T(8,128)(2,1)S(1)}, bf16[7,384,512]{2,1,0:T(8,128)(2,1)S(1)}) custom-call(s32[1]{0:T(128)} %bitcast.rank_ref, f32[1,768]{1,0:T(1,128)S(1)} %copy-done.11, f32[1,768]{1,0:T(1,128)S(1)} %copy-done.10, f32[64,8,128]{2,1,0:T(8,128)S(1)} %copy-done.9, f32[64,8,128]{2,1,0:T(8,128)S(1)} %copy-done.8, ...), custom_call_target="tpu_custom_call" | custom-call | tf_op jit(solution)/shard_map/legendre/pallas_call | solution.py:113
  43.5 0.0 copy-start.3
  43.5 1.5 copy-done.3
  45.1 21.1 %all-to-all-done = bf16[64,2,6528]{2,1,0:T(2,128)(2,1)} async-done(((bf16[64,2,6528]{2,1,0:T(2,128)(2,1)}), bf16[64,2,6528]{2,1,0:T(2,128)(2,1)}, u32[]{:S(2)}, u32[]{:S(2)}) %all-to-all-start) | async-done | bytes 1671200 | tf_op jit(solution)/shard_map/all_to_all | solution.py:473
  66.1 1.6 copy.28
  67.8 2.1 forward.1
  69.9 66.2 %all_to_all.20 = bf16[256,2,2176]{2,1,0:T(2,128)(2,1)S(1)} all-to-all(bf16[256,2,2176]{2,1,0:T(2,128)(2,1)S(1)} %forward.1), channel_id=1, replica_groups=mesh['lat'=64,'chan'=4] {'chan','lat'}, dimensions={0} | all-to-all | bytes 4456448 | tf_op jit(solution)/shard_map/all_to_all | solution.py:483
  136.1 0.2 copy.24
  136.3 0.8 copy-done.7
  137.1 1.6 degree.1
  138.8 0.0 copy-start
  138.8 1.0 copy-done
  139.8 5.2 %all-to-all-start.2 = ((bf16[256,2,1088]{2,1,0:T(2,128)(2,1)}), bf16[256,2,1088]{2,1,0:T(2,128)(2,1)S(1)}, u32[]{:S(2)}, u32[]{:S(2)}) async-start(bf16[256,2,1088]{2,1,0:T(2,128)(2,1)} %copy-done), calls=%async_computation.2 | async-start | bytes 2359296 | tf_op jit(solution)/shard_map/all_to_all | solution.py:492
  145.0 2.8 %gradient.1 = f32[2,384,384]{2,1,0:T(8,128)} custom-call(bf16[2,4,64,2176]{3,2,1,0:T(8,128)(2,1)S(1)} %bitcast.11), custom_call_target="tpu_custom_call" | custom-call | tf_op jit(solution)/shard_map/gradient/pallas_call | solution.py:113
  147.8 31.9 %all-to-all-done.2.back_ref = bf16[256,2,1088]{2,1,0:T(2,128)(2,1)S(1)} async-done(((bf16[256,2,1088]{2,1,0:T(2,128)(2,1)}), bf16[256,2,1088]{2,1,0:T(2,128)(2,1)S(1)}, u32[]{:S(2)}, u32[]{:S(2)}) %all-to-all-start.2) | async-done | bytes 1114144 | tf_op jit(solution)/shard_map/all_to_all | solution.py:492
  179.6 1.8 copy-done.4
  181.4 1.3 backward.1
  182.7 0.0 copy-start.6
  182.7 28.2 %all_to_all.21 = bf16[64,2,3264]{2,1,0:T(2,128)(2,1)S(1)} all-to-all(bf16[64,2,3264]{2,1,0:T(2,128)(2,1)S(1)} %backward.1), channel_id=1, replica_groups=mesh['lat'=64,'chan'=4] {'lat'}, dimensions={0} | all-to-all | bytes 1671168 | tf_op jit(solution)/shard_map/all_to_all | solution.py:503
  210.9 0.1 copy.29
  211.0 0.0 copy-done.6
  211.0 1.5 synthesis.1.mine_ref
  212.5 0.5 collective-permute-start.2
  212.9 2.1 collective-permute-done.2.theirs_ref
  215.0 1.9 placing.1
  (8 shorter events, 0.0 us)
Async XLA Ops:
  0.6 4.8 %copy-start.1 = (bf16[12,96,720]{2,1,0:T(8,128)(2,1)S(1)}, bf16[12,96,720]{2,1,0:T(8,128)(2,1)}, u32[]{:S(2)}) copy-start(bf16[12,96,720]{2,1,0:T(8,128)(2,1)} %field_ref.1) | copy-start | bytes 4976644
  0.7 8.1 %copy-start.2 = (bf16[12,96,720]{2,1,0:T(8,128)(2,1)S(1)}, bf16[12,96,720]{2,1,0:T(8,128)(2,1)}, u32[]{:S(2)}) copy-start(bf16[12,96,720]{2,1,0:T(8,128)(2,1)} %cotan_ref.1) | copy-start | bytes 4976644
  0.7 8.0 %copy-start.12 = (s32[64]{0:T(128)S(1)}, s32[64]{0:T(128)}, u32[]{:S(2)}) copy-start(s32[64]{0:T(128)} %counts_ref.3) | copy-start | bytes 772
  2.1 5.4 %collective-permute-start.1 = (bf16[6,96,720]{2,1,0:T(8,128)(2,1)S(1)}, bf16[6,96,720]{2,1,0:T(8,128)(2,1)S(1)}, u32[]{:S(2)}, u32[]{:S(2)}) collective-permute-start(bf16[6,96,720]{2,1,0:T(8,128)(2,1)S(1)} %constant_dynamic-slice_fusion), channel_id=1, source_target_pairs={{0,4},{4,0},{8,12},{12,8},{16,20},{20,16},{24,28},{28,24},{32,36},... | collective-permute-start | bytes 2488328 | tf_op jit(solution)/shard_map/ppermute | solution.py:462
  5.5 3.3 %collective-permute-start = (bf16[6,96,720]{2,1,0:T(8,128)(2,1)S(1)}, bf16[6,96,720]{2,1,0:T(8,128)(2,1)S(1)}, u32[]{:S(2)}, u32[]{:S(2)}) collective-permute-start(bf16[6,96,720]{2,1,0:T(8,128)(2,1)S(1)} %constant_dynamic-slice_fusion.1), channel_id=1, source_target_pairs={{0,4},{4,0},{8,12},{12,8},{16,20},{20,16},{24,28},{28,24},{32,36},... | collective-permute-start | bytes 2488328 | tf_op jit(solution)/shard_map/ppermute | solution.py:459
  8.7 1.2 copy-start.5
  13.8 10.5 %copy-start.13 = (s32[512]{0:T(512)S(1)}, s32[512]{0:T(512)}, u32[]{:S(2)}) copy-start(s32[512]{0:T(512)} %param.15) | copy-start | bytes 6148
  13.8 10.8 %copy-start.8 = (f32[64,8,128]{2,1,0:T(8,128)S(1)}, f32[64,8,128]{2,1,0:T(8,128)}, u32[]{:S(2)}) copy-start(f32[64,8,128]{2,1,0:T(8,128)} %constant.42.clone.norm_ref) | copy-start | bytes 786436
  13.9 10.8 %copy-start.9 = (f32[64,8,128]{2,1,0:T(8,128)S(1)}, f32[64,8,128]{2,1,0:T(8,128)}, u32[]{:S(2)}) copy-start(f32[64,8,128]{2,1,0:T(8,128)} %constant.41.clone.order_ref) | copy-start | bytes 786436
  13.9 10.8 %copy-start.10 = (f32[1,768]{1,0:T(1,128)S(1)}, f32[1,768]{1,0:T(1,128)}, u32[]{:S(2)}) copy-start(f32[1,768]{1,0:T(1,128)} %constant.40.clone.logsine_ref) | copy-start | bytes 9220
  13.9 10.8 %copy-start.11 = (f32[1,768]{1,0:T(1,128)S(1)}, f32[1,768]{1,0:T(1,128)}, u32[]{:S(2)}) copy-start(f32[1,768]{1,0:T(1,128)} %constant.39.clone.cosine_ref) | copy-start | bytes 9220
  13.9 52.3 %all-to-all-start = ((bf16[64,2,6528]{2,1,0:T(2,128)(2,1)}), bf16[64,2,6528]{2,1,0:T(2,128)(2,1)}, u32[]{:S(2)}, u32[]{:S(2)}) async-start(bf16[64,2,6528]{2,1,0:T(2,128)(2,1)} %analysis.1), calls=%async_computation | async-start | bytes 3342336 | tf_op jit(solution)/shard_map/all_to_all | solution.py:473
  43.5 1.6 copy-start.3
  136.1 1.1 copy-start.7
  138.8 1.0 copy-start
  139.8 39.8 %all-to-all-start.2 = ((bf16[256,2,1088]{2,1,0:T(2,128)(2,1)}), bf16[256,2,1088]{2,1,0:T(2,128)(2,1)S(1)}, u32[]{:S(2)}, u32[]{:S(2)}) async-start(bf16[256,2,1088]{2,1,0:T(2,128)(2,1)} %copy-done), calls=%async_computation.2 | async-start | bytes 2359296 | tf_op jit(solution)/shard_map/all_to_all | solution.py:492
  179.6 1.8 copy-start.4
  182.7 28.3 %copy-start.6 = (bf16[720,720]{1,0:T(8,128)(2,1)S(1)}, bf16[720,720]{1,0:T(8,128)(2,1)}, u32[]{:S(2)}) copy-start(bf16[720,720]{1,0:T(8,128)(2,1)} %constant.38.clone.fourier_ref) | copy-start | bytes 3110404
  212.5 2.5 %collective-permute-start.2 = (bf16[6,96,720]{2,1,0:T(8,128)(2,1)S(1)}, bf16[6,96,720]{2,1,0:T(8,128)(2,1)S(1)}, u32[]{:S(2)}, u32[]{:S(2)}) collective-permute-start(bf16[6,96,720]{2,1,0:T(8,128)(2,1)S(1)} %synthesis.1.mine_ref), channel_id=1, source_target_pairs={{0,4},{4,0},{8,12},{12,8},{16,20},{20,16},{24,28},{28,24},{32,36},... | collective-permute-start | bytes 2488328 | tf_op jit(solution)/shard_map/ppermute | solution.py:510

commit v7 on v6

--- a/solution.py
+++ b/solution.py
@@ -102,14 +102,16 @@
     return np.cos(theta).astype(np.float32), np.log(np.sin(theta)).astype(np.float32)
 
 
-def run(kernel, name, outs, args, scratch=(), home=pltpu.VMEM):
-    vmem = pl.BlockSpec(memory_space=pltpu.VMEM)
-    scalar = pl.BlockSpec(memory_space=pltpu.SMEM)
+def run(kernel, name, outs, args, scratch=(), home=pltpu.VMEM, far=()):
     specs, operands = [], []
-    for arg in args:
-        small = arg.dtype == jnp.int32 and arg.ndim == 1
-        specs.append(scalar if small else vmem)
-        operands.append(arg if small else pltpu.with_memory_space_constraint(arg, pltpu.VMEM))
+    for at, arg in enumerate(args):
+        if arg.dtype == jnp.int32 and arg.ndim == 1:
+            space = pltpu.SMEM
+        else:
+            space = pltpu.HBM if at in far else pltpu.VMEM
+            arg = pltpu.with_memory_space_constraint(arg, space)
+        specs.append(pl.BlockSpec(memory_space=space))
+        operands.append(arg)
     results = pl.pallas_call(
         kernel,
         out_shape=tuple(outs),
@@ -120,6 +122,23 @@
         name=name,
     )(*operands)
     return results if len(outs) > 1 else results[0]
+
+
+def loading_kernel(stored_ref, out_ref, sem):
+    copy = pltpu.make_async_copy(stored_ref, out_ref, sem)
+    copy.start()
+    copy.wait()
+
+
+def loaded(array, name):
+    return run(
+        loading_kernel,
+        name,
+        [pltpu.VMEM(array.shape, array.dtype)],
+        [array],
+        [pltpu.SemaphoreType.DMA],
+        far=(0,),
+    )
 
 
 def legendre_kernel(
@@ -211,7 +230,7 @@
 
 def analysis_kernel(
     counts_ref, rank_ref, field_ref, cotan_ref, field_in_ref, cotan_in_ref, fourier_ref,
-    out_ref, rows_ref,
+    out_ref, rows_ref, held_ref, sems,
 ):
     narrow = field_ref.shape[1]
     lat_count = out_ref.shape[0]
@@ -236,13 +255,31 @@
 
     contract = (((1,), (1,)), ((), ()))
     full = 2 * lat_count * FULL
-    modes = lax.dot_general(
-        fourier_ref[:full, :], rows_ref[...], contract, preferred_element_type=F32
-    ).astype(BF16)
-    for j in range(FULL):
-        out_ref[:, :, j * width : (j + 1) * width] = modes[
-            2 * lat_count * j : 2 * lat_count * (j + 1)
-        ].reshape(lat_count, 2, width)
+    stores = []
+
+    def send(lo, hi):
+        lanes = pl.ds(lo, hi - lo)
+        store = pltpu.make_async_copy(
+            held_ref.at[:, :, lanes], out_ref.at[:, :, lanes], sems.at[len(stores)]
+        )
+        store.start()
+        stores.append(store)
+
+    step = 2
+    for j0 in range(0, FULL, step):
+        j1 = min(j0 + step, FULL)
+        modes = lax.dot_general(
+            fourier_ref[2 * lat_count * j0 : 2 * lat_count * j1, :],
+            rows_ref[...],
+            contract,
+            preferred_element_type=F32,
+        ).astype(BF16)
+        for j in range(j0, j1):
+            held_ref[:, :, j * width : (j + 1) * width] = modes[
+                2 * lat_count * (j - j0) : 2 * lat_count * (j - j0 + 1)
+            ].reshape(lat_count, 2, width)
+        if j1 < FULL:
+            send(j0 * width, j1 * width)
     third = narrow // BLOCKS
     blocks = []
     for b in range(BLOCKS):
@@ -260,10 +297,15 @@
         )
     for u, unit in enumerate(unit_rows(blocks, lat_count, 2)):
         at = FULL * width + u * (width // BLOCKS)
-        out_ref[:, :, at : at + width // BLOCKS] = unit.reshape(lat_count, 2, width // BLOCKS)
-
-
-def forward_kernel(rank_ref, modes_ref, legendre_ref, out_ref):
+        held_ref[:, :, at : at + width // BLOCKS] = unit.reshape(lat_count, 2, width // BLOCKS)
+    send((FULL - 1) // step * step * width, out_ref.shape[2])
+    for store in stores:
+        store.wait()
+
+
+def forward_kernel(rank_ref, modes_ref, legendre_ref, stored_ref, out_ref, weights_ref, sem):
+    load = pltpu.make_async_copy(stored_ref, weights_ref, sem)
+    load.start()
     owners = out_ref.shape[0]
     slots = legendre_ref.shape[1]
     read = write = 0
@@ -292,6 +334,7 @@
         )
         read += ROWS * width
         write += 2 * width
+    load.wait()
 
 
 def side(coeffs_ref, s, w):
@@ -456,29 +499,39 @@
     third = narrow // BLOCKS
     everyone = ("chan", "lat")
 
-    field_swap = lax.ppermute(
-        lax.dynamic_slice_in_dim(field_in, (1 - odd) * ROWS, ROWS), "lat", pairs
-    )
-    cotan_swap = lax.ppermute(
-        lax.dynamic_slice_in_dim(cotangent, (1 - odd) * ROWS, ROWS), "lat", pairs
-    )
+    field_send = lax.dynamic_slice_in_dim(field_in, (1 - odd) * ROWS, ROWS)
+    cotan_send = lax.dynamic_slice_in_dim(cotangent, (1 - odd) * ROWS, ROWS)
+    field_send, by_rank = lax.optimization_barrier((field_send, by_rank))
+    field_swap = lax.ppermute(field_send, "lat", pairs)
+    cotan_swap = lax.ppermute(cotan_send, "lat", pairs)
+    by_rank = loaded(by_rank, "fourier")
     width = 2 * ROWS * narrow
     modes = run(
         analysis_kernel,
         "analysis",
-        [pltpu.VMEM((lat_count, 2, pieces * width // BLOCKS), BF16)],
+        [pltpu.HBM((lat_count, 2, pieces * width // BLOCKS), BF16)],
         [row_counts, at_rank, field_in, cotangent, field_swap, cotan_swap, by_rank],
-        [pltpu.VMEM((width, NLON), BF16)],
+        [
+            pltpu.VMEM((width, NLON), BF16),
+            pltpu.VMEM((lat_count, 2, pieces * width // BLOCKS), BF16),
+            pltpu.SemaphoreType.DMA((GROUPS,)),
+        ],
+        home=pltpu.HBM,
     )
     modes = lax.all_to_all(modes, "lat", split_axis=0, concat_axis=0, tiled=True)
     modes = modes.transpose(1, 0, 2)
     slot_rows = slot_degree.reshape(lat_count, chan_count, held).transpose(1, 0, 2).reshape(-1)
     legendre, legendre_pairs = legendre_slots(at_rank, lat_count, slot_rows)
-    coeffs = run(
+    coeffs, weights = run(
         forward_kernel,
         "forward",
-        [pltpu.VMEM((devices, held, 4 * pieces * third), BF16)],
-        [at_rank, modes, legendre],
+        [
+            pltpu.VMEM((devices, held, 4 * pieces * third), BF16),
+            pltpu.VMEM(weights.shape, BF16),
+        ],
+        [at_rank, modes, legendre, weights],
+        [pltpu.SemaphoreType.DMA],
+        far=(3,),
     )
     coeffs = lax.all_to_all(coeffs, everyone, split_axis=0, concat_axis=0, tiled=True)
     coeffs = coeffs.transpose(1, 0, 2).reshape(held, chan_count, lat_count, 4 * pieces * third)
@@ -488,12 +541,7 @@
         [pltpu.VMEM((devices, held, 2 * pieces * third), BF16)],
         [coeffs, weights],
     )
-    back, coeffs = lax.optimization_barrier((back, coeffs))
     back = lax.all_to_all(back, everyone, split_axis=0, concat_axis=0, tiled=True)
-    weight_grad = run(
-        gradient_kernel, "gradient", [jax.ShapeDtypeStruct((held, full, full), F32)], [coeffs]
-    )
-    back, weight_grad = lax.optimization_barrier((back, weight_grad))
     modes_back = run(
         backward_kernel,
         "backward",
@@ -507,7 +555,12 @@
         [pltpu.VMEM((ROWS, narrow, NLON), BF16)],
         [modes_back.transpose(1, 0, 2), by_part],
     )
+    grad, coeffs = lax.optimization_barrier((grad, coeffs))
     grad_swap = lax.ppermute(grad, "lat", pairs)
+    weight_grad = run(
+        gradient_kernel, "gradient", [jax.ShapeDtypeStruct((held, full, full), F32)], [coeffs]
+    )
+    grad_swap, weight_grad = lax.optimization_barrier((grad_swap, weight_grad))
     field_grad = run(
         placing_kernel,
         "placing",

time: 217 us -> 214 us (0.986)
  blocking collectives: 94.4 us -> 134 us
  waiting for transfers between devices: 57.9 us -> 22.8 us
  starting transfers between devices: 19.7 us -> 14.6 us
  local copies, waits for them, and re-layouts: 10.1 us -> 5.9 us
    all_to_all x0 -> x1, blocking collectives: none -> 39.7 us  [on_device(): lax.all_to_all(back, everyone, split_axis=0, concat_axis=0, tiled=True)]
    all_to_all x1 -> x0, waiting for transfers between devices: 31.9 us -> none  [on_device(): lax.all_to_all(back, everyone, split_axis=0, concat_axis=0, tiled=True)]
    all_to_all x1 -> x0, starting transfers between devices: 5.18 us -> none  [on_device(): lax.all_to_all(back, everyone, split_axis=0, concat_axis=0, tiled=True)]
    unnamed x28 -> x22, local copies, waits for them, and re-layouts: 6.46 us -> 2.11 us
    pallas_call x8 -> x9, Pallas kernels: 33.8 us -> 35.1 us  [run(): pl.pallas_call(kernel, out_shape=tuple(outs), in_specs=specs, out_specs=t...]
  transfers between devices with their start and end apart: 5 -> 4, of which waited for: 5 -> 3; matrix products, arithmetic and copies ran while one was open for 0% -> 0% of each run, Pallas kernels for 10% -> 11%
where the time goes in v7:
time: 214 us; the launch traced here: 213 us
  blocking collectives  134 us (63%)
  Pallas kernels  35.1 us (16%)
  waiting for transfers between devices  22.8 us (11%)
  starting transfers between devices  14.6 us (7%)
  local copies, waits for them, and re-layouts  5.9 us (3%)
    all_to_all x1, blocking collectives, on_device(): lax.all_to_all(coeffs, everyone, split_axis=0, concat_axis=0, tiled=True)  66.2 us
    all_to_all x1, blocking collectives, on_device(): lax.all_to_all(back, everyone, split_axis=0, concat_axis=0, tiled=True)  39.7 us
    pallas_call x9, Pallas kernels, run(): pl.pallas_call(kernel, out_shape=tuple(outs), in_specs=specs, out_specs=t...  35.1 us
    all_to_all x1, blocking collectives, on_device(): lax.all_to_all(modes_back, 'lat', split_axis=0, concat_axis=0, tiled=True)  28.2 us
    all_to_all x1, waiting for transfers between devices, on_device(): lax.all_to_all(modes, 'lat', split_axis=0, concat_axis=0, tiled=True)  21.1 us
    all_to_all x1, starting transfers between devices, on_device(): lax.all_to_all(modes, 'lat', split_axis=0, concat_axis=0, tiled=True)  10.4 us
  transfers between devices with their start and end apart: 4, of which 3 were waited for; matrix products, arithmetic and copies ran while one was open for 0% of the time, Pallas kernels for 11%

profile of v7, /device:TPU:1, one launch (start us, length us, event | category | flops | bytes accessed | tf_op | source)
XLA Modules:
  0.0 213.4 jit_solution(4781001336618067734)
XLA Ops:
  0.6 0.0 copy-start
  0.7 1.4 constant_dynamic-slice_fusion
  2.0 0.0 copy-start.1
  2.0 0.0 copy-start.9
  2.0 3.3 %collective-permute-start.1 = (bf16[6,96,720]{2,1,0:T(8,128)(2,1)S(1)}, bf16[6,96,720]{2,1,0:T(8,128)(2,1)S(1)}, u32[]{:S(2)}, u32[]{:S(2)}) collective-permute-start(bf16[6,96,720]{2,1,0:T(8,128)(2,1)S(1)} %constant_dynamic-slice_fusion), channel_id=1, source_target_pairs={{0,4},{4,0},{8,12},{12,8},{16,20},{20,16},{24,28},{28,24},{32,36},... | collective-permute-start | bytes 2488328 | tf_op jit(solution)/shard_map/ppermute | solution.py:506
  5.4 0.0 copy-done
  5.4 0.1 constant_dynamic-slice_fusion.1
  5.4 0.3 collective-permute-start
  5.8 1.3 fourier.1.fourier_ref
  7.0 0.4 collective-permute-done.1.cotan_in_ref
  7.4 1.3 collective-permute-done.field_in_ref
  8.7 0.0 copy-done.1
  8.7 0.0 copy-done.9
  8.7 3.8 %analysis.1 = bf16[64,2,6528]{2,1,0:T(2,128)(2,1)} custom-call(s32[64]{0:T(128)S(1)} %copy-done.9, s32[1]{0:T(128)} %bitcast.rank_ref, bf16[12,96,720]{2,1,0:T(8,128)(2,1)S(1)} %copy-done, bf16[12,96,720]{2,1,0:T(8,128)(2,1)S(1)} %copy-done.1, bf16[6,96,720]{2,1,0:T(8,128)(2,1)S(1)} %collective-permute-done.field_in_ref, ...), custom_call_target="tpu_custom_call" | custom-call | tf_op jit(solution)/shard_map/analysis/pallas_call | solution.py:115
  12.5 0.0 copy-start.10
  12.6 0.0 copy-start.5
  12.6 0.0 copy-start.6
  12.6 0.0 copy-start.7
  12.6 0.0 copy-start.8
  12.6 10.4 %all-to-all-start = ((bf16[64,2,6528]{2,1,0:T(2,128)(2,1)}), bf16[64,2,6528]{2,1,0:T(2,128)(2,1)}, u32[]{:S(2)}, u32[]{:S(2)}) async-start(bf16[64,2,6528]{2,1,0:T(2,128)(2,1)} %analysis.1), calls=%async_computation | async-start | bytes 3342336 | tf_op jit(solution)/shard_map/all_to_all | solution.py:521
  23.1 0.0 copy-done.10
  23.1 0.2 reshape.14
  23.3 0.1 broadcast_in_dim_reshape.4.slot_ref
  23.4 0.0 copy-done.5
  23.4 0.0 copy-done.6
  23.4 0.0 copy-done.7
  23.4 0.0 copy-done.8
  23.4 18.8 %legendre.1 = (bf16[7,512,384]{2,1,0:T(8,128)(2,1)S(1)}, bf16[7,384,512]{2,1,0:T(8,128)(2,1)S(1)}) custom-call(s32[1]{0:T(128)} %bitcast.rank_ref, f32[1,768]{1,0:T(1,128)S(1)} %copy-done.8, f32[1,768]{1,0:T(1,128)S(1)} %copy-done.7, f32[64,8,128]{2,1,0:T(8,128)S(1)} %copy-done.6, f32[64,8,128]{2,1,0:T(8,128)S(1)} %copy-done.5, ...), custom_call_target="tpu_custom_call" | custom-call | tf_op jit(solution)/shard_map/legendre/pallas_call | solution.py:115
  42.3 0.0 copy-start.2
  42.3 1.5 copy-done.2
  43.8 21.1 %all-to-all-done = bf16[64,2,6528]{2,1,0:T(2,128)(2,1)} async-done(((bf16[64,2,6528]{2,1,0:T(2,128)(2,1)}), bf16[64,2,6528]{2,1,0:T(2,128)(2,1)}, u32[]{:S(2)}, u32[]{:S(2)}) %all-to-all-start) | async-done | bytes 1671200 | tf_op jit(solution)/shard_map/all_to_all | solution.py:521
  64.9 1.8 copy.28
  66.7 0.5 copy-done.3
  67.2 2.1 forward.1
  69.3 66.2 %all_to_all.20 = bf16[256,2,2176]{2,1,0:T(2,128)(2,1)S(1)} all-to-all(bf16[256,2,2176]{2,1,0:T(2,128)(2,1)S(1)} %get-tuple-element.15), channel_id=1, replica_groups=mesh['lat'=64,'chan'=4] {'chan','lat'}, dimensions={0} | all-to-all | bytes 4456448 | tf_op jit(solution)/shard_map/all_to_all | solution.py:536
  135.5 0.2 copy.24
  135.7 1.6 degree.1
  137.3 39.7 %all_to_all.21.back_ref = bf16[256,2,1088]{2,1,0:T(2,128)(2,1)S(1)} all-to-all(bf16[256,2,1088]{2,1,0:T(2,128)(2,1)S(1)} %degree.1), channel_id=1, replica_groups=mesh['lat'=64,'chan'=4] {'chan','lat'}, dimensions={0} | all-to-all | bytes 2228224 | tf_op jit(solution)/shard_map/all_to_all | solution.py:544
  177.0 1.3 backward.1
  178.3 0.0 copy-start.4
  178.3 28.2 %all_to_all.22 = bf16[64,2,3264]{2,1,0:T(2,128)(2,1)S(1)} all-to-all(bf16[64,2,3264]{2,1,0:T(2,128)(2,1)S(1)} %backward.1), channel_id=1, replica_groups=mesh['lat'=64,'chan'=4] {'lat'}, dimensions={0} | all-to-all | bytes 1671168 | tf_op jit(solution)/shard_map/all_to_all | solution.py:551
  206.5 0.1 copy.29
  206.6 0.0 copy-done.4
  206.6 1.5 synthesis.1.mine_ref
  208.1 0.5 collective-permute-start.2
  208.6 2.8 %gradient.1 = f32[2,384,384]{2,1,0:T(8,128)} custom-call(bf16[2,4,64,2176]{3,2,1,0:T(8,128)(2,1)S(1)} %bitcast.11), custom_call_target="tpu_custom_call" | custom-call | tf_op jit(solution)/shard_map/gradient/pallas_call | solution.py:115
  211.4 0.0 collective-permute-done.2.theirs_ref
  211.4 1.9 placing.1
  (2 shorter events, 0.0 us)
Async XLA Ops:
  0.6 4.7 %copy-start = (bf16[12,96,720]{2,1,0:T(8,128)(2,1)S(1)}, bf16[12,96,720]{2,1,0:T(8,128)(2,1)}, u32[]{:S(2)}) copy-start(bf16[12,96,720]{2,1,0:T(8,128)(2,1)} %field_ref.1) | copy-start | bytes 4976644
  2.0 6.7 %copy-start.1 = (bf16[12,96,720]{2,1,0:T(8,128)(2,1)S(1)}, bf16[12,96,720]{2,1,0:T(8,128)(2,1)}, u32[]{:S(2)}) copy-start(bf16[12,96,720]{2,1,0:T(8,128)(2,1)} %cotan_ref.1) | copy-start | bytes 4976644
  2.0 6.7 %copy-start.9 = (s32[64]{0:T(128)S(1)}, s32[64]{0:T(128)}, u32[]{:S(2)}) copy-start(s32[64]{0:T(128)} %counts_ref.3) | copy-start | bytes 772
  2.0 5.4 %collective-permute-start.1 = (bf16[6,96,720]{2,1,0:T(8,128)(2,1)S(1)}, bf16[6,96,720]{2,1,0:T(8,128)(2,1)S(1)}, u32[]{:S(2)}, u32[]{:S(2)}) collective-permute-start(bf16[6,96,720]{2,1,0:T(8,128)(2,1)S(1)} %constant_dynamic-slice_fusion), channel_id=1, source_target_pairs={{0,4},{4,0},{8,12},{12,8},{16,20},{20,16},{24,28},{28,24},{32,36},... | collective-permute-start | bytes 2488328 | tf_op jit(solution)/shard_map/ppermute | solution.py:506
  5.4 3.3 %collective-permute-start = (bf16[6,96,720]{2,1,0:T(8,128)(2,1)S(1)}, bf16[6,96,720]{2,1,0:T(8,128)(2,1)S(1)}, u32[]{:S(2)}, u32[]{:S(2)}) collective-permute-start(bf16[6,96,720]{2,1,0:T(8,128)(2,1)S(1)} %constant_dynamic-slice_fusion.1), channel_id=1, source_target_pairs={{0,4},{4,0},{8,12},{12,8},{16,20},{20,16},{24,28},{28,24},{32,36},... | collective-permute-start | bytes 2488328 | tf_op jit(solution)/shard_map/ppermute | solution.py:505
  12.5 10.5 %copy-start.10 = (s32[512]{0:T(512)S(1)}, s32[512]{0:T(512)}, u32[]{:S(2)}) copy-start(s32[512]{0:T(512)} %param.15) | copy-start | bytes 6148
  12.6 10.8 %copy-start.5 = (f32[64,8,128]{2,1,0:T(8,128)S(1)}, f32[64,8,128]{2,1,0:T(8,128)}, u32[]{:S(2)}) copy-start(f32[64,8,128]{2,1,0:T(8,128)} %constant.42.clone.norm_ref) | copy-start | bytes 786436
  12.6 10.8 %copy-start.6 = (f32[64,8,128]{2,1,0:T(8,128)S(1)}, f32[64,8,128]{2,1,0:T(8,128)}, u32[]{:S(2)}) copy-start(f32[64,8,128]{2,1,0:T(8,128)} %constant.41.clone.order_ref) | copy-start | bytes 786436
  12.6 10.8 %copy-start.7 = (f32[1,768]{1,0:T(1,128)S(1)}, f32[1,768]{1,0:T(1,128)}, u32[]{:S(2)}) copy-start(f32[1,768]{1,0:T(1,128)} %constant.40.clone.logsine_ref) | copy-start | bytes 9220
  12.6 10.8 %copy-start.8 = (f32[1,768]{1,0:T(1,128)S(1)}, f32[1,768]{1,0:T(1,128)}, u32[]{:S(2)}) copy-start(f32[1,768]{1,0:T(1,128)} %constant.39.clone.cosine_ref) | copy-start | bytes 9220
  12.6 52.3 %all-to-all-start = ((bf16[64,2,6528]{2,1,0:T(2,128)(2,1)}), bf16[64,2,6528]{2,1,0:T(2,128)(2,1)}, u32[]{:S(2)}, u32[]{:S(2)}) async-start(bf16[64,2,6528]{2,1,0:T(2,128)(2,1)} %analysis.1), calls=%async_computation | async-start | bytes 3342336 | tf_op jit(solution)/shard_map/all_to_all | solution.py:521
  42.3 1.5 copy-start.2
  64.9 2.3 %copy-start.3 = (bf16[7,512,384]{2,1,0:T(8,128)(2,1)S(1)}, bf16[7,512,384]{2,1,0:T(8,128)(2,1)}, u32[]{:S(2)}) copy-start(bf16[7,512,384]{2,1,0:T(8,128)(2,1)} %copy-done.2) | copy-start | bytes 8257540
  178.3 28.3 %copy-start.4 = (bf16[720,720]{1,0:T(8,128)(2,1)S(1)}, bf16[720,720]{1,0:T(8,128)(2,1)}, u32[]{:S(2)}) copy-start(bf16[720,720]{1,0:T(8,128)(2,1)} %constant.38.clone.fourier_ref) | copy-start | bytes 3110404
  208.1 3.3 %collective-permute-start.2 = (bf16[6,96,720]{2,1,0:T(8,128)(2,1)S(1)}, bf16[6,96,720]{2,1,0:T(8,128)(2,1)S(1)}, u32[]{:S(2)}, u32[]{:S(2)}) collective-permute-start(bf16[6,96,720]{2,1,0:T(8,128)(2,1)S(1)} %synthesis.1.mine_ref), channel_id=1, source_target_pairs={{0,4},{4,0},{8,12},{12,8},{16,20},{20,16},{24,28},{28,24},{32,36},... | collective-permute-start | bytes 2488328 | tf_op jit(solution)/shard_map/ppermute | solution.py:559

commit v8 on v7

--- a/solution.py
+++ b/solution.py
@@ -102,7 +102,7 @@
     return np.cos(theta).astype(np.float32), np.log(np.sin(theta)).astype(np.float32)
 
 
-def run(kernel, name, outs, args, scratch=(), home=pltpu.VMEM, far=()):
+def run(kernel, name, outs, args, scratch=(), home=pltpu.VMEM, far=(), aliases={}):
     specs, operands = [], []
     for at, arg in enumerate(args):
         if arg.dtype == jnp.int32 and arg.ndim == 1:
@@ -118,6 +118,7 @@
         in_specs=specs,
         out_specs=tuple(pl.BlockSpec(memory_space=home) for _ in outs),
         scratch_shapes=list(scratch),
+        input_output_aliases=aliases,
         compiler_params=pltpu.CompilerParams(vmem_limit_bytes=VMEM_BYTES),
         name=name,
     )(*operands)
@@ -215,7 +216,7 @@
     return run(
         legendre_kernel,
         "legendre",
-        [pltpu.VMEM((GROUPS, slots, latitudes), BF16), pltpu.VMEM((GROUPS, latitudes, slots), BF16)],
+        [pltpu.VMEM((GROUPS, slots, latitudes), BF16), pltpu.HBM((GROUPS, latitudes, slots), BF16)],
         [
             at_rank,
             jnp.asarray(cosine),
@@ -265,9 +266,26 @@
         store.start()
         stores.append(store)
 
-    step = 2
-    for j0 in range(0, FULL, step):
-        j1 = min(j0 + step, FULL)
+    third = narrow // BLOCKS
+    blocks = []
+    for b in range(BLOCKS):
+        rows = jnp.concatenate(
+            [
+                rows_ref[i * narrow + b * third : i * narrow + (b + 1) * third, :]
+                for i in range(2 * ROWS)
+            ],
+            axis=0,
+        )
+        blocks.append(
+            lax.dot_general(
+                fourier_ref[full:, :], rows, contract, preferred_element_type=F32
+            ).astype(BF16)
+        )
+    for u, unit in enumerate(unit_rows(blocks, lat_count, 2)):
+        at = FULL * width + u * (width // BLOCKS)
+        held_ref[:, :, at : at + width // BLOCKS] = unit.reshape(lat_count, 2, width // BLOCKS)
+    send(FULL * width, out_ref.shape[2])
+    for j0, j1 in ((0, 2), (2, 4), (4, FULL)):
         modes = lax.dot_general(
             fourier_ref[2 * lat_count * j0 : 2 * lat_count * j1, :],
             rows_ref[...],
@@ -278,34 +296,21 @@
             held_ref[:, :, j * width : (j + 1) * width] = modes[
                 2 * lat_count * (j - j0) : 2 * lat_count * (j - j0 + 1)
             ].reshape(lat_count, 2, width)
-        if j1 < FULL:
-            send(j0 * width, j1 * width)
-    third = narrow // BLOCKS
-    blocks = []
-    for b in range(BLOCKS):
-        rows = jnp.concatenate(
-            [
-                rows_ref[i * narrow + b * third : i * narrow + (b + 1) * third, :]
-                for i in range(2 * ROWS)
-            ],
-            axis=0,
-        )
-        blocks.append(
-            lax.dot_general(
-                fourier_ref[full:, :], rows, contract, preferred_element_type=F32
-            ).astype(BF16)
-        )
-    for u, unit in enumerate(unit_rows(blocks, lat_count, 2)):
-        at = FULL * width + u * (width // BLOCKS)
-        held_ref[:, :, at : at + width // BLOCKS] = unit.reshape(lat_count, 2, width // BLOCKS)
-    send((FULL - 1) // step * step * width, out_ref.shape[2])
+        send(j0 * width, j1 * width)
     for store in stores:
         store.wait()
 
 
-def forward_kernel(rank_ref, modes_ref, legendre_ref, stored_ref, out_ref, weights_ref, sem):
-    load = pltpu.make_async_copy(stored_ref, weights_ref, sem)
-    load.start()
+def forward_kernel(
+    rank_ref, modes_ref, legendre_ref, stored_ref, stored_pairs_ref,
+    out_ref, weights_ref, pairs_ref, sems,
+):
+    loads = [
+        pltpu.make_async_copy(stored_pairs_ref, pairs_ref, sems.at[0]),
+        pltpu.make_async_copy(stored_ref, weights_ref, sems.at[1]),
+    ]
+    for load in loads:
+        load.start()
     owners = out_ref.shape[0]
     slots = legendre_ref.shape[1]
     read = write = 0
@@ -334,7 +339,8 @@
         )
         read += ROWS * width
         write += 2 * width
-    load.wait()
+    for load in loads:
+        load.wait()
 
 
 def side(coeffs_ref, s, w):
@@ -397,16 +403,6 @@
             back_ref[y * lat_count : (y + 1) * lat_count, s, :] = jnp.concatenate(pieces, axis=1)
 
 
-def gradient_kernel(coeffs_ref, grad_ref):
-    for s in range(2):
-        grad_ref[s] = lax.dot_general(
-            side(coeffs_ref, s, 0),
-            side(coeffs_ref, s, 1),
-            (((0,), (0,)), ((), ())),
-            preferred_element_type=F32,
-        )
-
-
 def backward_kernel(back_ref, legendre_ref, out_ref):
     slots = legendre_ref.shape[2]
     lat_count = out_ref.shape[0]
@@ -456,32 +452,55 @@
         out_ref[k] = grad[k * narrow : (k + 1) * narrow, :]
 
 
-def placing_kernel(counts_ref, rank_ref, mine_ref, theirs_ref, out_ref, empty_ref, sems):
+def held_rows(counts_ref, rank_ref):
     rank = rank_ref[0]
     odd = rank % 2
     first = counts_ref[rank - odd]
-    start = odd * first
     count = jnp.where(odd == 1, 2 * ROWS - first, first)
+    slots = []
+    for r in range(2 * ROWS):
+        at = odd * first + r
+        slots.append((r < count, (at // ROWS) == odd, jnp.clip(at % ROWS, 0, ROWS - 1)))
+    return slots
+
+
+def gradient_kernel(
+    counts_ref, rank_ref, coeffs_ref, mine_ref, grad_ref, out_ref, held_ref, empty_ref, sems, grad_sems
+):
     empty_ref[...] = jnp.zeros_like(empty_ref)
-    copies = []
-    for r in range(2 * ROWS):
-        at = start + r
-        live = r < count
-        own = (at // ROWS) == odd
+    rows = []
+    for r, (live, own, at) in enumerate(held_rows(counts_ref, rank_ref)):
         target, sem = out_ref.at[r], sems.at[r]
-        near = pltpu.make_async_copy(
-            mine_ref.at[jnp.clip(at - odd * ROWS, 0, ROWS - 1)], target, sem
-        )
-        far = pltpu.make_async_copy(
-            theirs_ref.at[jnp.clip(at - (1 - odd) * ROWS, 0, ROWS - 1)], target, sem
-        )
+        near = pltpu.make_async_copy(mine_ref.at[at], target, sem)
         dead = pltpu.make_async_copy(empty_ref, target, sem)
         pl.when(live & own)(near.start)
-        pl.when(live & jnp.logical_not(own))(far.start)
         pl.when(jnp.logical_not(live))(dead.start)
-        copies.append(near)
-    for copy in copies:
-        copy.wait()
+        rows.append((jnp.logical_not(live) | own, near))
+    stores = []
+    for s in range(2):
+        held_ref[s] = lax.dot_general(
+            side(coeffs_ref, s, 0),
+            side(coeffs_ref, s, 1),
+            (((0,), (0,)), ((), ())),
+            preferred_element_type=F32,
+        )
+        stores.append(pltpu.make_async_copy(held_ref.at[s], grad_ref.at[s], grad_sems.at[s]))
+        stores[-1].start()
+    for started, row in rows:
+        pl.when(started)(row.wait)
+    for store in stores:
+        store.wait()
+
+
+def placing_kernel(counts_ref, rank_ref, theirs_ref, placed_ref, out_ref, sems):
+    rows = []
+    for r, (live, own, at) in enumerate(held_rows(counts_ref, rank_ref)):
+        wanted = live & jnp.logical_not(own)
+        row = pltpu.make_async_copy(theirs_ref.at[at], out_ref.at[r], sems.at[r])
+        pl.when(wanted)(row.start)
+        rows.append((wanted, row))
+    for wanted, row in rows:
+        pl.when(wanted)(row.wait)
 
 
 def on_device(field_in, cotangent, weights, row_counts, slot_degree):
@@ -522,16 +541,17 @@
     modes = modes.transpose(1, 0, 2)
     slot_rows = slot_degree.reshape(lat_count, chan_count, held).transpose(1, 0, 2).reshape(-1)
     legendre, legendre_pairs = legendre_slots(at_rank, lat_count, slot_rows)
-    coeffs, weights = run(
+    coeffs, weights, legendre_pairs = run(
         forward_kernel,
         "forward",
         [
             pltpu.VMEM((devices, held, 4 * pieces * third), BF16),
             pltpu.VMEM(weights.shape, BF16),
+            pltpu.VMEM(legendre_pairs.shape, BF16),
         ],
-        [at_rank, modes, legendre, weights],
-        [pltpu.SemaphoreType.DMA],
-        far=(3,),
+        [at_rank, modes, legendre, weights, legendre_pairs],
+        [pltpu.SemaphoreType.DMA((2,))],
+        far=(3, 4),
     )
     coeffs = lax.all_to_all(coeffs, everyone, split_axis=0, concat_axis=0, tiled=True)
     coeffs = coeffs.transpose(1, 0, 2).reshape(held, chan_count, lat_count, 4 * pieces * third)
@@ -557,17 +577,29 @@
     )
     grad, coeffs = lax.optimization_barrier((grad, coeffs))
     grad_swap = lax.ppermute(grad, "lat", pairs)
-    weight_grad = run(
-        gradient_kernel, "gradient", [jax.ShapeDtypeStruct((held, full, full), F32)], [coeffs]
-    )
-    grad_swap, weight_grad = lax.optimization_barrier((grad_swap, weight_grad))
+    weight_grad, placed = run(
+        gradient_kernel,
+        "gradient",
+        [pltpu.HBM((held, full, full), F32), pltpu.HBM(field_in.shape, BF16)],
+        [row_counts, at_rank, coeffs, grad],
+        [
+            pltpu.VMEM((held, full, full), F32),
+            pltpu.VMEM((narrow, NLON), BF16),
+            pltpu.SemaphoreType.DMA((2 * ROWS,)),
+            pltpu.SemaphoreType.DMA((held,)),
+        ],
+        home=pltpu.HBM,
+    )
+    grad_swap, placed = lax.optimization_barrier((grad_swap, placed))
     field_grad = run(
         placing_kernel,
         "placing",
-        [jax.ShapeDtypeStruct(field_in.shape, BF16)],
-        [row_counts, at_rank, grad, grad_swap],
-        [pltpu.VMEM((narrow, NLON), BF16), pltpu.SemaphoreType.DMA((2 * ROWS,))],
-        pl.ANY,
+        [pltpu.HBM(field_in.shape, BF16)],
+        [row_counts, at_rank, grad_swap, placed],
+        [pltpu.SemaphoreType.DMA((2 * ROWS,))],
+        home=pltpu.HBM,
+        far=(3,),
+        aliases={3: 0},
     )
     return field_grad, weight_grad
 

time: 214 us -> 213 us (level)
  local copies, waits for them, and re-layouts: 5.9 us -> 3.69 us
  transfers between devices with their start and end apart: 4 -> 4, of which waited for: 3 -> 3; matrix products, arithmetic and copies ran while one was open for 0% -> 0% of each run, Pallas kernels for 11% -> 12%
where the time goes in v8:
time: 213 us
  blocking collectives  134 us (63%)
  Pallas kernels  36.6 us (17%)
  waiting for transfers between devices  22.7 us (11%)
  starting transfers between devices  14.6 us (7%)
  local copies, waits for them, and re-layouts  3.69 us (2%)
    all_to_all x1, blocking collectives, on_device(): lax.all_to_all(coeffs, everyone, split_axis=0, concat_axis=0, tiled=True)  66.2 us
    all_to_all x1, blocking collectives, on_device(): lax.all_to_all(back, everyone, split_axis=0, concat_axis=0, tiled=True)  39.6 us
    pallas_call x9, Pallas kernels, run(): pl.pallas_call(kernel, out_shape=tuple(outs), in_specs=specs, out_specs=t...  36.6 us
    all_to_all x1, blocking collectives, on_device(): lax.all_to_all(modes_back, 'lat', split_axis=0, concat_axis=0, tiled=True)  28.2 us
    all_to_all x1, waiting for transfers between devices, on_device(): lax.all_to_all(modes, 'lat', split_axis=0, concat_axis=0, tiled=True)  21.1 us
    all_to_all x1, starting transfers between devices, on_device(): lax.all_to_all(modes, 'lat', split_axis=0, concat_axis=0, tiled=True)  10.4 us
  transfers between devices with their start and end apart: 4, of which 3 were waited for; matrix products, arithmetic and copies ran while one was open for 0% of the time, Pallas kernels for 12%

profile of v8, /device:TPU:1, one launch (start us, length us, event | category | flops | bytes accessed | tf_op | source)
XLA Modules:
  0.0 212.6 jit_solution(16014756088958095987)
XLA Ops:
  0.6 0.0 copy-start
  0.7 1.4 constant_dynamic-slice_fusion
  2.0 0.0 copy-start.1
  2.0 0.0 copy-start.5
  2.0 3.3 %collective-permute-start.1 = (bf16[6,96,720]{2,1,0:T(8,128)(2,1)S(1)}, bf16[6,96,720]{2,1,0:T(8,128)(2,1)S(1)}, u32[]{:S(2)}, u32[]{:S(2)}) collective-permute-start(bf16[6,96,720]{2,1,0:T(8,128)(2,1)S(1)} %constant_dynamic-slice_fusion), channel_id=1, source_target_pairs={{0,4},{4,0},{8,12},{12,8},{16,20},{20,16},{24,28},{28,24},{32,36},... | collective-permute-start | bytes 2488328 | tf_op jit(solution)/shard_map/ppermute | solution.py:525
  5.4 0.0 copy-done
  5.4 0.1 constant_dynamic-slice_fusion.1
  5.4 0.3 collective-permute-start
  5.8 1.3 fourier.1.fourier_ref
  7.0 0.4 collective-permute-done.1.cotan_in_ref
  7.4 1.3 collective-permute-done.field_in_ref
  8.7 0.0 copy-done.1
  8.7 0.0 copy-done.5
  8.7 3.8 %analysis.1 = bf16[64,2,6528]{2,1,0:T(2,128)(2,1)} custom-call(s32[64]{0:T(128)S(1)} %copy-done.5, s32[1]{0:T(128)} %bitcast.rank_ref, bf16[12,96,720]{2,1,0:T(8,128)(2,1)S(1)} %copy-done, bf16[12,96,720]{2,1,0:T(8,128)(2,1)S(1)} %copy-done.1, bf16[6,96,720]{2,1,0:T(8,128)(2,1)S(1)} %collective-permute-done.field_in_ref, ...), custom_call_target="tpu_custom_call" | custom-call | tf_op jit(solution)/shard_map/analysis/pallas_call | solution.py:115
  12.5 0.0 copy-start.8
  12.5 0.0 copy-start.3
  12.5 0.0 copy-start.4
  12.5 0.0 copy-start.6
  12.5 0.0 copy-start.7
  12.6 10.4 %all-to-all-start = ((bf16[64,2,6528]{2,1,0:T(2,128)(2,1)}), bf16[64,2,6528]{2,1,0:T(2,128)(2,1)}, u32[]{:S(2)}, u32[]{:S(2)}) async-start(bf16[64,2,6528]{2,1,0:T(2,128)(2,1)} %analysis.1), calls=%async_computation | async-start | bytes 3342336 | tf_op jit(solution)/shard_map/all_to_all | solution.py:540
  23.0 0.0 copy-done.8
  23.0 0.2 reshape.14
  23.2 0.1 broadcast_in_dim_reshape.4.slot_ref
  23.3 0.0 copy-done.3
  23.3 0.0 copy-done.4
  23.3 0.0 copy-done.6
  23.4 0.0 copy-done.7
  23.4 20.4 %legendre.1 = (bf16[7,512,384]{2,1,0:T(8,128)(2,1)S(1)}, bf16[7,384,512]{2,1,0:T(8,128)(2,1)}) custom-call(s32[1]{0:T(128)} %bitcast.rank_ref, f32[1,768]{1,0:T(1,128)S(1)} %copy-done.7, f32[1,768]{1,0:T(1,128)S(1)} %copy-done.6, f32[64,8,128]{2,1,0:T(8,128)S(1)} %copy-done.4, f32[64,8,128]{2,1,0:T(8,128)S(1)} %copy-done.3, ...), custom_call_target="tpu_custom_call" | custom-call | tf_op jit(solution)/shard_map/legendre/pallas_call | solution.py:115
  43.8 21.1 %all-to-all-done = bf16[64,2,6528]{2,1,0:T(2,128)(2,1)} async-done(((bf16[64,2,6528]{2,1,0:T(2,128)(2,1)}), bf16[64,2,6528]{2,1,0:T(2,128)(2,1)}, u32[]{:S(2)}, u32[]{:S(2)}) %all-to-all-start) | async-done | bytes 1671200 | tf_op jit(solution)/shard_map/all_to_all | solution.py:540
  64.8 1.6 copy.29
  66.4 2.2 %forward.1 = (bf16[256,2,2176]{2,1,0:T(2,128)(2,1)S(1)}, bf16[2,384,384]{2,1,0:T(8,128)(2,1)S(1)}, bf16[7,384,512]{2,1,0:T(8,128)(2,1)S(1)}) custom-call(s32[1]{0:T(128)} %bitcast.rank_ref, bf16[2,64,6528]{2,1,0:T(8,128)(2,1)S(1)} %bitcast.12, bf16[7,512,384]{2,1,0:T(8,128)(2,1)S(1)} %get-tuple-element.17.legendre_ref, bf16[2,384,384]{2,1,0:T(8,128)(2,1)} %stored_ref.1, ...), custom_call_target="tpu_custom_call" | custom-call | tf_op jit(solution)/shard_map/forward/pallas_call | solution.py:115
  68.6 66.2 %all_to_all.20 = bf16[256,2,2176]{2,1,0:T(2,128)(2,1)S(1)} all-to-all(bf16[256,2,2176]{2,1,0:T(2,128)(2,1)S(1)} %get-tuple-element.19), channel_id=1, replica_groups=mesh['lat'=64,'chan'=4] {'chan','lat'}, dimensions={0} | all-to-all | bytes 4456448 | tf_op jit(solution)/shard_map/all_to_all | solution.py:556
  134.8 0.2 copy.25
  135.0 1.7 degree.1
  136.7 39.6 %all_to_all.21.back_ref = bf16[256,2,1088]{2,1,0:T(2,128)(2,1)S(1)} all-to-all(bf16[256,2,1088]{2,1,0:T(2,128)(2,1)S(1)} %degree.1), channel_id=1, replica_groups=mesh['lat'=64,'chan'=4] {'chan','lat'}, dimensions={0} | all-to-all | bytes 2228224 | tf_op jit(solution)/shard_map/all_to_all | solution.py:564
  176.3 1.3 backward.1
  177.6 0.0 copy-start.2
  177.6 28.2 %all_to_all.22 = bf16[64,2,3264]{2,1,0:T(2,128)(2,1)S(1)} all-to-all(bf16[64,2,3264]{2,1,0:T(2,128)(2,1)S(1)} %backward.1), channel_id=1, replica_groups=mesh['lat'=64,'chan'=4] {'lat'}, dimensions={0} | all-to-all | bytes 1671168 | tf_op jit(solution)/shard_map/all_to_all | solution.py:571
  205.9 0.1 copy.30
  205.9 0.0 copy-done.2
  206.0 1.5 synthesis.1.mine_ref
  207.4 0.5 collective-permute-start.2
  207.9 3.7 %gradient.1 = (f32[2,384,384]{2,1,0:T(8,128)}, bf16[12,96,720]{2,1,0:T(8,128)(2,1)}) custom-call(s32[64]{0:T(128)S(1)} %copy-done.5, s32[1]{0:T(128)} %bitcast.rank_ref, bf16[2,4,64,2176]{3,2,1,0:T(8,128)(2,1)S(1)} %bitcast.11, bf16[6,96,720]{2,1,0:T(8,128)(2,1)S(1)} %synthesis.1.mine_ref), custom_call_target="tpu_custom_call" | custom-call | tf_op jit(solution)/shard_map/gradient/pallas_call | solution.py:115
  211.6 0.0 collective-permute-done.2.theirs_ref
  211.6 0.8 placing.1
  (1 shorter events, 0.0 us)
Async XLA Ops:
  0.6 4.7 %copy-start = (bf16[12,96,720]{2,1,0:T(8,128)(2,1)S(1)}, bf16[12,96,720]{2,1,0:T(8,128)(2,1)}, u32[]{:S(2)}) copy-start(bf16[12,96,720]{2,1,0:T(8,128)(2,1)} %field_ref.1) | copy-start | bytes 4976644
  2.0 6.7 %copy-start.1 = (bf16[12,96,720]{2,1,0:T(8,128)(2,1)S(1)}, bf16[12,96,720]{2,1,0:T(8,128)(2,1)}, u32[]{:S(2)}) copy-start(bf16[12,96,720]{2,1,0:T(8,128)(2,1)} %cotan_ref.1) | copy-start | bytes 4976644
  2.0 6.7 %copy-start.5 = (s32[64]{0:T(128)S(1)}, s32[64]{0:T(128)}, u32[]{:S(2)}) copy-start(s32[64]{0:T(128)} %counts_ref.5) | copy-start | bytes 772
  2.0 5.4 %collective-permute-start.1 = (bf16[6,96,720]{2,1,0:T(8,128)(2,1)S(1)}, bf16[6,96,720]{2,1,0:T(8,128)(2,1)S(1)}, u32[]{:S(2)}, u32[]{:S(2)}) collective-permute-start(bf16[6,96,720]{2,1,0:T(8,128)(2,1)S(1)} %constant_dynamic-slice_fusion), channel_id=1, source_target_pairs={{0,4},{4,0},{8,12},{12,8},{16,20},{20,16},{24,28},{28,24},{32,36},... | collective-permute-start | bytes 2488328 | tf_op jit(solution)/shard_map/ppermute | solution.py:525
  5.4 3.3 %collective-permute-start = (bf16[6,96,720]{2,1,0:T(8,128)(2,1)S(1)}, bf16[6,96,720]{2,1,0:T(8,128)(2,1)S(1)}, u32[]{:S(2)}, u32[]{:S(2)}) collective-permute-start(bf16[6,96,720]{2,1,0:T(8,128)(2,1)S(1)} %constant_dynamic-slice_fusion.1), channel_id=1, source_target_pairs={{0,4},{4,0},{8,12},{12,8},{16,20},{20,16},{24,28},{28,24},{32,36},... | collective-permute-start | bytes 2488328 | tf_op jit(solution)/shard_map/ppermute | solution.py:524
  12.5 10.5 %copy-start.8 = (s32[512]{0:T(512)S(1)}, s32[512]{0:T(512)}, u32[]{:S(2)}) copy-start(s32[512]{0:T(512)} %param.15) | copy-start | bytes 6148
  12.5 10.8 %copy-start.3 = (f32[64,8,128]{2,1,0:T(8,128)S(1)}, f32[64,8,128]{2,1,0:T(8,128)}, u32[]{:S(2)}) copy-start(f32[64,8,128]{2,1,0:T(8,128)} %constant.42.clone.norm_ref) | copy-start | bytes 786436
  12.5 10.8 %copy-start.4 = (f32[64,8,128]{2,1,0:T(8,128)S(1)}, f32[64,8,128]{2,1,0:T(8,128)}, u32[]{:S(2)}) copy-start(f32[64,8,128]{2,1,0:T(8,128)} %constant.41.clone.order_ref) | copy-start | bytes 786436
  12.5 10.8 %copy-start.6 = (f32[1,768]{1,0:T(1,128)S(1)}, f32[1,768]{1,0:T(1,128)}, u32[]{:S(2)}) copy-start(f32[1,768]{1,0:T(1,128)} %constant.40.clone.logsine_ref) | copy-start | bytes 9220
  12.5 10.8 %copy-start.7 = (f32[1,768]{1,0:T(1,128)S(1)}, f32[1,768]{1,0:T(1,128)}, u32[]{:S(2)}) copy-start(f32[1,768]{1,0:T(1,128)} %constant.39.clone.cosine_ref) | copy-start | bytes 9220
  12.6 52.3 %all-to-all-start = ((bf16[64,2,6528]{2,1,0:T(2,128)(2,1)}), bf16[64,2,6528]{2,1,0:T(2,128)(2,1)}, u32[]{:S(2)}, u32[]{:S(2)}) async-start(bf16[64,2,6528]{2,1,0:T(2,128)(2,1)} %analysis.1), calls=%async_computation | async-start | bytes 3342336 | tf_op jit(solution)/shard_map/all_to_all | solution.py:540
  177.6 28.3 %copy-start.2 = (bf16[720,720]{1,0:T(8,128)(2,1)S(1)}, bf16[720,720]{1,0:T(8,128)(2,1)}, u32[]{:S(2)}) copy-start(bf16[720,720]{1,0:T(8,128)(2,1)} %constant.38.clone.fourier_ref) | copy-start | bytes 3110404
  207.4 4.2 %collective-permute-start.2 = (bf16[6,96,720]{2,1,0:T(8,128)(2,1)S(1)}, bf16[6,96,720]{2,1,0:T(8,128)(2,1)S(1)}, u32[]{:S(2)}, u32[]{:S(2)}) collective-permute-start(bf16[6,96,720]{2,1,0:T(8,128)(2,1)S(1)} %synthesis.1.mine_ref), channel_id=1, source_target_pairs={{0,4},{4,0},{8,12},{12,8},{16,20},{20,16},{24,28},{28,24},{32,36},... | collective-permute-start | bytes 2488328 | tf_op jit(solution)/shard_map/ppermute | solution.py:579

commit v9 on v8

--- a/solution.py
+++ b/solution.py
@@ -102,7 +102,7 @@
     return np.cos(theta).astype(np.float32), np.log(np.sin(theta)).astype(np.float32)
 
 
-def run(kernel, name, outs, args, scratch=(), home=pltpu.VMEM, far=(), aliases={}):
+def run(kernel, name, outs, args, scratch=(), far=(), aliases={}):
     specs, operands = [], []
     for at, arg in enumerate(args):
         if arg.dtype == jnp.int32 and arg.ndim == 1:
@@ -116,7 +116,7 @@
         kernel,
         out_shape=tuple(outs),
         in_specs=specs,
-        out_specs=tuple(pl.BlockSpec(memory_space=home) for _ in outs),
+        out_specs=tuple(pl.BlockSpec(memory_space=out.memory_space) for out in outs),
         scratch_shapes=list(scratch),
         input_output_aliases=aliases,
         compiler_params=pltpu.CompilerParams(vmem_limit_bytes=VMEM_BYTES),
@@ -129,6 +129,24 @@
     copy = pltpu.make_async_copy(stored_ref, out_ref, sem)
     copy.start()
     copy.wait()
+
+
+def slicing_kernel(rank_ref, stored_ref, out_ref, sem):
+    start = (1 - rank_ref[0] % 2) * ROWS
+    copy = pltpu.make_async_copy(stored_ref.at[pl.ds(start, ROWS)], out_ref, sem)
+    copy.start()
+    copy.wait()
+
+
+def surplus(at_rank, array, name):
+    return run(
+        slicing_kernel,
+        name,
+        [pltpu.VMEM((ROWS,) + array.shape[1:], array.dtype)],
+        [at_rank, array],
+        [pltpu.SemaphoreType.DMA],
+        far=(1,),
+    )
 
 
 def loaded(array, name):
@@ -142,10 +160,28 @@
     )
 
 
+def held_rows(counts_ref, rank_ref):
+    rank = rank_ref[0]
+    odd = rank % 2
+    first = counts_ref[rank - odd]
+    count = jnp.where(odd == 1, 2 * ROWS - first, first)
+    slots = []
+    for r in range(2 * ROWS):
+        at = odd * first + r
+        slots.append((r < count, (at // ROWS) == odd, jnp.clip(at % ROWS, 0, ROWS - 1)))
+    return slots
+
+
 def legendre_kernel(
-    rank_ref, cosine_ref, logsine_ref, order_ref, norm_ref, slot_ref,
-    rows_out_ref, pairs_out_ref, rows_ref,
+    counts_ref, rank_ref, cosine_ref, logsine_ref, order_ref, norm_ref, slot_ref,
+    rows_out_ref, pairs_out_ref, placed_ref, rows_ref, table_ref, empty_ref, sems,
 ):
+    empty_ref[...] = jnp.zeros_like(empty_ref)
+    stores = []
+    for r, (live, _, _) in enumerate(held_rows(counts_ref, rank_ref)):
+        store = pltpu.make_async_copy(empty_ref, placed_ref.at[r], sems.at[r])
+        pl.when(jnp.logical_not(live))(store.start)
+        stores.append((jnp.logical_not(live), store))
     rank = rank_ref[0]
     latitudes = rows_out_ref.shape[2]
     shape = (8, 128)
@@ -203,12 +239,19 @@
         table = rows_ref[:, j, :latitudes].astype(BF16)
         rows_out_ref[j] = jnp.dot(pick, table, preferred_element_type=F32).astype(BF16)
         table = rows_ref[:, j, latitudes:].astype(BF16)
-        pairs_out_ref[j] = lax.dot_general(
+        table_ref[j] = lax.dot_general(
             table, pick, (((0,), (1,)), ((), ())), preferred_element_type=F32
         ).astype(BF16)
-
-
-def legendre_slots(at_rank, lat_count, slot_rows):
+        store = pltpu.make_async_copy(
+            table_ref.at[j], pairs_out_ref.at[j], sems.at[2 * ROWS + j]
+        )
+        store.start()
+        stores.append((True, store))
+    for started, store in stores:
+        pl.when(started)(store.wait)
+
+
+def legendre_slots(row_counts, at_rank, lat_count, slot_rows, placed):
     slots = slot_rows.shape[0]
     latitudes = ROWS * lat_count
     cosine, logsine = latitude_rows(lat_count)
@@ -216,8 +259,13 @@
     return run(
         legendre_kernel,
         "legendre",
-        [pltpu.VMEM((GROUPS, slots, latitudes), BF16), pltpu.HBM((GROUPS, latitudes, slots), BF16)],
         [
+            pltpu.VMEM((GROUPS, slots, latitudes), BF16),
+            pltpu.HBM((GROUPS, latitudes, slots), BF16),
+            pltpu.HBM(placed, BF16),
+        ],
+        [
+            row_counts,
             at_rank,
             jnp.asarray(cosine),
             jnp.asarray(logsine),
@@ -225,7 +273,12 @@
             jnp.asarray(norms),
             slot_rows[:, None],
         ],
-        [pltpu.VMEM((LPAD, 8, 2 * latitudes), F32)],
+        [
+            pltpu.VMEM((LPAD, 8, 2 * latitudes), F32),
+            pltpu.VMEM((GROUPS, latitudes, slots), BF16),
+            pltpu.VMEM(placed[1:], BF16),
+            pltpu.SemaphoreType.DMA((2 * ROWS + GROUPS,)),
+        ],
     )
 
 
@@ -452,30 +505,14 @@
         out_ref[k] = grad[k * narrow : (k + 1) * narrow, :]
 
 
-def held_rows(counts_ref, rank_ref):
-    rank = rank_ref[0]
-    odd = rank % 2
-    first = counts_ref[rank - odd]
-    count = jnp.where(odd == 1, 2 * ROWS - first, first)
-    slots = []
-    for r in range(2 * ROWS):
-        at = odd * first + r
-        slots.append((r < count, (at // ROWS) == odd, jnp.clip(at % ROWS, 0, ROWS - 1)))
-    return slots
-
-
 def gradient_kernel(
-    counts_ref, rank_ref, coeffs_ref, mine_ref, grad_ref, out_ref, held_ref, empty_ref, sems, grad_sems
+    counts_ref, rank_ref, coeffs_ref, mine_ref, placed_ref, grad_ref, out_ref, held_ref, sems, grad_sems
 ):
-    empty_ref[...] = jnp.zeros_like(empty_ref)
     rows = []
     for r, (live, own, at) in enumerate(held_rows(counts_ref, rank_ref)):
-        target, sem = out_ref.at[r], sems.at[r]
-        near = pltpu.make_async_copy(mine_ref.at[at], target, sem)
-        dead = pltpu.make_async_copy(empty_ref, target, sem)
-        pl.when(live & own)(near.start)
-        pl.when(jnp.logical_not(live))(dead.start)
-        rows.append((jnp.logical_not(live) | own, near))
+        row = pltpu.make_async_copy(mine_ref.at[at], out_ref.at[r], sems.at[r])
+        pl.when(live & own)(row.start)
+        rows.append((live & own, row))
     stores = []
     for s in range(2):
         held_ref[s] = lax.dot_general(
@@ -511,15 +548,14 @@
     held, full = weights.shape[:2]
     devices = lat_count * chan_count
     pairs = [(i, i ^ 1) for i in range(lat_count)]
-    odd = rank % 2
     at_rank = jnp.reshape(rank, (1,)).astype(jnp.int32)
     by_rank, by_part = (jnp.asarray(table) for table in fourier_tables(lat_count))
     pieces = FULL * BLOCKS + UNITS
     third = narrow // BLOCKS
     everyone = ("chan", "lat")
 
-    field_send = lax.dynamic_slice_in_dim(field_in, (1 - odd) * ROWS, ROWS)
-    cotan_send = lax.dynamic_slice_in_dim(cotangent, (1 - odd) * ROWS, ROWS)
+    cotan_send = surplus(at_rank, cotangent, "cotangent_rows")
+    field_send = surplus(at_rank, field_in, "field_rows")
     field_send, by_rank = lax.optimization_barrier((field_send, by_rank))
     field_swap = lax.ppermute(field_send, "lat", pairs)
     cotan_swap = lax.ppermute(cotan_send, "lat", pairs)
@@ -535,12 +571,13 @@
             pltpu.VMEM((lat_count, 2, pieces * width // BLOCKS), BF16),
             pltpu.SemaphoreType.DMA((GROUPS,)),
         ],
-        home=pltpu.HBM,
     )
     modes = lax.all_to_all(modes, "lat", split_axis=0, concat_axis=0, tiled=True)
     modes = modes.transpose(1, 0, 2)
     slot_rows = slot_degree.reshape(lat_count, chan_count, held).transpose(1, 0, 2).reshape(-1)
-    legendre, legendre_pairs = legendre_slots(at_rank, lat_count, slot_rows)
+    legendre, legendre_pairs, placed = legendre_slots(
+        row_counts, at_rank, lat_count, slot_rows, field_in.shape
+    )
     coeffs, weights, legendre_pairs = run(
         forward_kernel,
         "forward",
@@ -581,14 +618,14 @@
         gradient_kernel,
         "gradient",
         [pltpu.HBM((held, full, full), F32), pltpu.HBM(field_in.shape, BF16)],
-        [row_counts, at_rank, coeffs, grad],
+        [row_counts, at_rank, coeffs, grad, placed],
         [
             pltpu.VMEM((held, full, full), F32),
-            pltpu.VMEM((narrow, NLON), BF16),
             pltpu.SemaphoreType.DMA((2 * ROWS,)),
             pltpu.SemaphoreType.DMA((held,)),
         ],
-        home=pltpu.HBM,
+        far=(4,),
+        aliases={4: 1},
     )
     grad_swap, placed = lax.optimization_barrier((grad_swap, placed))
     field_grad = run(
@@ -597,7 +634,6 @@
         [pltpu.HBM(field_in.shape, BF16)],
         [row_counts, at_rank, grad_swap, placed],
         [pltpu.SemaphoreType.DMA((2 * ROWS,))],
-        home=pltpu.HBM,
         far=(3,),
         aliases={3: 0},
     )

time: 213 us -> 213 us (level)
  Pallas kernels: 36.6 us -> 38.9 us
    pallas_call x9 -> x11, Pallas kernels: 36.6 us -> 38.9 us  [run(): pl.pallas_call(kernel, out_shape=tuple(outs), in_specs=specs, out_specs=t...]
  transfers between devices with their start and end apart: 4 -> 4, of which waited for: 3 -> 2; matrix products, arithmetic and copies ran while one was open for 0% -> 0% of each run, Pallas kernels for 12% -> 12%
where the time goes in v9:
time: 213 us; the launch traced here: 212 us
  blocking collectives  134 us (63%)
  Pallas kernels  38.9 us (18%)
  waiting for transfers between devices  21.9 us (10%)
  starting transfers between devices  14.1 us (7%)
  local copies, waits for them, and re-layouts  2.28 us (1%)
    all_to_all x1, blocking collectives, on_device(): lax.all_to_all(coeffs, everyone, split_axis=0, concat_axis=0, tiled=True)  66.2 us
    all_to_all x1, blocking collectives, on_device(): lax.all_to_all(back, everyone, split_axis=0, concat_axis=0, tiled=True)  39.7 us
    pallas_call x11, Pallas kernels, run(): pl.pallas_call(kernel, out_shape=tuple(outs), in_specs=specs, out_specs=t...  38.9 us
    all_to_all x1, blocking collectives, on_device(): lax.all_to_all(modes_back, 'lat', split_axis=0, concat_axis=0, tiled=True)  28.2 us
    all_to_all x1, waiting for transfers between devices, on_device(): lax.all_to_all(modes, 'lat', split_axis=0, concat_axis=0, tiled=True)  20.9 us
    all_to_all x1, starting transfers between devices, on_device(): lax.all_to_all(modes, 'lat', split_axis=0, concat_axis=0, tiled=True)  10.2 us
  transfers between devices with their start and end apart: 4, of which 2 were waited for; matrix products, arithmetic and copies ran while one was open for 0% of the time, Pallas kernels for 12%

profile of v9, /device:TPU:1, one launch (start us, length us, event | category | flops | bytes accessed | tf_op | source)
XLA Modules:
  0.0 212.4 jit_solution(8820144041117470332)
XLA Ops:
  0.6 1.2 cotangent_rows.1
  1.8 3.3 %collective-permute-start.1 = (bf16[6,96,720]{2,1,0:T(8,128)(2,1)S(1)}, bf16[6,96,720]{2,1,0:T(8,128)(2,1)S(1)}, u32[]{:S(2)}, u32[]{:S(2)}) collective-permute-start(bf16[6,96,720]{2,1,0:T(8,128)(2,1)S(1)} %cotangent_rows.1), channel_id=1, source_target_pairs={{0,4},{4,0},{8,12},{12,8},{16,20},{20,16},{24,28},{28,24},{32,36},... | collective-permute-start | bytes 2488328 | tf_op jit(solution)/shard_map/ppermute | solution.py:561
  5.2 0.0 copy-start.1
  5.2 1.3 field_rows.1
  6.5 0.0 copy-start
  6.5 0.0 copy-start.5
  6.5 0.1 collective-permute-start
  6.6 1.4 fourier.1.fourier_ref
  8.0 0.0 collective-permute-done.1.cotan_in_ref
  8.0 1.0 collective-permute-done.field_in_ref
  9.0 0.0 copy-done.1
  9.0 0.0 copy-done
  9.0 0.0 copy-done.5
  9.0 3.9 %analysis.1 = bf16[64,2,6528]{2,1,0:T(2,128)(2,1)} custom-call(s32[64]{0:T(128)S(1)} %copy-done.5, s32[1]{0:T(128)} %bitcast.rank_ref, bf16[12,96,720]{2,1,0:T(8,128)(2,1)S(1)} %copy-done, bf16[12,96,720]{2,1,0:T(8,128)(2,1)S(1)} %copy-done.1, bf16[6,96,720]{2,1,0:T(8,128)(2,1)S(1)} %collective-permute-done.field_in_ref, ...), custom_call_target="tpu_custom_call" | custom-call | tf_op jit(solution)/shard_map/analysis/pallas_call | solution.py:115
  12.9 0.0 copy-start.8
  12.9 0.0 copy-start.3
  12.9 0.0 copy-start.4
  12.9 0.0 copy-start.6
  12.9 0.0 copy-start.7
  13.0 10.2 %all-to-all-start = ((bf16[64,2,6528]{2,1,0:T(2,128)(2,1)}), bf16[64,2,6528]{2,1,0:T(2,128)(2,1)}, u32[]{:S(2)}, u32[]{:S(2)}) async-start(bf16[64,2,6528]{2,1,0:T(2,128)(2,1)} %analysis.1), calls=%async_computation | async-start | bytes 3342336 | tf_op jit(solution)/shard_map/all_to_all | solution.py:575
  23.2 0.0 copy-done.8
  23.2 0.2 reshape.14
  23.4 0.1 broadcast_in_dim_reshape.4.slot_ref
  23.5 0.0 copy-done.3
  23.5 0.0 copy-done.4
  23.5 0.0 copy-done.6
  23.5 0.0 copy-done.7
  23.5 20.5 %legendre.1 = (bf16[7,512,384]{2,1,0:T(8,128)(2,1)S(1)}, bf16[7,384,512]{2,1,0:T(8,128)(2,1)}, bf16[12,96,720]{2,1,0:T(8,128)(2,1)}) custom-call(s32[64]{0:T(128)S(1)} %copy-done.5, s32[1]{0:T(128)} %bitcast.rank_ref, f32[1,768]{1,0:T(1,128)S(1)} %copy-done.7, f32[1,768]{1,0:T(1,128)S(1)} %copy-done.6, f32[64,8,128]{2,1,0:T(8,128)S(1)} %copy-done.4, ...), custom_call_target="tpu_custom_call" | custom-call | tf_op jit(solution)/shard_map/legendre/pallas_call | solution.py:115
  44.1 20.9 %all-to-all-done = bf16[64,2,6528]{2,1,0:T(2,128)(2,1)} async-done(((bf16[64,2,6528]{2,1,0:T(2,128)(2,1)}), bf16[64,2,6528]{2,1,0:T(2,128)(2,1)}, u32[]{:S(2)}, u32[]{:S(2)}) %all-to-all-start) | async-done | bytes 1671200 | tf_op jit(solution)/shard_map/all_to_all | solution.py:575
  65.0 1.6 copy.30
  66.6 2.2 %forward.1 = (bf16[256,2,2176]{2,1,0:T(2,128)(2,1)S(1)}, bf16[2,384,384]{2,1,0:T(8,128)(2,1)S(1)}, bf16[7,384,512]{2,1,0:T(8,128)(2,1)S(1)}) custom-call(s32[1]{0:T(128)} %bitcast.rank_ref, bf16[2,64,6528]{2,1,0:T(8,128)(2,1)S(1)} %bitcast.12, bf16[7,512,384]{2,1,0:T(8,128)(2,1)S(1)} %get-tuple-element.18.legendre_ref, bf16[2,384,384]{2,1,0:T(8,128)(2,1)} %stored_ref.5, ...), custom_call_target="tpu_custom_call" | custom-call | tf_op jit(solution)/shard_map/forward/pallas_call | solution.py:115
  68.8 66.2 %all_to_all.20 = bf16[256,2,2176]{2,1,0:T(2,128)(2,1)S(1)} all-to-all(bf16[256,2,2176]{2,1,0:T(2,128)(2,1)S(1)} %get-tuple-element.20), channel_id=1, replica_groups=mesh['lat'=64,'chan'=4] {'chan','lat'}, dimensions={0} | all-to-all | bytes 4456448 | tf_op jit(solution)/shard_map/all_to_all | solution.py:593
  135.0 0.2 copy.26
  135.2 1.6 degree.1
  136.9 39.7 %all_to_all.21.back_ref = bf16[256,2,1088]{2,1,0:T(2,128)(2,1)S(1)} all-to-all(bf16[256,2,1088]{2,1,0:T(2,128)(2,1)S(1)} %degree.1), channel_id=1, replica_groups=mesh['lat'=64,'chan'=4] {'chan','lat'}, dimensions={0} | all-to-all | bytes 2228224 | tf_op jit(solution)/shard_map/all_to_all | solution.py:601
  176.5 1.3 backward.1
  177.8 0.0 copy-start.2
  177.8 28.2 %all_to_all.22 = bf16[64,2,3264]{2,1,0:T(2,128)(2,1)S(1)} all-to-all(bf16[64,2,3264]{2,1,0:T(2,128)(2,1)S(1)} %backward.1), channel_id=1, replica_groups=mesh['lat'=64,'chan'=4] {'lat'}, dimensions={0} | all-to-all | bytes 1671168 | tf_op jit(solution)/shard_map/all_to_all | solution.py:608
  206.1 0.1 copy.31
  206.1 0.0 copy-done.2
  206.2 1.5 synthesis.1.mine_ref
  207.6 0.5 collective-permute-start.2
  208.1 3.3 %gradient.1 = (f32[2,384,384]{2,1,0:T(8,128)}, bf16[12,96,720]{2,1,0:T(8,128)(2,1)}) custom-call(s32[64]{0:T(128)S(1)} %copy-done.5, s32[1]{0:T(128)} %bitcast.rank_ref, bf16[2,4,64,2176]{3,2,1,0:T(8,128)(2,1)S(1)} %bitcast.11, bf16[6,96,720]{2,1,0:T(8,128)(2,1)S(1)} %synthesis.1.mine_ref, ...), custom_call_target="tpu_custom_call", output_to_operand_aliasing={{1}: (4, {})} | custom-call | tf_op jit(solution)/shard_map/gradient/pallas_call | solution.py:115
  211.4 0.0 collective-permute-done.2.theirs_ref
  211.4 0.8 placing.1
  (1 shorter events, 0.0 us)
Async XLA Ops:
  1.8 6.2 %collective-permute-start.1 = (bf16[6,96,720]{2,1,0:T(8,128)(2,1)S(1)}, bf16[6,96,720]{2,1,0:T(8,128)(2,1)S(1)}, u32[]{:S(2)}, u32[]{:S(2)}) collective-permute-start(bf16[6,96,720]{2,1,0:T(8,128)(2,1)S(1)} %cotangent_rows.1), channel_id=1, source_target_pairs={{0,4},{4,0},{8,12},{12,8},{16,20},{20,16},{24,28},{28,24},{32,36},... | collective-permute-start | bytes 2488328 | tf_op jit(solution)/shard_map/ppermute | solution.py:561
  5.2 3.9 %copy-start.1 = (bf16[12,96,720]{2,1,0:T(8,128)(2,1)S(1)}, bf16[12,96,720]{2,1,0:T(8,128)(2,1)}, u32[]{:S(2)}) copy-start(bf16[12,96,720]{2,1,0:T(8,128)(2,1)} %cotan_ref.1) | copy-start | bytes 4976644
  6.5 2.5 %copy-start = (bf16[12,96,720]{2,1,0:T(8,128)(2,1)S(1)}, bf16[12,96,720]{2,1,0:T(8,128)(2,1)}, u32[]{:S(2)}) copy-start(bf16[12,96,720]{2,1,0:T(8,128)(2,1)} %field_ref.1) | copy-start | bytes 4976644
  6.5 2.5 %copy-start.5 = (s32[64]{0:T(128)S(1)}, s32[64]{0:T(128)}, u32[]{:S(2)}) copy-start(s32[64]{0:T(128)} %counts_ref.7) | copy-start | bytes 772
  6.5 2.5 %collective-permute-start = (bf16[6,96,720]{2,1,0:T(8,128)(2,1)S(1)}, bf16[6,96,720]{2,1,0:T(8,128)(2,1)S(1)}, u32[]{:S(2)}, u32[]{:S(2)}) collective-permute-start(bf16[6,96,720]{2,1,0:T(8,128)(2,1)S(1)} %field_rows.1), channel_id=1, source_target_pairs={{0,4},{4,0},{8,12},{12,8},{16,20},{20,16},{24,28},{28,24},{32,36},... | collective-permute-start | bytes 2488328 | tf_op jit(solution)/shard_map/ppermute | solution.py:560
  12.9 10.3 %copy-start.8 = (s32[512]{0:T(512)S(1)}, s32[512]{0:T(512)}, u32[]{:S(2)}) copy-start(s32[512]{0:T(512)} %param.15) | copy-start | bytes 6148
  12.9 10.6 %copy-start.3 = (f32[64,8,128]{2,1,0:T(8,128)S(1)}, f32[64,8,128]{2,1,0:T(8,128)}, u32[]{:S(2)}) copy-start(f32[64,8,128]{2,1,0:T(8,128)} %constant.23.clone.norm_ref) | copy-start | bytes 786436
  12.9 10.6 %copy-start.4 = (f32[64,8,128]{2,1,0:T(8,128)S(1)}, f32[64,8,128]{2,1,0:T(8,128)}, u32[]{:S(2)}) copy-start(f32[64,8,128]{2,1,0:T(8,128)} %constant.22.clone.order_ref) | copy-start | bytes 786436
  12.9 10.6 %copy-start.6 = (f32[1,768]{1,0:T(1,128)S(1)}, f32[1,768]{1,0:T(1,128)}, u32[]{:S(2)}) copy-start(f32[1,768]{1,0:T(1,128)} %constant.21.clone.logsine_ref) | copy-start | bytes 9220
  12.9 10.6 %copy-start.7 = (f32[1,768]{1,0:T(1,128)S(1)}, f32[1,768]{1,0:T(1,128)}, u32[]{:S(2)}) copy-start(f32[1,768]{1,0:T(1,128)} %constant.20.clone.cosine_ref) | copy-start | bytes 9220
  13.0 52.0 %all-to-all-start = ((bf16[64,2,6528]{2,1,0:T(2,128)(2,1)}), bf16[64,2,6528]{2,1,0:T(2,128)(2,1)}, u32[]{:S(2)}, u32[]{:S(2)}) async-start(bf16[64,2,6528]{2,1,0:T(2,128)(2,1)} %analysis.1), calls=%async_computation | async-start | bytes 3342336 | tf_op jit(solution)/shard_map/all_to_all | solution.py:575
  177.8 28.3 %copy-start.2 = (bf16[720,720]{1,0:T(8,128)(2,1)S(1)}, bf16[720,720]{1,0:T(8,128)(2,1)}, u32[]{:S(2)}) copy-start(bf16[720,720]{1,0:T(8,128)(2,1)} %constant.19.clone.fourier_ref) | copy-start | bytes 3110404
  207.6 3.8 %collective-permute-start.2 = (bf16[6,96,720]{2,1,0:T(8,128)(2,1)S(1)}, bf16[6,96,720]{2,1,0:T(8,128)(2,1)S(1)}, u32[]{:S(2)}, u32[]{:S(2)}) collective-permute-start(bf16[6,96,720]{2,1,0:T(8,128)(2,1)S(1)} %synthesis.1.mine_ref), channel_id=1, source_target_pairs={{0,4},{4,0},{8,12},{12,8},{16,20},{20,16},{24,28},{28,24},{32,36},... | collective-permute-start | bytes 2488328 | tf_op jit(solution)/shard_map/ppermute | solution.py:616

commit v10 on v9

--- a/solution.py
+++ b/solution.py
@@ -129,24 +129,6 @@
     copy = pltpu.make_async_copy(stored_ref, out_ref, sem)
     copy.start()
     copy.wait()
-
-
-def slicing_kernel(rank_ref, stored_ref, out_ref, sem):
-    start = (1 - rank_ref[0] % 2) * ROWS
-    copy = pltpu.make_async_copy(stored_ref.at[pl.ds(start, ROWS)], out_ref, sem)
-    copy.start()
-    copy.wait()
-
-
-def surplus(at_rank, array, name):
-    return run(
-        slicing_kernel,
-        name,
-        [pltpu.VMEM((ROWS,) + array.shape[1:], array.dtype)],
-        [at_rank, array],
-        [pltpu.SemaphoreType.DMA],
-        far=(1,),
-    )
 
 
 def loaded(array, name):
@@ -505,39 +487,40 @@
         out_ref[k] = grad[k * narrow : (k + 1) * narrow, :]
 
 
-def gradient_kernel(
-    counts_ref, rank_ref, coeffs_ref, mine_ref, placed_ref, grad_ref, out_ref, held_ref, sems, grad_sems
-):
-    rows = []
+def finish(slot, near, counts_ref, rank_ref, coeffs_ref, rows_ref, grad_ref, out_ref, held_ref, sems):
+    copies = []
     for r, (live, own, at) in enumerate(held_rows(counts_ref, rank_ref)):
-        row = pltpu.make_async_copy(mine_ref.at[at], out_ref.at[r], sems.at[r])
-        pl.when(live & own)(row.start)
-        rows.append((live & own, row))
+        wanted = live & (own if near else jnp.logical_not(own))
+        copy = pltpu.make_async_copy(rows_ref.at[at], out_ref.at[r], sems.at[r])
+        pl.when(wanted)(copy.start)
+        copies.append((wanted, copy))
+    coeffs = side(coeffs_ref, slot, 0)
+    dcoeffs = side(coeffs_ref, slot, 1)
+    full = held_ref.shape[0]
     stores = []
-    for s in range(2):
-        held_ref[s] = lax.dot_general(
-            side(coeffs_ref, s, 0),
-            side(coeffs_ref, s, 1),
-            (((0,), (0,)), ((), ())),
-            preferred_element_type=F32,
-        )
-        stores.append(pltpu.make_async_copy(held_ref.at[s], grad_ref.at[s], grad_sems.at[s]))
+    for i, (lo, hi) in enumerate(((0, 256), (256, full))):
+        held_ref[lo:hi, :] = lax.dot_general(
+            coeffs[:, lo:hi], dcoeffs, (((0,), (0,)), ((), ())), preferred_element_type=F32
+        )
+        part = pl.ds(lo, hi - lo)
+        stores.append(
+            pltpu.make_async_copy(
+                held_ref.at[part], grad_ref.at[slot, part], sems.at[2 * ROWS + i]
+            )
+        )
         stores[-1].start()
-    for started, row in rows:
-        pl.when(started)(row.wait)
+    for wanted, copy in copies:
+        pl.when(wanted)(copy.wait)
     for store in stores:
         store.wait()
 
 
-def placing_kernel(counts_ref, rank_ref, theirs_ref, placed_ref, out_ref, sems):
-    rows = []
-    for r, (live, own, at) in enumerate(held_rows(counts_ref, rank_ref)):
-        wanted = live & jnp.logical_not(own)
-        row = pltpu.make_async_copy(theirs_ref.at[at], out_ref.at[r], sems.at[r])
-        pl.when(wanted)(row.start)
-        rows.append((wanted, row))
-    for wanted, row in rows:
-        pl.when(wanted)(row.wait)
+def first_kernel(counts_ref, rank_ref, coeffs_ref, rows_ref, _, grad_ref, out_ref, held_ref, sems):
+    finish(0, True, counts_ref, rank_ref, coeffs_ref, rows_ref, grad_ref, out_ref, held_ref, sems)
+
+
+def second_kernel(counts_ref, rank_ref, coeffs_ref, rows_ref, _, __, grad_ref, out_ref, held_ref, sems):
+    finish(1, False, counts_ref, rank_ref, coeffs_ref, rows_ref, grad_ref, out_ref, held_ref, sems)
 
 
 def on_device(field_in, cotangent, weights, row_counts, slot_degree):
@@ -548,14 +531,15 @@
     held, full = weights.shape[:2]
     devices = lat_count * chan_count
     pairs = [(i, i ^ 1) for i in range(lat_count)]
+    odd = rank % 2
     at_rank = jnp.reshape(rank, (1,)).astype(jnp.int32)
     by_rank, by_part = (jnp.asarray(table) for table in fourier_tables(lat_count))
     pieces = FULL * BLOCKS + UNITS
     third = narrow // BLOCKS
     everyone = ("chan", "lat")
 
-    cotan_send = surplus(at_rank, cotangent, "cotangent_rows")
-    field_send = surplus(at_rank, field_in, "field_rows")
+    field_send = lax.dynamic_slice_in_dim(field_in, (1 - odd) * ROWS, ROWS)
+    cotan_send = lax.dynamic_slice_in_dim(cotangent, (1 - odd) * ROWS, ROWS)
     field_send, by_rank = lax.optimization_barrier((field_send, by_rank))
     field_swap = lax.ppermute(field_send, "lat", pairs)
     cotan_swap = lax.ppermute(cotan_send, "lat", pairs)
@@ -614,28 +598,26 @@
     )
     grad, coeffs = lax.optimization_barrier((grad, coeffs))
     grad_swap = lax.ppermute(grad, "lat", pairs)
+    outs = [pltpu.HBM((held, full, full), F32), pltpu.HBM(field_in.shape, BF16)]
+    scratch = [pltpu.VMEM((full, full), F32), pltpu.SemaphoreType.DMA((2 * ROWS + 2,))]
     weight_grad, placed = run(
-        gradient_kernel,
-        "gradient",
-        [pltpu.HBM((held, full, full), F32), pltpu.HBM(field_in.shape, BF16)],
+        first_kernel,
+        "first_slot",
+        outs,
         [row_counts, at_rank, coeffs, grad, placed],
-        [
-            pltpu.VMEM((held, full, full), F32),
-            pltpu.SemaphoreType.DMA((2 * ROWS,)),
-            pltpu.SemaphoreType.DMA((held,)),
-        ],
+        scratch,
         far=(4,),
         aliases={4: 1},
     )
     grad_swap, placed = lax.optimization_barrier((grad_swap, placed))
-    field_grad = run(
-        placing_kernel,
-        "placing",
-        [pltpu.HBM(field_in.shape, BF16)],
-        [row_counts, at_rank, grad_swap, placed],
-        [pltpu.SemaphoreType.DMA((2 * ROWS,))],
-        far=(3,),
-        aliases={3: 0},
+    weight_grad, field_grad = run(
+        second_kernel,
+        "second_slot",
+        outs,
+        [row_counts, at_rank, coeffs, grad_swap, weight_grad, placed],
+        scratch,
+        far=(4, 5),
+        aliases={4: 0, 5: 1},
     )
     return field_grad, weight_grad
 

time: 213 us -> 214 us (level)
    pallas_call x11 -> x9, Pallas kernels: 38.9 us -> 37.3 us  [run(): pl.pallas_call(kernel, out_shape=tuple(outs), in_specs=specs, out_specs=t...]
  transfers between devices with their start and end apart: 4 -> 4, of which waited for: 2 -> 3; matrix products, arithmetic and copies ran while one was open for 0% -> 0% of each run, Pallas kernels for 12% -> 11%
where the time goes in v10:
time: 214 us; the launch traced here: 213 us
  blocking collectives  134 us (63%)
  Pallas kernels  37.3 us (17%)
  waiting for transfers between devices  22.6 us (11%)
  starting transfers between devices  14.6 us (7%)
  local copies, waits for them, and re-layouts  3.69 us (2%)
    all_to_all x1, blocking collectives, on_device(): lax.all_to_all(coeffs, everyone, split_axis=0, concat_axis=0, tiled=True)  66.2 us
    all_to_all x1, blocking collectives, on_device(): lax.all_to_all(back, everyone, split_axis=0, concat_axis=0, tiled=True)  39.7 us
    pallas_call x9, Pallas kernels, run(): pl.pallas_call(kernel, out_shape=tuple(outs), in_specs=specs, out_specs=t...  37.3 us
    all_to_all x1, blocking collectives, on_device(): lax.all_to_all(modes_back, 'lat', split_axis=0, concat_axis=0, tiled=True)  28.2 us
    all_to_all x1, waiting for transfers between devices, on_device(): lax.all_to_all(modes, 'lat', split_axis=0, concat_axis=0, tiled=True)  20.9 us
    all_to_all x1, starting transfers between devices, on_device(): lax.all_to_all(modes, 'lat', split_axis=0, concat_axis=0, tiled=True)  10.4 us
  transfers between devices with their start and end apart: 4, of which 3 were waited for; matrix products, arithmetic and copies ran while one was open for 0% of the time, Pallas kernels for 11%

profile of v10, /device:TPU:1, one launch (start us, length us, event | category | flops | bytes accessed | tf_op | source)
XLA Modules:
  0.0 213.3 jit_solution(5135214805696926840)
XLA Ops:
  0.6 0.0 copy-start
  0.7 1.4 constant_dynamic-slice_fusion
  2.0 0.0 copy-start.1
  2.0 0.0 copy-start.5
  2.0 3.3 %collective-permute-start.1 = (bf16[6,96,720]{2,1,0:T(8,128)(2,1)S(1)}, bf16[6,96,720]{2,1,0:T(8,128)(2,1)S(1)}, u32[]{:S(2)}, u32[]{:S(2)}) collective-permute-start(bf16[6,96,720]{2,1,0:T(8,128)(2,1)S(1)} %constant_dynamic-slice_fusion), channel_id=1, source_target_pairs={{0,4},{4,0},{8,12},{12,8},{16,20},{20,16},{24,28},{28,24},{32,36},... | collective-permute-start | bytes 2488328 | tf_op jit(solution)/shard_map/ppermute | solution.py:545
  5.4 0.0 copy-done
  5.4 0.1 constant_dynamic-slice_fusion.1
  5.4 0.3 collective-permute-start
  5.8 1.3 fourier.1.fourier_ref
  7.0 0.4 collective-permute-done.1.cotan_in_ref
  7.4 1.3 collective-permute-done.field_in_ref
  8.7 0.0 copy-done.1
  8.7 0.0 copy-done.5
  8.7 3.8 %analysis.1 = bf16[64,2,6528]{2,1,0:T(2,128)(2,1)} custom-call(s32[64]{0:T(128)S(1)} %copy-done.5, s32[1]{0:T(128)} %bitcast.rank_ref, bf16[12,96,720]{2,1,0:T(8,128)(2,1)S(1)} %copy-done, bf16[12,96,720]{2,1,0:T(8,128)(2,1)S(1)} %copy-done.1, bf16[6,96,720]{2,1,0:T(8,128)(2,1)S(1)} %collective-permute-done.field_in_ref, ...), custom_call_target="tpu_custom_call" | custom-call | tf_op jit(solution)/shard_map/analysis/pallas_call | solution.py:115
  12.5 0.0 copy-start.8
  12.5 0.0 copy-start.3
  12.5 0.0 copy-start.4
  12.6 0.0 copy-start.6
  12.6 0.0 copy-start.7
  12.6 10.4 %all-to-all-start = ((bf16[64,2,6528]{2,1,0:T(2,128)(2,1)}), bf16[64,2,6528]{2,1,0:T(2,128)(2,1)}, u32[]{:S(2)}, u32[]{:S(2)}) async-start(bf16[64,2,6528]{2,1,0:T(2,128)(2,1)} %analysis.1), calls=%async_computation | async-start | bytes 3342336 | tf_op jit(solution)/shard_map/all_to_all | solution.py:559
  23.0 0.0 copy-done.8
  23.0 0.2 reshape.14
  23.3 0.1 broadcast_in_dim_reshape.4.slot_ref
  23.4 0.0 copy-done.3
  23.4 0.0 copy-done.4
  23.4 0.0 copy-done.6
  23.4 0.0 copy-done.7
  23.4 20.5 %legendre.1 = (bf16[7,512,384]{2,1,0:T(8,128)(2,1)S(1)}, bf16[7,384,512]{2,1,0:T(8,128)(2,1)}, bf16[12,96,720]{2,1,0:T(8,128)(2,1)}) custom-call(s32[64]{0:T(128)S(1)} %copy-done.5, s32[1]{0:T(128)} %bitcast.rank_ref, f32[1,768]{1,0:T(1,128)S(1)} %copy-done.7, f32[1,768]{1,0:T(1,128)S(1)} %copy-done.6, f32[64,8,128]{2,1,0:T(8,128)S(1)} %copy-done.4, ...), custom_call_target="tpu_custom_call" | custom-call | tf_op jit(solution)/shard_map/legendre/pallas_call | solution.py:115
  43.9 20.9 %all-to-all-done = bf16[64,2,6528]{2,1,0:T(2,128)(2,1)} async-done(((bf16[64,2,6528]{2,1,0:T(2,128)(2,1)}), bf16[64,2,6528]{2,1,0:T(2,128)(2,1)}, u32[]{:S(2)}, u32[]{:S(2)}) %all-to-all-start) | async-done | bytes 1671200 | tf_op jit(solution)/shard_map/all_to_all | solution.py:559
  64.9 1.6 copy.31
  66.5 2.2 %forward.1 = (bf16[256,2,2176]{2,1,0:T(2,128)(2,1)S(1)}, bf16[2,384,384]{2,1,0:T(8,128)(2,1)S(1)}, bf16[7,384,512]{2,1,0:T(8,128)(2,1)S(1)}) custom-call(s32[1]{0:T(128)} %bitcast.rank_ref, bf16[2,64,6528]{2,1,0:T(8,128)(2,1)S(1)} %bitcast.13, bf16[7,512,384]{2,1,0:T(8,128)(2,1)S(1)} %get-tuple-element.20.legendre_ref, bf16[2,384,384]{2,1,0:T(8,128)(2,1)} %stored_ref.1, ...), custom_call_target="tpu_custom_call" | custom-call | tf_op jit(solution)/shard_map/forward/pallas_call | solution.py:115
  68.6 66.2 %all_to_all.20 = bf16[256,2,2176]{2,1,0:T(2,128)(2,1)S(1)} all-to-all(bf16[256,2,2176]{2,1,0:T(2,128)(2,1)S(1)} %get-tuple-element.22), channel_id=1, replica_groups=mesh['lat'=64,'chan'=4] {'chan','lat'}, dimensions={0} | all-to-all | bytes 4456448 | tf_op jit(solution)/shard_map/all_to_all | solution.py:577
  134.8 0.2 copy.27
  135.1 1.6 degree.1
  136.7 39.7 %all_to_all.21.back_ref = bf16[256,2,1088]{2,1,0:T(2,128)(2,1)S(1)} all-to-all(bf16[256,2,1088]{2,1,0:T(2,128)(2,1)S(1)} %degree.1), channel_id=1, replica_groups=mesh['lat'=64,'chan'=4] {'chan','lat'}, dimensions={0} | all-to-all | bytes 2228224 | tf_op jit(solution)/shard_map/all_to_all | solution.py:585
  176.4 1.3 backward.1
  177.7 0.0 copy-start.2
  177.7 28.2 %all_to_all.22 = bf16[64,2,3264]{2,1,0:T(2,128)(2,1)S(1)} all-to-all(bf16[64,2,3264]{2,1,0:T(2,128)(2,1)S(1)} %backward.1), channel_id=1, replica_groups=mesh['lat'=64,'chan'=4] {'lat'}, dimensions={0} | all-to-all | bytes 1671168 | tf_op jit(solution)/shard_map/all_to_all | solution.py:592
  205.9 0.1 copy.32
  206.0 0.0 copy-done.2
  206.0 1.5 synthesis.1.rows_ref
  207.5 0.5 collective-permute-start.2
  207.9 2.7 %first_slot.1 = (f32[2,384,384]{2,1,0:T(8,128)}, bf16[12,96,720]{2,1,0:T(8,128)(2,1)}) custom-call(s32[64]{0:T(128)S(1)} %copy-done.5, s32[1]{0:T(128)} %bitcast.rank_ref, bf16[2,4,64,2176]{3,2,1,0:T(8,128)(2,1)S(1)} %bitcast.11, bf16[6,96,720]{2,1,0:T(8,128)(2,1)S(1)} %synthesis.1.rows_ref, ...), custom_call_target="tpu_custom_call", output_to_operand_aliasing={{1}: (4, {})} | custom-call | tf_op jit(solution)/shard_map/first_slot/pallas_call | solution.py:115
  210.6 0.0 collective-permute-done.2.rows_ref
  210.6 2.5 %second_slot.1 = (f32[2,384,384]{2,1,0:T(8,128)}, bf16[12,96,720]{2,1,0:T(8,128)(2,1)}) custom-call(s32[64]{0:T(128)S(1)} %copy-done.5, s32[1]{0:T(128)} %bitcast.rank_ref, bf16[2,4,64,2176]{3,2,1,0:T(8,128)(2,1)S(1)} %bitcast.12, bf16[6,96,720]{2,1,0:T(8,128)(2,1)S(1)} %collective-permute-done.2.rows_ref, ...), custom_call_target="tpu_custom_call", output_to_operand_aliasing={{0}: (4, {}), {1}: (5, {})} | custom-call | tf_op jit(solution)/shard_map/second_slot/pallas_call | solution.py:115
  (1 shorter events, 0.0 us)
Async XLA Ops:
  0.6 4.7 %copy-start = (bf16[12,96,720]{2,1,0:T(8,128)(2,1)S(1)}, bf16[12,96,720]{2,1,0:T(8,128)(2,1)}, u32[]{:S(2)}) copy-start(bf16[12,96,720]{2,1,0:T(8,128)(2,1)} %field_ref.1) | copy-start | bytes 4976644
  2.0 6.7 %copy-start.1 = (bf16[12,96,720]{2,1,0:T(8,128)(2,1)S(1)}, bf16[12,96,720]{2,1,0:T(8,128)(2,1)}, u32[]{:S(2)}) copy-start(bf16[12,96,720]{2,1,0:T(8,128)(2,1)} %cotan_ref.1) | copy-start | bytes 4976644
  2.0 6.7 %copy-start.5 = (s32[64]{0:T(128)S(1)}, s32[64]{0:T(128)}, u32[]{:S(2)}) copy-start(s32[64]{0:T(128)} %counts_ref.7) | copy-start | bytes 772
  2.0 5.4 %collective-permute-start.1 = (bf16[6,96,720]{2,1,0:T(8,128)(2,1)S(1)}, bf16[6,96,720]{2,1,0:T(8,128)(2,1)S(1)}, u32[]{:S(2)}, u32[]{:S(2)}) collective-permute-start(bf16[6,96,720]{2,1,0:T(8,128)(2,1)S(1)} %constant_dynamic-slice_fusion), channel_id=1, source_target_pairs={{0,4},{4,0},{8,12},{12,8},{16,20},{20,16},{24,28},{28,24},{32,36},... | collective-permute-start | bytes 2488328 | tf_op jit(solution)/shard_map/ppermute | solution.py:545
  5.4 3.3 %collective-permute-start = (bf16[6,96,720]{2,1,0:T(8,128)(2,1)S(1)}, bf16[6,96,720]{2,1,0:T(8,128)(2,1)S(1)}, u32[]{:S(2)}, u32[]{:S(2)}) collective-permute-start(bf16[6,96,720]{2,1,0:T(8,128)(2,1)S(1)} %constant_dynamic-slice_fusion.1), channel_id=1, source_target_pairs={{0,4},{4,0},{8,12},{12,8},{16,20},{20,16},{24,28},{28,24},{32,36},... | collective-permute-start | bytes 2488328 | tf_op jit(solution)/shard_map/ppermute | solution.py:544
  12.5 10.5 %copy-start.8 = (s32[512]{0:T(512)S(1)}, s32[512]{0:T(512)}, u32[]{:S(2)}) copy-start(s32[512]{0:T(512)} %param.15) | copy-start | bytes 6148
  12.5 10.8 %copy-start.3 = (f32[64,8,128]{2,1,0:T(8,128)S(1)}, f32[64,8,128]{2,1,0:T(8,128)}, u32[]{:S(2)}) copy-start(f32[64,8,128]{2,1,0:T(8,128)} %constant.42.clone.norm_ref) | copy-start | bytes 786436
  12.5 10.8 %copy-start.4 = (f32[64,8,128]{2,1,0:T(8,128)S(1)}, f32[64,8,128]{2,1,0:T(8,128)}, u32[]{:S(2)}) copy-start(f32[64,8,128]{2,1,0:T(8,128)} %constant.41.clone.order_ref) | copy-start | bytes 786436
  12.6 10.8 %copy-start.6 = (f32[1,768]{1,0:T(1,128)S(1)}, f32[1,768]{1,0:T(1,128)}, u32[]{:S(2)}) copy-start(f32[1,768]{1,0:T(1,128)} %constant.40.clone.logsine_ref) | copy-start | bytes 9220
  12.6 10.8 %copy-start.7 = (f32[1,768]{1,0:T(1,128)S(1)}, f32[1,768]{1,0:T(1,128)}, u32[]{:S(2)}) copy-start(f32[1,768]{1,0:T(1,128)} %constant.39.clone.cosine_ref) | copy-start | bytes 9220
  12.6 52.3 %all-to-all-start = ((bf16[64,2,6528]{2,1,0:T(2,128)(2,1)}), bf16[64,2,6528]{2,1,0:T(2,128)(2,1)}, u32[]{:S(2)}, u32[]{:S(2)}) async-start(bf16[64,2,6528]{2,1,0:T(2,128)(2,1)} %analysis.1), calls=%async_computation | async-start | bytes 3342336 | tf_op jit(solution)/shard_map/all_to_all | solution.py:559
  177.7 28.3 %copy-start.2 = (bf16[720,720]{1,0:T(8,128)(2,1)S(1)}, bf16[720,720]{1,0:T(8,128)(2,1)}, u32[]{:S(2)}) copy-start(bf16[720,720]{1,0:T(8,128)(2,1)} %constant.38.clone.fourier_ref) | copy-start | bytes 3110404
  207.5 3.2 %collective-permute-start.2 = (bf16[6,96,720]{2,1,0:T(8,128)(2,1)S(1)}, bf16[6,96,720]{2,1,0:T(8,128)(2,1)S(1)}, u32[]{:S(2)}, u32[]{:S(2)}) collective-permute-start(bf16[6,96,720]{2,1,0:T(8,128)(2,1)S(1)} %synthesis.1.rows_ref), channel_id=1, source_target_pairs={{0,4},{4,0},{8,12},{12,8},{16,20},{20,16},{24,28},{28,24},{32,36},... | collective-permute-start | bytes 2488328 | tf_op jit(solution)/shard_map/ppermute | solution.py:600

commit v11 on v10

--- a/solution.py
+++ b/solution.py
@@ -487,40 +487,45 @@
         out_ref[k] = grad[k * narrow : (k + 1) * narrow, :]
 
 
-def finish(slot, near, counts_ref, rank_ref, coeffs_ref, rows_ref, grad_ref, out_ref, held_ref, sems):
+def place(near, counts_ref, rank_ref, rows_ref, out_ref, sems):
     copies = []
     for r, (live, own, at) in enumerate(held_rows(counts_ref, rank_ref)):
         wanted = live & (own if near else jnp.logical_not(own))
         copy = pltpu.make_async_copy(rows_ref.at[at], out_ref.at[r], sems.at[r])
         pl.when(wanted)(copy.start)
         copies.append((wanted, copy))
-    coeffs = side(coeffs_ref, slot, 0)
-    dcoeffs = side(coeffs_ref, slot, 1)
-    full = held_ref.shape[0]
+    return copies
+
+
+def gradient_kernel(
+    counts_ref, rank_ref, coeffs_ref, mine_ref, _, grad_ref, out_ref, held_ref, sems, grad_sems
+):
+    copies = place(True, counts_ref, rank_ref, mine_ref, out_ref, sems)
+    full = held_ref.shape[1]
     stores = []
-    for i, (lo, hi) in enumerate(((0, 256), (256, full))):
-        held_ref[lo:hi, :] = lax.dot_general(
-            coeffs[:, lo:hi], dcoeffs, (((0,), (0,)), ((), ())), preferred_element_type=F32
-        )
-        part = pl.ds(lo, hi - lo)
-        stores.append(
-            pltpu.make_async_copy(
-                held_ref.at[part], grad_ref.at[slot, part], sems.at[2 * ROWS + i]
+    for s in range(2):
+        coeffs = side(coeffs_ref, s, 0)
+        dcoeffs = side(coeffs_ref, s, 1)
+        for lo, hi in ((0, 256), (256, full)):
+            held_ref[s, lo:hi, :] = lax.dot_general(
+                coeffs[:, lo:hi], dcoeffs, (((0,), (0,)), ((), ())), preferred_element_type=F32
             )
-        )
-        stores[-1].start()
+            part = pl.ds(lo, hi - lo)
+            stores.append(
+                pltpu.make_async_copy(
+                    held_ref.at[s, part], grad_ref.at[s, part], grad_sems.at[len(stores)]
+                )
+            )
+            stores[-1].start()
     for wanted, copy in copies:
         pl.when(wanted)(copy.wait)
     for store in stores:
         store.wait()
 
 
-def first_kernel(counts_ref, rank_ref, coeffs_ref, rows_ref, _, grad_ref, out_ref, held_ref, sems):
-    finish(0, True, counts_ref, rank_ref, coeffs_ref, rows_ref, grad_ref, out_ref, held_ref, sems)
-
-
-def second_kernel(counts_ref, rank_ref, coeffs_ref, rows_ref, _, __, grad_ref, out_ref, held_ref, sems):
-    finish(1, False, counts_ref, rank_ref, coeffs_ref, rows_ref, grad_ref, out_ref, held_ref, sems)
+def placing_kernel(counts_ref, rank_ref, theirs_ref, _, out_ref, sems):
+    for wanted, copy in place(False, counts_ref, rank_ref, theirs_ref, out_ref, sems):
+        pl.when(wanted)(copy.wait)
 
 
 def on_device(field_in, cotangent, weights, row_counts, slot_degree):
@@ -598,26 +603,28 @@
     )
     grad, coeffs = lax.optimization_barrier((grad, coeffs))
     grad_swap = lax.ppermute(grad, "lat", pairs)
-    outs = [pltpu.HBM((held, full, full), F32), pltpu.HBM(field_in.shape, BF16)]
-    scratch = [pltpu.VMEM((full, full), F32), pltpu.SemaphoreType.DMA((2 * ROWS + 2,))]
     weight_grad, placed = run(
-        first_kernel,
-        "first_slot",
-        outs,
+        gradient_kernel,
+        "gradient",
+        [pltpu.HBM((held, full, full), F32), pltpu.HBM(field_in.shape, BF16)],
         [row_counts, at_rank, coeffs, grad, placed],
-        scratch,
+        [
+            pltpu.VMEM((held, full, full), F32),
+            pltpu.SemaphoreType.DMA((2 * ROWS,)),
+            pltpu.SemaphoreType.DMA((2 * held,)),
+        ],
         far=(4,),
         aliases={4: 1},
     )
     grad_swap, placed = lax.optimization_barrier((grad_swap, placed))
-    weight_grad, field_grad = run(
-        second_kernel,
-        "second_slot",
-        outs,
-        [row_counts, at_rank, coeffs, grad_swap, weight_grad, placed],
-        scratch,
-        far=(4, 5),
-        aliases={4: 0, 5: 1},
+    field_grad = run(
+        placing_kernel,
+        "placing",
+        [pltpu.HBM(field_in.shape, BF16)],
+        [row_counts, at_rank, grad_swap, placed],
+        [pltpu.SemaphoreType.DMA((2 * ROWS,))],
+        far=(3,),
+        aliases={3: 0},
     )
     return field_grad, weight_grad
 

time: 214 us -> 213 us (level)
  transfers between devices with their start and end apart: 4 -> 4, of which waited for: 3 -> 3; matrix products, arithmetic and copies ran while one was open for 0% -> 0% of each run, Pallas kernels for 11% -> 12%
where the time goes in v11:
time: 213 us; the launch traced here: 212 us
  blocking collectives  134 us (63%)
  Pallas kernels  36.3 us (17%)
  waiting for transfers between devices  22.6 us (11%)
  starting transfers between devices  14.5 us (7%)
  local copies, waits for them, and re-layouts  3.69 us (2%)
    all_to_all x1, blocking collectives, on_device(): lax.all_to_all(coeffs, everyone, split_axis=0, concat_axis=0, tiled=True)  66.2 us
    all_to_all x1, blocking collectives, on_device(): lax.all_to_all(back, everyone, split_axis=0, concat_axis=0, tiled=True)  39.7 us
    pallas_call x9, Pallas kernels, run(): pl.pallas_call(kernel, out_shape=tuple(outs), in_specs=specs, out_specs=t...  36.3 us
    all_to_all x1, blocking collectives, on_device(): lax.all_to_all(modes_back, 'lat', split_axis=0, concat_axis=0, tiled=True)  28.2 us
    all_to_all x1, waiting for transfers between devices, on_device(): lax.all_to_all(modes, 'lat', split_axis=0, concat_axis=0, tiled=True)  20.9 us
    all_to_all x1, starting transfers between devices, on_device(): lax.all_to_all(modes, 'lat', split_axis=0, concat_axis=0, tiled=True)  10.4 us
  transfers between devices with their start and end apart: 4, of which 3 were waited for; matrix products, arithmetic and copies ran while one was open for 0% of the time, Pallas kernels for 12%

profile of v11, /device:TPU:1, one launch (start us, length us, event | category | flops | bytes accessed | tf_op | source)
XLA Modules:
  0.0 212.3 jit_solution(3929815223383155486)
XLA Ops:
  0.6 0.0 copy-start
  0.7 1.4 constant_dynamic-slice_fusion
  2.0 0.0 copy-start.1
  2.0 0.0 copy-start.5
  2.0 3.3 %collective-permute-start.1 = (bf16[6,96,720]{2,1,0:T(8,128)(2,1)S(1)}, bf16[6,96,720]{2,1,0:T(8,128)(2,1)S(1)}, u32[]{:S(2)}, u32[]{:S(2)}) collective-permute-start(bf16[6,96,720]{2,1,0:T(8,128)(2,1)S(1)} %constant_dynamic-slice_fusion), channel_id=1, source_target_pairs={{0,4},{4,0},{8,12},{12,8},{16,20},{20,16},{24,28},{28,24},{32,36},... | collective-permute-start | bytes 2488328 | tf_op jit(solution)/shard_map/ppermute | solution.py:550
  5.4 0.0 copy-done
  5.4 0.1 constant_dynamic-slice_fusion.1
  5.4 0.3 collective-permute-start
  5.8 1.3 fourier.1.fourier_ref
  7.0 0.4 collective-permute-done.1.cotan_in_ref
  7.4 1.3 collective-permute-done.field_in_ref
  8.7 0.0 copy-done.1
  8.7 0.0 copy-done.5
  8.7 3.9 %analysis.1 = bf16[64,2,6528]{2,1,0:T(2,128)(2,1)} custom-call(s32[64]{0:T(128)S(1)} %copy-done.5, s32[1]{0:T(128)} %bitcast.rank_ref, bf16[12,96,720]{2,1,0:T(8,128)(2,1)S(1)} %copy-done, bf16[12,96,720]{2,1,0:T(8,128)(2,1)S(1)} %copy-done.1, bf16[6,96,720]{2,1,0:T(8,128)(2,1)S(1)} %collective-permute-done.field_in_ref, ...), custom_call_target="tpu_custom_call" | custom-call | tf_op jit(solution)/shard_map/analysis/pallas_call | solution.py:115
  12.6 0.0 copy-start.8
  12.6 0.0 copy-start.3
  12.6 0.0 copy-start.4
  12.6 0.0 copy-start.6
  12.6 0.0 copy-start.7
  12.6 10.4 %all-to-all-start = ((bf16[64,2,6528]{2,1,0:T(2,128)(2,1)}), bf16[64,2,6528]{2,1,0:T(2,128)(2,1)}, u32[]{:S(2)}, u32[]{:S(2)}) async-start(bf16[64,2,6528]{2,1,0:T(2,128)(2,1)} %analysis.1), calls=%async_computation | async-start | bytes 3342336 | tf_op jit(solution)/shard_map/all_to_all | solution.py:564
  23.1 0.0 copy-done.8
  23.1 0.2 reshape.14
  23.3 0.1 broadcast_in_dim_reshape.4.slot_ref
  23.4 0.0 copy-done.3
  23.4 0.0 copy-done.4
  23.4 0.0 copy-done.6
  23.4 0.0 copy-done.7
  23.4 20.5 %legendre.1 = (bf16[7,512,384]{2,1,0:T(8,128)(2,1)S(1)}, bf16[7,384,512]{2,1,0:T(8,128)(2,1)}, bf16[12,96,720]{2,1,0:T(8,128)(2,1)}) custom-call(s32[64]{0:T(128)S(1)} %copy-done.5, s32[1]{0:T(128)} %bitcast.rank_ref, f32[1,768]{1,0:T(1,128)S(1)} %copy-done.7, f32[1,768]{1,0:T(1,128)S(1)} %copy-done.6, f32[64,8,128]{2,1,0:T(8,128)S(1)} %copy-done.4, ...), custom_call_target="tpu_custom_call" | custom-call | tf_op jit(solution)/shard_map/legendre/pallas_call | solution.py:115
  44.0 20.9 %all-to-all-done = bf16[64,2,6528]{2,1,0:T(2,128)(2,1)} async-done(((bf16[64,2,6528]{2,1,0:T(2,128)(2,1)}), bf16[64,2,6528]{2,1,0:T(2,128)(2,1)}, u32[]{:S(2)}, u32[]{:S(2)}) %all-to-all-start) | async-done | bytes 1671200 | tf_op jit(solution)/shard_map/all_to_all | solution.py:564
  64.9 1.6 copy.30
  66.5 2.2 %forward.1 = (bf16[256,2,2176]{2,1,0:T(2,128)(2,1)S(1)}, bf16[2,384,384]{2,1,0:T(8,128)(2,1)S(1)}, bf16[7,384,512]{2,1,0:T(8,128)(2,1)S(1)}) custom-call(s32[1]{0:T(128)} %bitcast.rank_ref, bf16[2,64,6528]{2,1,0:T(8,128)(2,1)S(1)} %bitcast.12, bf16[7,512,384]{2,1,0:T(8,128)(2,1)S(1)} %get-tuple-element.18.legendre_ref, bf16[2,384,384]{2,1,0:T(8,128)(2,1)} %stored_ref.1, ...), custom_call_target="tpu_custom_call" | custom-call | tf_op jit(solution)/shard_map/forward/pallas_call | solution.py:115
  68.7 66.2 %all_to_all.20 = bf16[256,2,2176]{2,1,0:T(2,128)(2,1)S(1)} all-to-all(bf16[256,2,2176]{2,1,0:T(2,128)(2,1)S(1)} %get-tuple-element.20), channel_id=1, replica_groups=mesh['lat'=64,'chan'=4] {'chan','lat'}, dimensions={0} | all-to-all | bytes 4456448 | tf_op jit(solution)/shard_map/all_to_all | solution.py:582
  134.9 0.2 copy.26
  135.1 1.6 degree.1
  136.8 39.7 %all_to_all.21.back_ref = bf16[256,2,1088]{2,1,0:T(2,128)(2,1)S(1)} all-to-all(bf16[256,2,1088]{2,1,0:T(2,128)(2,1)S(1)} %degree.1), channel_id=1, replica_groups=mesh['lat'=64,'chan'=4] {'chan','lat'}, dimensions={0} | all-to-all | bytes 2228224 | tf_op jit(solution)/shard_map/all_to_all | solution.py:590
  176.4 1.3 backward.1
  177.7 0.0 copy-start.2
  177.7 28.2 %all_to_all.22 = bf16[64,2,3264]{2,1,0:T(2,128)(2,1)S(1)} all-to-all(bf16[64,2,3264]{2,1,0:T(2,128)(2,1)S(1)} %backward.1), channel_id=1, replica_groups=mesh['lat'=64,'chan'=4] {'lat'}, dimensions={0} | all-to-all | bytes 1671168 | tf_op jit(solution)/shard_map/all_to_all | solution.py:597
  205.9 0.1 copy.31
  206.0 0.0 copy-done.2
  206.0 1.5 synthesis.1.mine_ref
  207.5 0.5 collective-permute-start.2
  208.0 3.3 %gradient.1 = (f32[2,384,384]{2,1,0:T(8,128)}, bf16[12,96,720]{2,1,0:T(8,128)(2,1)}) custom-call(s32[64]{0:T(128)S(1)} %copy-done.5, s32[1]{0:T(128)} %bitcast.rank_ref, bf16[2,4,64,2176]{3,2,1,0:T(8,128)(2,1)S(1)} %bitcast.11, bf16[6,96,720]{2,1,0:T(8,128)(2,1)S(1)} %synthesis.1.mine_ref, ...), custom_call_target="tpu_custom_call", output_to_operand_aliasing={{1}: (4, {})} | custom-call | tf_op jit(solution)/shard_map/gradient/pallas_call | solution.py:115
  211.3 0.0 collective-permute-done.2.theirs_ref
  211.3 0.8 placing.1
  (1 shorter events, 0.0 us)
Async XLA Ops:
  0.6 4.7 %copy-start = (bf16[12,96,720]{2,1,0:T(8,128)(2,1)S(1)}, bf16[12,96,720]{2,1,0:T(8,128)(2,1)}, u32[]{:S(2)}) copy-start(bf16[12,96,720]{2,1,0:T(8,128)(2,1)} %field_ref.1) | copy-start | bytes 4976644
  2.0 6.7 %copy-start.1 = (bf16[12,96,720]{2,1,0:T(8,128)(2,1)S(1)}, bf16[12,96,720]{2,1,0:T(8,128)(2,1)}, u32[]{:S(2)}) copy-start(bf16[12,96,720]{2,1,0:T(8,128)(2,1)} %cotan_ref.1) | copy-start | bytes 4976644
  2.0 6.7 %copy-start.5 = (s32[64]{0:T(128)S(1)}, s32[64]{0:T(128)}, u32[]{:S(2)}) copy-start(s32[64]{0:T(128)} %counts_ref.7) | copy-start | bytes 772
  2.0 5.4 %collective-permute-start.1 = (bf16[6,96,720]{2,1,0:T(8,128)(2,1)S(1)}, bf16[6,96,720]{2,1,0:T(8,128)(2,1)S(1)}, u32[]{:S(2)}, u32[]{:S(2)}) collective-permute-start(bf16[6,96,720]{2,1,0:T(8,128)(2,1)S(1)} %constant_dynamic-slice_fusion), channel_id=1, source_target_pairs={{0,4},{4,0},{8,12},{12,8},{16,20},{20,16},{24,28},{28,24},{32,36},... | collective-permute-start | bytes 2488328 | tf_op jit(solution)/shard_map/ppermute | solution.py:550
  5.4 3.3 %collective-permute-start = (bf16[6,96,720]{2,1,0:T(8,128)(2,1)S(1)}, bf16[6,96,720]{2,1,0:T(8,128)(2,1)S(1)}, u32[]{:S(2)}, u32[]{:S(2)}) collective-permute-start(bf16[6,96,720]{2,1,0:T(8,128)(2,1)S(1)} %constant_dynamic-slice_fusion.1), channel_id=1, source_target_pairs={{0,4},{4,0},{8,12},{12,8},{16,20},{20,16},{24,28},{28,24},{32,36},... | collective-permute-start | bytes 2488328 | tf_op jit(solution)/shard_map/ppermute | solution.py:549
  12.6 10.5 %copy-start.8 = (s32[512]{0:T(512)S(1)}, s32[512]{0:T(512)}, u32[]{:S(2)}) copy-start(s32[512]{0:T(512)} %param.15) | copy-start | bytes 6148
  12.6 10.8 %copy-start.3 = (f32[64,8,128]{2,1,0:T(8,128)S(1)}, f32[64,8,128]{2,1,0:T(8,128)}, u32[]{:S(2)}) copy-start(f32[64,8,128]{2,1,0:T(8,128)} %constant.42.clone.norm_ref) | copy-start | bytes 786436
  12.6 10.8 %copy-start.4 = (f32[64,8,128]{2,1,0:T(8,128)S(1)}, f32[64,8,128]{2,1,0:T(8,128)}, u32[]{:S(2)}) copy-start(f32[64,8,128]{2,1,0:T(8,128)} %constant.41.clone.order_ref) | copy-start | bytes 786436
  12.6 10.8 %copy-start.6 = (f32[1,768]{1,0:T(1,128)S(1)}, f32[1,768]{1,0:T(1,128)}, u32[]{:S(2)}) copy-start(f32[1,768]{1,0:T(1,128)} %constant.40.clone.logsine_ref) | copy-start | bytes 9220
  12.6 10.8 %copy-start.7 = (f32[1,768]{1,0:T(1,128)S(1)}, f32[1,768]{1,0:T(1,128)}, u32[]{:S(2)}) copy-start(f32[1,768]{1,0:T(1,128)} %constant.39.clone.cosine_ref) | copy-start | bytes 9220
  12.6 52.3 %all-to-all-start = ((bf16[64,2,6528]{2,1,0:T(2,128)(2,1)}), bf16[64,2,6528]{2,1,0:T(2,128)(2,1)}, u32[]{:S(2)}, u32[]{:S(2)}) async-start(bf16[64,2,6528]{2,1,0:T(2,128)(2,1)} %analysis.1), calls=%async_computation | async-start | bytes 3342336 | tf_op jit(solution)/shard_map/all_to_all | solution.py:564
  177.7 28.3 %copy-start.2 = (bf16[720,720]{1,0:T(8,128)(2,1)S(1)}, bf16[720,720]{1,0:T(8,128)(2,1)}, u32[]{:S(2)}) copy-start(bf16[720,720]{1,0:T(8,128)(2,1)} %constant.38.clone.fourier_ref) | copy-start | bytes 3110404
  207.5 3.8 %collective-permute-start.2 = (bf16[6,96,720]{2,1,0:T(8,128)(2,1)S(1)}, bf16[6,96,720]{2,1,0:T(8,128)(2,1)S(1)}, u32[]{:S(2)}, u32[]{:S(2)}) collective-permute-start(bf16[6,96,720]{2,1,0:T(8,128)(2,1)S(1)} %synthesis.1.mine_ref), channel_id=1, source_target_pairs={{0,4},{4,0},{8,12},{12,8},{16,20},{20,16},{24,28},{28,24},{32,36},... | collective-permute-start | bytes 2488328 | tf_op jit(solution)/shard_map/ppermute | solution.py:605

commit v12 on v8

--- a/solution.py
+++ b/solution.py
@@ -371,7 +371,9 @@
     return jnp.concatenate(rows, axis=0)
 
 
-def degree_kernel(coeffs_ref, weights_ref, back_ref):
+def degree_kernel(coeffs_ref, weights_ref, stored_ref, back_ref, table_ref, sem):
+    load = pltpu.make_async_copy(stored_ref, table_ref, sem)
+    load.start()
     chans, lat_count = coeffs_ref.shape[1:3]
     third = coeffs_ref.shape[3] // (4 * (FULL * BLOCKS + UNITS))
     narrow = BLOCKS * third
@@ -401,6 +403,7 @@
                 )
             pieces += [units[p][u] for u in range(UNITS) for p in range(2)]
             back_ref[y * lat_count : (y + 1) * lat_count, s, :] = jnp.concatenate(pieces, axis=1)
+    load.wait()
 
 
 def backward_kernel(back_ref, legendre_ref, out_ref):
@@ -464,9 +467,22 @@
     return slots
 
 
-def gradient_kernel(
-    counts_ref, rank_ref, coeffs_ref, mine_ref, grad_ref, out_ref, held_ref, empty_ref, sems, grad_sems
-):
+def gradient_kernel(coeffs_ref, grad_ref, held_ref, sems):
+    stores = []
+    for s in range(2):
+        held_ref[s] = lax.dot_general(
+            side(coeffs_ref, s, 0),
+            side(coeffs_ref, s, 1),
+            (((0,), (0,)), ((), ())),
+            preferred_element_type=F32,
+        )
+        stores.append(pltpu.make_async_copy(held_ref.at[s], grad_ref.at[s], sems.at[s]))
+        stores[-1].start()
+    for store in stores:
+        store.wait()
+
+
+def own_kernel(counts_ref, rank_ref, mine_ref, out_ref, empty_ref, sems):
     empty_ref[...] = jnp.zeros_like(empty_ref)
     rows = []
     for r, (live, own, at) in enumerate(held_rows(counts_ref, rank_ref)):
@@ -476,20 +492,8 @@
         pl.when(live & own)(near.start)
         pl.when(jnp.logical_not(live))(dead.start)
         rows.append((jnp.logical_not(live) | own, near))
-    stores = []
-    for s in range(2):
-        held_ref[s] = lax.dot_general(
-            side(coeffs_ref, s, 0),
-            side(coeffs_ref, s, 1),
-            (((0,), (0,)), ((), ())),
-            preferred_element_type=F32,
-        )
-        stores.append(pltpu.make_async_copy(held_ref.at[s], grad_ref.at[s], grad_sems.at[s]))
-        stores[-1].start()
     for started, row in rows:
         pl.when(started)(row.wait)
-    for store in stores:
-        store.wait()
 
 
 def placing_kernel(counts_ref, rank_ref, theirs_ref, placed_ref, out_ref, sems):
@@ -555,11 +559,16 @@
     )
     coeffs = lax.all_to_all(coeffs, everyone, split_axis=0, concat_axis=0, tiled=True)
     coeffs = coeffs.transpose(1, 0, 2).reshape(held, chan_count, lat_count, 4 * pieces * third)
-    back = run(
+    back, by_part = run(
         degree_kernel,
         "degree",
-        [pltpu.VMEM((devices, held, 2 * pieces * third), BF16)],
-        [coeffs, weights],
+        [
+            pltpu.VMEM((devices, held, 2 * pieces * third), BF16),
+            pltpu.VMEM(by_part.shape, BF16),
+        ],
+        [coeffs, weights, by_part],
+        [pltpu.SemaphoreType.DMA],
+        far=(2,),
     )
     back = lax.all_to_all(back, everyone, split_axis=0, concat_axis=0, tiled=True)
     modes_back = run(
@@ -568,26 +577,30 @@
         [pltpu.VMEM((lat_count, 2, ROWS * pieces * third), BF16)],
         [back, legendre_pairs],
     )
+    modes_back, coeffs = lax.optimization_barrier((modes_back, coeffs))
     modes_back = lax.all_to_all(modes_back, "lat", split_axis=0, concat_axis=0, tiled=True)
+    weight_grad = run(
+        gradient_kernel,
+        "gradient",
+        [pltpu.HBM((held, full, full), F32)],
+        [coeffs],
+        [pltpu.VMEM((held, full, full), F32), pltpu.SemaphoreType.DMA((held,))],
+        home=pltpu.HBM,
+    )
+    modes_back, weight_grad = lax.optimization_barrier((modes_back, weight_grad))
     grad = run(
         synthesis_kernel,
         "synthesis",
         [pltpu.VMEM((ROWS, narrow, NLON), BF16)],
         [modes_back.transpose(1, 0, 2), by_part],
     )
-    grad, coeffs = lax.optimization_barrier((grad, coeffs))
     grad_swap = lax.ppermute(grad, "lat", pairs)
-    weight_grad, placed = run(
-        gradient_kernel,
-        "gradient",
-        [pltpu.HBM((held, full, full), F32), pltpu.HBM(field_in.shape, BF16)],
-        [row_counts, at_rank, coeffs, grad],
-        [
-            pltpu.VMEM((held, full, full), F32),
-            pltpu.VMEM((narrow, NLON), BF16),
-            pltpu.SemaphoreType.DMA((2 * ROWS,)),
-            pltpu.SemaphoreType.DMA((held,)),
-        ],
+    placed = run(
+        own_kernel,
+        "own",
+        [pltpu.HBM(field_in.shape, BF16)],
+        [row_counts, at_rank, grad],
+        [pltpu.VMEM((narrow, NLON), BF16), pltpu.SemaphoreType.DMA((2 * ROWS,))],
         home=pltpu.HBM,
     )
     grad_swap, placed = lax.optimization_barrier((grad_swap, placed))

time: 213 us -> 214 us (level)
  blocking collectives: 134 us -> 106 us
  waiting for transfers between devices: 22.7 us -> 43.8 us
  starting transfers between devices: 14.6 us -> 19.6 us
  Pallas kernels: 36.6 us -> 38.8 us
    all_to_all x1 -> x0, blocking collectives: 28.2 us -> none  [on_device(): lax.all_to_all(modes_back, 'lat', split_axis=0, concat_axis=0, tiled=True)]
    all_to_all x0 -> x1, waiting for transfers between devices: none -> 20.7 us  [on_device(): lax.all_to_all(modes_back, 'lat', split_axis=0, concat_axis=0, tiled=True)]
    all_to_all x0 -> x1, starting transfers between devices: none -> 5.04 us  [on_device(): lax.all_to_all(modes_back, 'lat', split_axis=0, concat_axis=0, tiled=True)]
    pallas_call x9 -> x10, Pallas kernels: 36.6 us -> 38.8 us  [run(): pl.pallas_call(kernel, out_shape=tuple(outs), in_specs=specs, out_specs=t...]
  transfers between devices with their start and end apart: 4 -> 5, of which waited for: 3 -> 5; matrix products, arithmetic and copies ran while one was open for 0% -> 0% of each run, Pallas kernels for 12% -> 12%
where the time goes in v12:
time: 214 us
  blocking collectives  106 us (50%)
  waiting for transfers between devices  43.8 us (20%)
  Pallas kernels  38.8 us (18%)
  starting transfers between devices  19.6 us (9%)
  local copies, waits for them, and re-layouts  4.84 us (2%)
    all_to_all x1, blocking collectives, on_device(): lax.all_to_all(coeffs, everyone, split_axis=0, concat_axis=0, tiled=True)  66.2 us
    all_to_all x1, blocking collectives, on_device(): lax.all_to_all(back, everyone, split_axis=0, concat_axis=0, tiled=True)  39.7 us
    pallas_call x10, Pallas kernels, run(): pl.pallas_call(kernel, out_shape=tuple(outs), in_specs=specs, out_specs=t...  38.8 us
    all_to_all x1, waiting for transfers between devices, on_device(): lax.all_to_all(modes, 'lat', split_axis=0, concat_axis=0, tiled=True)  21.1 us
    all_to_all x1, waiting for transfers between devices, on_device(): lax.all_to_all(modes_back, 'lat', split_axis=0, concat_axis=0, tiled=True)  20.7 us
    all_to_all x1, starting transfers between devices, on_device(): lax.all_to_all(modes, 'lat', split_axis=0, concat_axis=0, tiled=True)  10.4 us
    all_to_all x1, starting transfers between devices, on_device(): lax.all_to_all(modes_back, 'lat', split_axis=0, concat_axis=0, tiled=True)  5.04 us
  transfers between devices with their start and end apart: 5, of which 5 were waited for; matrix products, arithmetic and copies ran while one was open for 0% of the time, Pallas kernels for 12%

profile of v12, /device:TPU:1, one launch (start us, length us, event | category | flops | bytes accessed | tf_op | source)
XLA Modules:
  0.0 214.0 jit_solution(7316897643102933833)
XLA Ops:
  0.6 0.0 copy-start
  0.7 1.4 constant_dynamic-slice_fusion
  2.0 0.0 copy-start.1
  2.0 0.0 copy-start.4
  2.0 3.3 %collective-permute-start.1 = (bf16[6,96,720]{2,1,0:T(8,128)(2,1)S(1)}, bf16[6,96,720]{2,1,0:T(8,128)(2,1)S(1)}, u32[]{:S(2)}, u32[]{:S(2)}) collective-permute-start(bf16[6,96,720]{2,1,0:T(8,128)(2,1)S(1)} %constant_dynamic-slice_fusion), channel_id=1, source_target_pairs={{0,4},{4,0},{8,12},{12,8},{16,20},{20,16},{24,28},{28,24},{32,36},... | collective-permute-start | bytes 2488328 | tf_op jit(solution)/shard_map/ppermute | solution.py:529
  5.4 0.0 copy-done
  5.4 0.1 constant_dynamic-slice_fusion.1
  5.4 0.3 collective-permute-start
  5.8 1.3 fourier.1.fourier_ref
  7.0 0.4 collective-permute-done.1.cotan_in_ref
  7.4 1.3 collective-permute-done.field_in_ref
  8.7 0.0 copy-done.1
  8.7 0.0 copy-done.4
  8.7 3.8 %analysis.1 = bf16[64,2,6528]{2,1,0:T(2,128)(2,1)} custom-call(s32[64]{0:T(128)S(1)} %copy-done.4, s32[1]{0:T(128)} %bitcast.rank_ref, bf16[12,96,720]{2,1,0:T(8,128)(2,1)S(1)} %copy-done, bf16[12,96,720]{2,1,0:T(8,128)(2,1)S(1)} %copy-done.1, bf16[6,96,720]{2,1,0:T(8,128)(2,1)S(1)} %collective-permute-done.field_in_ref, ...), custom_call_target="tpu_custom_call" | custom-call | tf_op jit(solution)/shard_map/analysis/pallas_call | solution.py:115
  12.5 0.0 copy-start.7
  12.5 0.0 copy-start.2
  12.5 0.0 copy-start.3
  12.5 0.0 copy-start.5
  12.5 0.0 copy-start.6
  12.5 10.4 %all-to-all-start = ((bf16[64,2,6528]{2,1,0:T(2,128)(2,1)}), bf16[64,2,6528]{2,1,0:T(2,128)(2,1)}, u32[]{:S(2)}, u32[]{:S(2)}) async-start(bf16[64,2,6528]{2,1,0:T(2,128)(2,1)} %analysis.1), calls=%async_computation | async-start | bytes 3342336 | tf_op jit(solution)/shard_map/all_to_all | solution.py:544
  23.0 0.0 copy-done.7
  23.0 0.2 reshape.14
  23.2 0.1 broadcast_in_dim_reshape.4.slot_ref
  23.3 0.0 copy-done.2
  23.3 0.0 copy-done.3
  23.4 0.0 copy-done.5
  23.4 0.0 copy-done.6
  23.4 20.4 %legendre.1 = (bf16[7,512,384]{2,1,0:T(8,128)(2,1)S(1)}, bf16[7,384,512]{2,1,0:T(8,128)(2,1)}) custom-call(s32[1]{0:T(128)} %bitcast.rank_ref, f32[1,768]{1,0:T(1,128)S(1)} %copy-done.6, f32[1,768]{1,0:T(1,128)S(1)} %copy-done.5, f32[64,8,128]{2,1,0:T(8,128)S(1)} %copy-done.3, f32[64,8,128]{2,1,0:T(8,128)S(1)} %copy-done.2, ...), custom_call_target="tpu_custom_call" | custom-call | tf_op jit(solution)/shard_map/legendre/pallas_call | solution.py:115
  43.8 21.1 %all-to-all-done = bf16[64,2,6528]{2,1,0:T(2,128)(2,1)} async-done(((bf16[64,2,6528]{2,1,0:T(2,128)(2,1)}), bf16[64,2,6528]{2,1,0:T(2,128)(2,1)}, u32[]{:S(2)}, u32[]{:S(2)}) %all-to-all-start) | async-done | bytes 1671200 | tf_op jit(solution)/shard_map/all_to_all | solution.py:544
  64.8 1.6 copy.29
  66.4 2.2 %forward.1 = (bf16[256,2,2176]{2,1,0:T(2,128)(2,1)S(1)}, bf16[2,384,384]{2,1,0:T(8,128)(2,1)S(1)}, bf16[7,384,512]{2,1,0:T(8,128)(2,1)S(1)}) custom-call(s32[1]{0:T(128)} %bitcast.rank_ref, bf16[2,64,6528]{2,1,0:T(8,128)(2,1)S(1)} %bitcast.12, bf16[7,512,384]{2,1,0:T(8,128)(2,1)S(1)} %get-tuple-element.19.legendre_ref, bf16[2,384,384]{2,1,0:T(8,128)(2,1)} %stored_ref.2, ...), custom_call_target="tpu_custom_call" | custom-call | tf_op jit(solution)/shard_map/forward/pallas_call | solution.py:115
  68.6 66.2 %all_to_all.20 = bf16[256,2,2176]{2,1,0:T(2,128)(2,1)S(1)} all-to-all(bf16[256,2,2176]{2,1,0:T(2,128)(2,1)S(1)} %get-tuple-element.21), channel_id=1, replica_groups=mesh['lat'=64,'chan'=4] {'chan','lat'}, dimensions={0} | all-to-all | bytes 4456448 | tf_op jit(solution)/shard_map/all_to_all | solution.py:560
  134.8 0.2 copy.25
  135.0 1.7 degree.1
  136.7 39.7 %all_to_all.21.back_ref = bf16[256,2,1088]{2,1,0:T(2,128)(2,1)S(1)} all-to-all(bf16[256,2,1088]{2,1,0:T(2,128)(2,1)S(1)} %get-tuple-element.23), channel_id=1, replica_groups=mesh['lat'=64,'chan'=4] {'chan','lat'}, dimensions={0} | all-to-all | bytes 2228224 | tf_op jit(solution)/shard_map/all_to_all | solution.py:573
  176.4 2.2 %backward.1 = bf16[64,2,3264]{2,1,0:T(2,128)(2,1)} custom-call(bf16[256,2,1088]{2,1,0:T(2,128)(2,1)S(1)} %all_to_all.21.back_ref, bf16[7,384,512]{2,1,0:T(8,128)(2,1)S(1)} %get-tuple-element.24.legendre_ref), custom_call_target="tpu_custom_call" | custom-call | tf_op jit(solution)/shard_map/backward/pallas_call | solution.py:115
  178.6 5.0 %all-to-all-start.3 = ((bf16[64,2,3264]{2,1,0:T(2,128)(2,1)}), bf16[64,2,3264]{2,1,0:T(2,128)(2,1)}, u32[]{:S(2)}, u32[]{:S(2)}) async-start(bf16[64,2,3264]{2,1,0:T(2,128)(2,1)} %backward.1), calls=%async_computation.3 | async-start | bytes 1703936 | tf_op jit(solution)/shard_map/all_to_all | solution.py:581
  183.7 2.6 %gradient.1 = f32[2,384,384]{2,1,0:T(8,128)} custom-call(bf16[2,4,64,2176]{3,2,1,0:T(8,128)(2,1)S(1)} %bitcast.11), custom_call_target="tpu_custom_call" | custom-call | tf_op jit(solution)/shard_map/gradient/pallas_call | solution.py:115
  186.3 20.7 %all-to-all-done.3 = bf16[64,2,3264]{2,1,0:T(2,128)(2,1)} async-done(((bf16[64,2,3264]{2,1,0:T(2,128)(2,1)}), bf16[64,2,3264]{2,1,0:T(2,128)(2,1)}, u32[]{:S(2)}, u32[]{:S(2)}) %all-to-all-start.3) | async-done | bytes 835616 | tf_op jit(solution)/shard_map/all_to_all | solution.py:581
  207.0 1.2 copy.30
  208.2 1.5 synthesis.1.mine_ref
  209.7 0.5 collective-permute-start.2
  210.2 1.6 own.1.placed_ref
  211.8 0.4 collective-permute-done.2.theirs_ref
  212.2 1.6 placing.1
  (1 shorter events, 0.0 us)
Async XLA Ops:
  0.6 4.7 %copy-start = (bf16[12,96,720]{2,1,0:T(8,128)(2,1)S(1)}, bf16[12,96,720]{2,1,0:T(8,128)(2,1)}, u32[]{:S(2)}) copy-start(bf16[12,96,720]{2,1,0:T(8,128)(2,1)} %field_ref.1) | copy-start | bytes 4976644
  2.0 6.7 %copy-start.1 = (bf16[12,96,720]{2,1,0:T(8,128)(2,1)S(1)}, bf16[12,96,720]{2,1,0:T(8,128)(2,1)}, u32[]{:S(2)}) copy-start(bf16[12,96,720]{2,1,0:T(8,128)(2,1)} %cotan_ref.1) | copy-start | bytes 4976644
  2.0 6.7 %copy-start.4 = (s32[64]{0:T(128)S(1)}, s32[64]{0:T(128)}, u32[]{:S(2)}) copy-start(s32[64]{0:T(128)} %counts_ref.5) | copy-start | bytes 772
  2.0 5.4 %collective-permute-start.1 = (bf16[6,96,720]{2,1,0:T(8,128)(2,1)S(1)}, bf16[6,96,720]{2,1,0:T(8,128)(2,1)S(1)}, u32[]{:S(2)}, u32[]{:S(2)}) collective-permute-start(bf16[6,96,720]{2,1,0:T(8,128)(2,1)S(1)} %constant_dynamic-slice_fusion), channel_id=1, source_target_pairs={{0,4},{4,0},{8,12},{12,8},{16,20},{20,16},{24,28},{28,24},{32,36},... | collective-permute-start | bytes 2488328 | tf_op jit(solution)/shard_map/ppermute | solution.py:529
  5.4 3.3 %collective-permute-start = (bf16[6,96,720]{2,1,0:T(8,128)(2,1)S(1)}, bf16[6,96,720]{2,1,0:T(8,128)(2,1)S(1)}, u32[]{:S(2)}, u32[]{:S(2)}) collective-permute-start(bf16[6,96,720]{2,1,0:T(8,128)(2,1)S(1)} %constant_dynamic-slice_fusion.1), channel_id=1, source_target_pairs={{0,4},{4,0},{8,12},{12,8},{16,20},{20,16},{24,28},{28,24},{32,36},... | collective-permute-start | bytes 2488328 | tf_op jit(solution)/shard_map/ppermute | solution.py:528
  12.5 10.5 %copy-start.7 = (s32[512]{0:T(512)S(1)}, s32[512]{0:T(512)}, u32[]{:S(2)}) copy-start(s32[512]{0:T(512)} %param.15) | copy-start | bytes 6148
  12.5 10.8 %copy-start.2 = (f32[64,8,128]{2,1,0:T(8,128)S(1)}, f32[64,8,128]{2,1,0:T(8,128)}, u32[]{:S(2)}) copy-start(f32[64,8,128]{2,1,0:T(8,128)} %constant.42.clone.norm_ref) | copy-start | bytes 786436
  12.5 10.8 %copy-start.3 = (f32[64,8,128]{2,1,0:T(8,128)S(1)}, f32[64,8,128]{2,1,0:T(8,128)}, u32[]{:S(2)}) copy-start(f32[64,8,128]{2,1,0:T(8,128)} %constant.41.clone.order_ref) | copy-start | bytes 786436
  12.5 10.8 %copy-start.5 = (f32[1,768]{1,0:T(1,128)S(1)}, f32[1,768]{1,0:T(1,128)}, u32[]{:S(2)}) copy-start(f32[1,768]{1,0:T(1,128)} %constant.40.clone.logsine_ref) | copy-start | bytes 9220
  12.5 10.8 %copy-start.6 = (f32[1,768]{1,0:T(1,128)S(1)}, f32[1,768]{1,0:T(1,128)}, u32[]{:S(2)}) copy-start(f32[1,768]{1,0:T(1,128)} %constant.39.clone.cosine_ref) | copy-start | bytes 9220
  12.5 52.3 %all-to-all-start = ((bf16[64,2,6528]{2,1,0:T(2,128)(2,1)}), bf16[64,2,6528]{2,1,0:T(2,128)(2,1)}, u32[]{:S(2)}, u32[]{:S(2)}) async-start(bf16[64,2,6528]{2,1,0:T(2,128)(2,1)} %analysis.1), calls=%async_computation | async-start | bytes 3342336 | tf_op jit(solution)/shard_map/all_to_all | solution.py:544
  178.6 28.4 %all-to-all-start.3 = ((bf16[64,2,3264]{2,1,0:T(2,128)(2,1)}), bf16[64,2,3264]{2,1,0:T(2,128)(2,1)}, u32[]{:S(2)}, u32[]{:S(2)}) async-start(bf16[64,2,3264]{2,1,0:T(2,128)(2,1)} %backward.1), calls=%async_computation.3 | async-start | bytes 1703936 | tf_op jit(solution)/shard_map/all_to_all | solution.py:581
  209.7 2.5 %collective-permute-start.2 = (bf16[6,96,720]{2,1,0:T(8,128)(2,1)S(1)}, bf16[6,96,720]{2,1,0:T(8,128)(2,1)S(1)}, u32[]{:S(2)}, u32[]{:S(2)}) collective-permute-start(bf16[6,96,720]{2,1,0:T(8,128)(2,1)S(1)} %synthesis.1.mine_ref), channel_id=1, source_target_pairs={{0,4},{4,0},{8,12},{12,8},{16,20},{20,16},{24,28},{28,24},{32,36},... | collective-permute-start | bytes 2488328 | tf_op jit(solution)/shard_map/ppermute | solution.py:597

commit v13 on v8

--- a/solution.py
+++ b/solution.py
@@ -520,7 +520,7 @@
 
     field_send = lax.dynamic_slice_in_dim(field_in, (1 - odd) * ROWS, ROWS)
     cotan_send = lax.dynamic_slice_in_dim(cotangent, (1 - odd) * ROWS, ROWS)
-    field_send, by_rank = lax.optimization_barrier((field_send, by_rank))
+    field_send, cotan_send, by_rank = lax.optimization_barrier((field_send, cotan_send, by_rank))
     field_swap = lax.ppermute(field_send, "lat", pairs)
     cotan_swap = lax.ppermute(cotan_send, "lat", pairs)
     by_rank = loaded(by_rank, "fourier")

time: 213 us -> 214 us (level)
    ppermute x1, starting transfers between devices: 3.33 us -> 0.1 us  [on_device(): cotan_swap = lax.ppermute(cotan_send, 'lat', pairs)]
    ppermute x1, starting transfers between devices: 0.33 us -> 3.33 us  [on_device(): field_swap = lax.ppermute(field_send, 'lat', pairs)]
where the time goes in v13:
time: 214 us; the launch traced here: 213 us
  blocking collectives  134 us (63%)
  Pallas kernels  37 us (17%)
  waiting for transfers between devices  23 us (11%)
  starting transfers between devices  14.3 us (7%)
  local copies, waits for them, and re-layouts  3.96 us (2%)
    all_to_all x1, blocking collectives, on_device(): lax.all_to_all(coeffs, everyone, split_axis=0, concat_axis=0, tiled=True)  66.2 us
    all_to_all x1, blocking collectives, on_device(): lax.all_to_all(back, everyone, split_axis=0, concat_axis=0, tiled=True)  39.6 us
    pallas_call x9, Pallas kernels, run(): pl.pallas_call(kernel, out_shape=tuple(outs), in_specs=specs, out_specs=t...  37 us
    all_to_all x1, blocking collectives, on_device(): lax.all_to_all(modes_back, 'lat', split_axis=0, concat_axis=0, tiled=True)  28.2 us
    all_to_all x1, waiting for transfers between devices, on_device(): lax.all_to_all(modes, 'lat', split_axis=0, concat_axis=0, tiled=True)  21.1 us
    all_to_all x1, starting transfers between devices, on_device(): lax.all_to_all(modes, 'lat', split_axis=0, concat_axis=0, tiled=True)  10.4 us
  transfers between devices with their start and end apart: 4, of which 3 were waited for; matrix products, arithmetic and copies ran while one was open for 0% of the time, Pallas kernels for 12%

profile of v13, /device:TPU:1, one launch (start us, length us, event | category | flops | bytes accessed | tf_op | source)
XLA Modules:
  0.0 213.5 jit_solution(7568116488771366038)
XLA Ops:
  0.6 0.0 copy-start.1
  0.7 1.7 constant_dynamic-slice_fusion
  2.3 0.0 copy-start
  2.4 0.0 copy-start.5
  2.4 3.3 %collective-permute-start = (bf16[6,96,720]{2,1,0:T(8,128)(2,1)S(1)}, bf16[6,96,720]{2,1,0:T(8,128)(2,1)S(1)}, u32[]{:S(2)}, u32[]{:S(2)}) collective-permute-start(bf16[6,96,720]{2,1,0:T(8,128)(2,1)S(1)} %get-tuple-element.16), channel_id=1, source_target_pairs={{0,4},{4,0},{8,12},{12,8},{16,20},{20,16},{24,28},{28,24},{32,36},... | collective-permute-start | bytes 2488328 | tf_op jit(solution)/shard_map/ppermute | solution.py:524
  5.7 0.1 collective-permute-start.1
  5.8 1.3 fourier.1.fourier_ref
  7.1 0.7 collective-permute-done.field_in_ref
  7.7 1.3 collective-permute-done.1.cotan_in_ref
  9.0 0.0 copy-done.1
  9.0 0.0 copy-done
  9.0 0.0 copy-done.5
  9.0 3.8 %analysis.1 = bf16[64,2,6528]{2,1,0:T(2,128)(2,1)} custom-call(s32[64]{0:T(128)S(1)} %copy-done.5, s32[1]{0:T(128)} %bitcast.rank_ref, bf16[12,96,720]{2,1,0:T(8,128)(2,1)S(1)} %copy-done, bf16[12,96,720]{2,1,0:T(8,128)(2,1)S(1)} %copy-done.1, bf16[6,96,720]{2,1,0:T(8,128)(2,1)S(1)} %collective-permute-done.field_in_ref, ...), custom_call_target="tpu_custom_call" | custom-call | tf_op jit(solution)/shard_map/analysis/pallas_call | solution.py:115
  12.8 0.0 copy-start.8
  12.8 0.0 copy-start.3
  12.8 0.0 copy-start.4
  12.9 0.0 copy-start.6
  12.9 0.0 copy-start.7
  12.9 10.4 %all-to-all-start = ((bf16[64,2,6528]{2,1,0:T(2,128)(2,1)}), bf16[64,2,6528]{2,1,0:T(2,128)(2,1)}, u32[]{:S(2)}, u32[]{:S(2)}) async-start(bf16[64,2,6528]{2,1,0:T(2,128)(2,1)} %analysis.1), calls=%async_computation | async-start | bytes 3342336 | tf_op jit(solution)/shard_map/all_to_all | solution.py:540
  23.3 0.0 copy-done.8
  23.3 0.2 reshape.14
  23.6 0.1 broadcast_in_dim_reshape.4.slot_ref
  23.7 0.0 copy-done.3
  23.7 0.0 copy-done.4
  23.7 0.0 copy-done.6
  23.7 0.0 copy-done.7
  23.7 20.4 %legendre.1 = (bf16[7,512,384]{2,1,0:T(8,128)(2,1)S(1)}, bf16[7,384,512]{2,1,0:T(8,128)(2,1)}) custom-call(s32[1]{0:T(128)} %bitcast.rank_ref, f32[1,768]{1,0:T(1,128)S(1)} %copy-done.7, f32[1,768]{1,0:T(1,128)S(1)} %copy-done.6, f32[64,8,128]{2,1,0:T(8,128)S(1)} %copy-done.4, f32[64,8,128]{2,1,0:T(8,128)S(1)} %copy-done.3, ...), custom_call_target="tpu_custom_call" | custom-call | tf_op jit(solution)/shard_map/legendre/pallas_call | solution.py:115
  44.1 21.1 %all-to-all-done = bf16[64,2,6528]{2,1,0:T(2,128)(2,1)} async-done(((bf16[64,2,6528]{2,1,0:T(2,128)(2,1)}), bf16[64,2,6528]{2,1,0:T(2,128)(2,1)}, u32[]{:S(2)}, u32[]{:S(2)}) %all-to-all-start) | async-done | bytes 1671200 | tf_op jit(solution)/shard_map/all_to_all | solution.py:540
  65.2 1.6 copy.29
  66.8 2.2 %forward.1 = (bf16[256,2,2176]{2,1,0:T(2,128)(2,1)S(1)}, bf16[2,384,384]{2,1,0:T(8,128)(2,1)S(1)}, bf16[7,384,512]{2,1,0:T(8,128)(2,1)S(1)}) custom-call(s32[1]{0:T(128)} %bitcast.rank_ref, bf16[2,64,6528]{2,1,0:T(8,128)(2,1)S(1)} %bitcast.12, bf16[7,512,384]{2,1,0:T(8,128)(2,1)S(1)} %get-tuple-element.19.legendre_ref, bf16[2,384,384]{2,1,0:T(8,128)(2,1)} %stored_ref.1, ...), custom_call_target="tpu_custom_call" | custom-call | tf_op jit(solution)/shard_map/forward/pallas_call | solution.py:115
  68.9 66.2 %all_to_all.20 = bf16[256,2,2176]{2,1,0:T(2,128)(2,1)S(1)} all-to-all(bf16[256,2,2176]{2,1,0:T(2,128)(2,1)S(1)} %get-tuple-element.21), channel_id=1, replica_groups=mesh['lat'=64,'chan'=4] {'chan','lat'}, dimensions={0} | all-to-all | bytes 4456448 | tf_op jit(solution)/shard_map/all_to_all | solution.py:556
  135.1 0.2 copy.25
  135.4 1.7 degree.1
  137.0 39.6 %all_to_all.21.back_ref = bf16[256,2,1088]{2,1,0:T(2,128)(2,1)S(1)} all-to-all(bf16[256,2,1088]{2,1,0:T(2,128)(2,1)S(1)} %degree.1), channel_id=1, replica_groups=mesh['lat'=64,'chan'=4] {'chan','lat'}, dimensions={0} | all-to-all | bytes 2228224 | tf_op jit(solution)/shard_map/all_to_all | solution.py:564
  176.7 1.3 backward.1
  178.0 0.0 copy-start.2
  178.0 28.2 %all_to_all.22 = bf16[64,2,3264]{2,1,0:T(2,128)(2,1)S(1)} all-to-all(bf16[64,2,3264]{2,1,0:T(2,128)(2,1)S(1)} %backward.1), channel_id=1, replica_groups=mesh['lat'=64,'chan'=4] {'lat'}, dimensions={0} | all-to-all | bytes 1671168 | tf_op jit(solution)/shard_map/all_to_all | solution.py:571
  206.2 0.1 copy.30
  206.3 0.0 copy-done.2
  206.3 1.5 synthesis.1.mine_ref
  207.8 0.5 collective-permute-start.2
  208.2 3.6 %gradient.1 = (f32[2,384,384]{2,1,0:T(8,128)}, bf16[12,96,720]{2,1,0:T(8,128)(2,1)}) custom-call(s32[64]{0:T(128)S(1)} %copy-done.5, s32[1]{0:T(128)} %bitcast.rank_ref, bf16[2,4,64,2176]{3,2,1,0:T(8,128)(2,1)S(1)} %bitcast.11, bf16[6,96,720]{2,1,0:T(8,128)(2,1)S(1)} %synthesis.1.mine_ref), custom_call_target="tpu_custom_call" | custom-call | tf_op jit(solution)/shard_map/gradient/pallas_call | solution.py:115
  211.8 0.0 collective-permute-done.2.theirs_ref
  211.8 1.4 placing.1
  (1 shorter events, 0.0 us)
Async XLA Ops:
  0.6 8.4 %copy-start.1 = (bf16[12,96,720]{2,1,0:T(8,128)(2,1)S(1)}, bf16[12,96,720]{2,1,0:T(8,128)(2,1)}, u32[]{:S(2)}) copy-start(bf16[12,96,720]{2,1,0:T(8,128)(2,1)} %cotan_ref.1) | copy-start | bytes 4976644
  2.3 6.7 %copy-start = (bf16[12,96,720]{2,1,0:T(8,128)(2,1)S(1)}, bf16[12,96,720]{2,1,0:T(8,128)(2,1)}, u32[]{:S(2)}) copy-start(bf16[12,96,720]{2,1,0:T(8,128)(2,1)} %field_ref.1) | copy-start | bytes 4976644
  2.4 6.7 %copy-start.5 = (s32[64]{0:T(128)S(1)}, s32[64]{0:T(128)}, u32[]{:S(2)}) copy-start(s32[64]{0:T(128)} %counts_ref.5) | copy-start | bytes 772
  2.4 5.4 %collective-permute-start = (bf16[6,96,720]{2,1,0:T(8,128)(2,1)S(1)}, bf16[6,96,720]{2,1,0:T(8,128)(2,1)S(1)}, u32[]{:S(2)}, u32[]{:S(2)}) collective-permute-start(bf16[6,96,720]{2,1,0:T(8,128)(2,1)S(1)} %get-tuple-element.16), channel_id=1, source_target_pairs={{0,4},{4,0},{8,12},{12,8},{16,20},{20,16},{24,28},{28,24},{32,36},... | collective-permute-start | bytes 2488328 | tf_op jit(solution)/shard_map/ppermute | solution.py:524
  5.7 3.3 %collective-permute-start.1 = (bf16[6,96,720]{2,1,0:T(8,128)(2,1)S(1)}, bf16[6,96,720]{2,1,0:T(8,128)(2,1)S(1)}, u32[]{:S(2)}, u32[]{:S(2)}) collective-permute-start(bf16[6,96,720]{2,1,0:T(8,128)(2,1)S(1)} %get-tuple-element.17), channel_id=1, source_target_pairs={{0,4},{4,0},{8,12},{12,8},{16,20},{20,16},{24,28},{28,24},{32,36},... | collective-permute-start | bytes 2488328 | tf_op jit(solution)/shard_map/ppermute | solution.py:525
  12.8 10.5 %copy-start.8 = (s32[512]{0:T(512)S(1)}, s32[512]{0:T(512)}, u32[]{:S(2)}) copy-start(s32[512]{0:T(512)} %param.15) | copy-start | bytes 6148
  12.8 10.8 %copy-start.3 = (f32[64,8,128]{2,1,0:T(8,128)S(1)}, f32[64,8,128]{2,1,0:T(8,128)}, u32[]{:S(2)}) copy-start(f32[64,8,128]{2,1,0:T(8,128)} %constant.42.clone.norm_ref) | copy-start | bytes 786436
  12.8 10.8 %copy-start.4 = (f32[64,8,128]{2,1,0:T(8,128)S(1)}, f32[64,8,128]{2,1,0:T(8,128)}, u32[]{:S(2)}) copy-start(f32[64,8,128]{2,1,0:T(8,128)} %constant.41.clone.order_ref) | copy-start | bytes 786436
  12.9 10.8 %copy-start.6 = (f32[1,768]{1,0:T(1,128)S(1)}, f32[1,768]{1,0:T(1,128)}, u32[]{:S(2)}) copy-start(f32[1,768]{1,0:T(1,128)} %constant.40.clone.logsine_ref) | copy-start | bytes 9220
  12.9 10.8 %copy-start.7 = (f32[1,768]{1,0:T(1,128)S(1)}, f32[1,768]{1,0:T(1,128)}, u32[]{:S(2)}) copy-start(f32[1,768]{1,0:T(1,128)} %constant.39.clone.cosine_ref) | copy-start | bytes 9220
  12.9 52.3 %all-to-all-start = ((bf16[64,2,6528]{2,1,0:T(2,128)(2,1)}), bf16[64,2,6528]{2,1,0:T(2,128)(2,1)}, u32[]{:S(2)}, u32[]{:S(2)}) async-start(bf16[64,2,6528]{2,1,0:T(2,128)(2,1)} %analysis.1), calls=%async_computation | async-start | bytes 3342336 | tf_op jit(solution)/shard_map/all_to_all | solution.py:540
  178.0 28.3 %copy-start.2 = (bf16[720,720]{1,0:T(8,128)(2,1)S(1)}, bf16[720,720]{1,0:T(8,128)(2,1)}, u32[]{:S(2)}) copy-start(bf16[720,720]{1,0:T(8,128)(2,1)} %constant.38.clone.fourier_ref) | copy-start | bytes 3110404
  207.8 4.1 %collective-permute-start.2 = (bf16[6,96,720]{2,1,0:T(8,128)(2,1)S(1)}, bf16[6,96,720]{2,1,0:T(8,128)(2,1)S(1)}, u32[]{:S(2)}, u32[]{:S(2)}) collective-permute-start(bf16[6,96,720]{2,1,0:T(8,128)(2,1)S(1)} %synthesis.1.mine_ref), channel_id=1, source_target_pairs={{0,4},{4,0},{8,12},{12,8},{16,20},{20,16},{24,28},{28,24},{32,36},... | collective-permute-start | bytes 2488328 | tf_op jit(solution)/shard_map/ppermute | solution.py:579

commit v14 on v8

--- a/solution.py
+++ b/solution.py
@@ -285,7 +285,7 @@
         at = FULL * width + u * (width // BLOCKS)
         held_ref[:, :, at : at + width // BLOCKS] = unit.reshape(lat_count, 2, width // BLOCKS)
     send(FULL * width, out_ref.shape[2])
-    for j0, j1 in ((0, 2), (2, 4), (4, FULL)):
+    for j0, j1 in ((0, 3), (3, FULL)):
         modes = lax.dot_general(
             fourier_ref[2 * lat_count * j0 : 2 * lat_count * j1, :],
             rows_ref[...],

time: 213 us -> 213 us (level)
  no operation moved by 1% of the time
where the time goes in v14:
time: 213 us
  blocking collectives  134 us (63%)
  Pallas kernels  36.4 us (17%)
  waiting for transfers between devices  22.7 us (11%)
  starting transfers between devices  14.6 us (7%)
  local copies, waits for them, and re-layouts  3.69 us (2%)
    all_to_all x1, blocking collectives, on_device(): lax.all_to_all(coeffs, everyone, split_axis=0, concat_axis=0, tiled=True)  66.2 us
    all_to_all x1, blocking collectives, on_device(): lax.all_to_all(back, everyone, split_axis=0, concat_axis=0, tiled=True)  39.6 us
    pallas_call x9, Pallas kernels, run(): pl.pallas_call(kernel, out_shape=tuple(outs), in_specs=specs, out_specs=t...  36.4 us
    all_to_all x1, blocking collectives, on_device(): lax.all_to_all(modes_back, 'lat', split_axis=0, concat_axis=0, tiled=True)  28.2 us
    all_to_all x1, waiting for transfers between devices, on_device(): lax.all_to_all(modes, 'lat', split_axis=0, concat_axis=0, tiled=True)  21.1 us
    all_to_all x1, starting transfers between devices, on_device(): lax.all_to_all(modes, 'lat', split_axis=0, concat_axis=0, tiled=True)  10.4 us
  transfers between devices with their start and end apart: 4, of which 3 were waited for; matrix products, arithmetic and copies ran while one was open for 0% of the time, Pallas kernels for 12%

profile of v14, /device:TPU:1, one launch (start us, length us, event | category | flops | bytes accessed | tf_op | source)
XLA Modules:
  0.0 212.5 jit_solution(3761454347146471097)
XLA Ops:
  0.6 0.0 copy-start
  0.7 1.4 constant_dynamic-slice_fusion
  2.0 0.0 copy-start.1
  2.0 0.0 copy-start.5
  2.0 3.3 %collective-permute-start.1 = (bf16[6,96,720]{2,1,0:T(8,128)(2,1)S(1)}, bf16[6,96,720]{2,1,0:T(8,128)(2,1)S(1)}, u32[]{:S(2)}, u32[]{:S(2)}) collective-permute-start(bf16[6,96,720]{2,1,0:T(8,128)(2,1)S(1)} %constant_dynamic-slice_fusion), channel_id=1, source_target_pairs={{0,4},{4,0},{8,12},{12,8},{16,20},{20,16},{24,28},{28,24},{32,36},... | collective-permute-start | bytes 2488328 | tf_op jit(solution)/shard_map/ppermute | solution.py:525
  5.4 0.0 copy-done
  5.4 0.1 constant_dynamic-slice_fusion.1
  5.4 0.3 collective-permute-start
  5.8 1.3 fourier.1.fourier_ref
  7.0 0.4 collective-permute-done.1.cotan_in_ref
  7.4 1.3 collective-permute-done.field_in_ref
  8.7 0.0 copy-done.1
  8.7 0.0 copy-done.5
  8.7 3.7 %analysis.1 = bf16[64,2,6528]{2,1,0:T(2,128)(2,1)} custom-call(s32[64]{0:T(128)S(1)} %copy-done.5, s32[1]{0:T(128)} %bitcast.rank_ref, bf16[12,96,720]{2,1,0:T(8,128)(2,1)S(1)} %copy-done, bf16[12,96,720]{2,1,0:T(8,128)(2,1)S(1)} %copy-done.1, bf16[6,96,720]{2,1,0:T(8,128)(2,1)S(1)} %collective-permute-done.field_in_ref, ...), custom_call_target="tpu_custom_call" | custom-call | tf_op jit(solution)/shard_map/analysis/pallas_call | solution.py:115
  12.4 0.0 copy-start.8
  12.4 0.0 copy-start.3
  12.4 0.0 copy-start.4
  12.4 0.0 copy-start.6
  12.4 0.0 copy-start.7
  12.4 10.4 %all-to-all-start = ((bf16[64,2,6528]{2,1,0:T(2,128)(2,1)}), bf16[64,2,6528]{2,1,0:T(2,128)(2,1)}, u32[]{:S(2)}, u32[]{:S(2)}) async-start(bf16[64,2,6528]{2,1,0:T(2,128)(2,1)} %analysis.1), calls=%async_computation | async-start | bytes 3342336 | tf_op jit(solution)/shard_map/all_to_all | solution.py:540
  22.9 0.0 copy-done.8
  22.9 0.2 reshape.14
  23.1 0.1 broadcast_in_dim_reshape.4.slot_ref
  23.2 0.0 copy-done.3
  23.2 0.0 copy-done.4
  23.2 0.0 copy-done.6
  23.2 0.0 copy-done.7
  23.3 20.4 %legendre.1 = (bf16[7,512,384]{2,1,0:T(8,128)(2,1)S(1)}, bf16[7,384,512]{2,1,0:T(8,128)(2,1)}) custom-call(s32[1]{0:T(128)} %bitcast.rank_ref, f32[1,768]{1,0:T(1,128)S(1)} %copy-done.7, f32[1,768]{1,0:T(1,128)S(1)} %copy-done.6, f32[64,8,128]{2,1,0:T(8,128)S(1)} %copy-done.4, f32[64,8,128]{2,1,0:T(8,128)S(1)} %copy-done.3, ...), custom_call_target="tpu_custom_call" | custom-call | tf_op jit(solution)/shard_map/legendre/pallas_call | solution.py:115
  43.6 21.1 %all-to-all-done = bf16[64,2,6528]{2,1,0:T(2,128)(2,1)} async-done(((bf16[64,2,6528]{2,1,0:T(2,128)(2,1)}), bf16[64,2,6528]{2,1,0:T(2,128)(2,1)}, u32[]{:S(2)}, u32[]{:S(2)}) %all-to-all-start) | async-done | bytes 1671200 | tf_op jit(solution)/shard_map/all_to_all | solution.py:540
  64.7 1.6 copy.29
  66.3 2.2 %forward.1 = (bf16[256,2,2176]{2,1,0:T(2,128)(2,1)S(1)}, bf16[2,384,384]{2,1,0:T(8,128)(2,1)S(1)}, bf16[7,384,512]{2,1,0:T(8,128)(2,1)S(1)}) custom-call(s32[1]{0:T(128)} %bitcast.rank_ref, bf16[2,64,6528]{2,1,0:T(8,128)(2,1)S(1)} %bitcast.12, bf16[7,512,384]{2,1,0:T(8,128)(2,1)S(1)} %get-tuple-element.17.legendre_ref, bf16[2,384,384]{2,1,0:T(8,128)(2,1)} %stored_ref.1, ...), custom_call_target="tpu_custom_call" | custom-call | tf_op jit(solution)/shard_map/forward/pallas_call | solution.py:115
  68.5 66.2 %all_to_all.20 = bf16[256,2,2176]{2,1,0:T(2,128)(2,1)S(1)} all-to-all(bf16[256,2,2176]{2,1,0:T(2,128)(2,1)S(1)} %get-tuple-element.19), channel_id=1, replica_groups=mesh['lat'=64,'chan'=4] {'chan','lat'}, dimensions={0} | all-to-all | bytes 4456448 | tf_op jit(solution)/shard_map/all_to_all | solution.py:556
  134.7 0.2 copy.25
  134.9 1.7 degree.1
  136.6 39.6 %all_to_all.21.back_ref = bf16[256,2,1088]{2,1,0:T(2,128)(2,1)S(1)} all-to-all(bf16[256,2,1088]{2,1,0:T(2,128)(2,1)S(1)} %degree.1), channel_id=1, replica_groups=mesh['lat'=64,'chan'=4] {'chan','lat'}, dimensions={0} | all-to-all | bytes 2228224 | tf_op jit(solution)/shard_map/all_to_all | solution.py:564
  176.2 1.3 backward.1
  177.5 0.0 copy-start.2
  177.5 28.2 %all_to_all.22 = bf16[64,2,3264]{2,1,0:T(2,128)(2,1)S(1)} all-to-all(bf16[64,2,3264]{2,1,0:T(2,128)(2,1)S(1)} %backward.1), channel_id=1, replica_groups=mesh['lat'=64,'chan'=4] {'lat'}, dimensions={0} | all-to-all | bytes 1671168 | tf_op jit(solution)/shard_map/all_to_all | solution.py:571
  205.7 0.1 copy.30
  205.8 0.0 copy-done.2
  205.8 1.5 synthesis.1.mine_ref
  207.3 0.5 collective-permute-start.2
  207.8 3.7 %gradient.1 = (f32[2,384,384]{2,1,0:T(8,128)}, bf16[12,96,720]{2,1,0:T(8,128)(2,1)}) custom-call(s32[64]{0:T(128)S(1)} %copy-done.5, s32[1]{0:T(128)} %bitcast.rank_ref, bf16[2,4,64,2176]{3,2,1,0:T(8,128)(2,1)S(1)} %bitcast.11, bf16[6,96,720]{2,1,0:T(8,128)(2,1)S(1)} %synthesis.1.mine_ref), custom_call_target="tpu_custom_call" | custom-call | tf_op jit(solution)/shard_map/gradient/pallas_call | solution.py:115
  211.5 0.0 collective-permute-done.2.theirs_ref
  211.5 0.8 placing.1
  (1 shorter events, 0.0 us)
Async XLA Ops:
  0.6 4.7 %copy-start = (bf16[12,96,720]{2,1,0:T(8,128)(2,1)S(1)}, bf16[12,96,720]{2,1,0:T(8,128)(2,1)}, u32[]{:S(2)}) copy-start(bf16[12,96,720]{2,1,0:T(8,128)(2,1)} %field_ref.1) | copy-start | bytes 4976644
  2.0 6.7 %copy-start.1 = (bf16[12,96,720]{2,1,0:T(8,128)(2,1)S(1)}, bf16[12,96,720]{2,1,0:T(8,128)(2,1)}, u32[]{:S(2)}) copy-start(bf16[12,96,720]{2,1,0:T(8,128)(2,1)} %cotan_ref.1) | copy-start | bytes 4976644
  2.0 6.7 %copy-start.5 = (s32[64]{0:T(128)S(1)}, s32[64]{0:T(128)}, u32[]{:S(2)}) copy-start(s32[64]{0:T(128)} %counts_ref.5) | copy-start | bytes 772
  2.0 5.4 %collective-permute-start.1 = (bf16[6,96,720]{2,1,0:T(8,128)(2,1)S(1)}, bf16[6,96,720]{2,1,0:T(8,128)(2,1)S(1)}, u32[]{:S(2)}, u32[]{:S(2)}) collective-permute-start(bf16[6,96,720]{2,1,0:T(8,128)(2,1)S(1)} %constant_dynamic-slice_fusion), channel_id=1, source_target_pairs={{0,4},{4,0},{8,12},{12,8},{16,20},{20,16},{24,28},{28,24},{32,36},... | collective-permute-start | bytes 2488328 | tf_op jit(solution)/shard_map/ppermute | solution.py:525
  5.4 3.3 %collective-permute-start = (bf16[6,96,720]{2,1,0:T(8,128)(2,1)S(1)}, bf16[6,96,720]{2,1,0:T(8,128)(2,1)S(1)}, u32[]{:S(2)}, u32[]{:S(2)}) collective-permute-start(bf16[6,96,720]{2,1,0:T(8,128)(2,1)S(1)} %constant_dynamic-slice_fusion.1), channel_id=1, source_target_pairs={{0,4},{4,0},{8,12},{12,8},{16,20},{20,16},{24,28},{28,24},{32,36},... | collective-permute-start | bytes 2488328 | tf_op jit(solution)/shard_map/ppermute | solution.py:524
  12.4 10.5 %copy-start.8 = (s32[512]{0:T(512)S(1)}, s32[512]{0:T(512)}, u32[]{:S(2)}) copy-start(s32[512]{0:T(512)} %param.15) | copy-start | bytes 6148
  12.4 10.8 %copy-start.3 = (f32[64,8,128]{2,1,0:T(8,128)S(1)}, f32[64,8,128]{2,1,0:T(8,128)}, u32[]{:S(2)}) copy-start(f32[64,8,128]{2,1,0:T(8,128)} %constant.42.clone.norm_ref) | copy-start | bytes 786436
  12.4 10.8 %copy-start.4 = (f32[64,8,128]{2,1,0:T(8,128)S(1)}, f32[64,8,128]{2,1,0:T(8,128)}, u32[]{:S(2)}) copy-start(f32[64,8,128]{2,1,0:T(8,128)} %constant.41.clone.order_ref) | copy-start | bytes 786436
  12.4 10.8 %copy-start.6 = (f32[1,768]{1,0:T(1,128)S(1)}, f32[1,768]{1,0:T(1,128)}, u32[]{:S(2)}) copy-start(f32[1,768]{1,0:T(1,128)} %constant.40.clone.logsine_ref) | copy-start | bytes 9220
  12.4 10.8 %copy-start.7 = (f32[1,768]{1,0:T(1,128)S(1)}, f32[1,768]{1,0:T(1,128)}, u32[]{:S(2)}) copy-start(f32[1,768]{1,0:T(1,128)} %constant.39.clone.cosine_ref) | copy-start | bytes 9220
  12.4 52.3 %all-to-all-start = ((bf16[64,2,6528]{2,1,0:T(2,128)(2,1)}), bf16[64,2,6528]{2,1,0:T(2,128)(2,1)}, u32[]{:S(2)}, u32[]{:S(2)}) async-start(bf16[64,2,6528]{2,1,0:T(2,128)(2,1)} %analysis.1), calls=%async_computation | async-start | bytes 3342336 | tf_op jit(solution)/shard_map/all_to_all | solution.py:540
  177.5 28.3 %copy-start.2 = (bf16[720,720]{1,0:T(8,128)(2,1)S(1)}, bf16[720,720]{1,0:T(8,128)(2,1)}, u32[]{:S(2)}) copy-start(bf16[720,720]{1,0:T(8,128)(2,1)} %constant.38.clone.fourier_ref) | copy-start | bytes 3110404
  207.3 4.2 %collective-permute-start.2 = (bf16[6,96,720]{2,1,0:T(8,128)(2,1)S(1)}, bf16[6,96,720]{2,1,0:T(8,128)(2,1)S(1)}, u32[]{:S(2)}, u32[]{:S(2)}) collective-permute-start(bf16[6,96,720]{2,1,0:T(8,128)(2,1)S(1)} %synthesis.1.mine_ref), channel_id=1, source_target_pairs={{0,4},{4,0},{8,12},{12,8},{16,20},{20,16},{24,28},{28,24},{32,36},... | collective-permute-start | bytes 2488328 | tf_op jit(solution)/shard_map/ppermute | solution.py:579
